TPU v7x, 128 devices: a whole 4x4x4 slice. The times are simulated.
128 devices in a mesh: expert: 16 (over z, y), tensor: 8 (over x, core).
Axes of the slice: x: 4, y: 4, z: 4, core: 2. Of those that a mesh axis runs over, the one named last changes fastest.
Arguments:
- tokens: bfloat16 [2048, 4096], P('expert'), may hold values from -6 to 6
- expert_ids: int32 [2048, 8], P('expert'), may hold values from 0 to 31, all different within a row; in each aligned block of 128 rows (0 to 127, 128 to 255, ...) at most 48 rows name the same one
- route_weights: float32 [2048, 8], P('expert'), may hold values from 0.1 to 0.5
- grad_out: bfloat16 [2048, 4096], P('expert'), may hold values from -6 to 6
- w_gate: bfloat16 [32, 1536, 4096], P('expert', 'tensor'), may hold values from -0.09375 to 0.09375
- w_up: bfloat16 [32, 1536, 4096], P('expert', 'tensor'), may hold values from -0.09375 to 0.09375
- w_down: bfloat16 [32, 1536, 4096], P('expert', 'tensor'), may hold values from -0.15625 to 0.15625
Outputs:
- grad_tokens: bfloat16 [2048, 4096], P('expert', 'tensor')
- grad_gate: bfloat16 [32, 1536, 4096], P('expert', 'tensor')
- grad_up: bfloat16 [32, 1536, 4096], P('expert', 'tensor')
- grad_down: bfloat16 [32, 1536, 4096], P('expert', 'tensor')
Inputs may be any that keep to these rules, and one draw needn't show every extreme that they name: `expert_ids`: each row names 8 different experts. Among the 128 rows of one block (aligned blocks of rows, one a device of the expert axis) no expert is named by more than 48 rows, and in every draw some expert is named by exactly 48 rows of some block.
All inputs are finite; a program needn't handle non-finite values.
Results may differ from a plain program's by a relative error of at most 0.02.
Values may be sent and summed in bfloat16 or wider, within the bound.
No kernel may reach another device: no remote copies, remote signals or barrier semaphores. Data moves between devices by JAX's collectives and lax.ppermute only.
A program may use at most 192 MiB of HBM per device.

v0:
```python
import jax
import jax.numpy as jnp
from jax import lax
from jax.sharding import PartitionSpec as P


def slot_numbers(id_block, experts, cap):
    flat = id_block.reshape(-1)
    onehot = (flat[:, None] == jnp.arange(experts, dtype=jnp.int32)[None, :]).astype(jnp.int32)
    before = jnp.cumsum(onehot, axis=0) - onehot
    position = jnp.sum(before * onehot, axis=1)
    return flat * cap + position


def shards(tokens, expert_ids, route_weights, grad_out, w_gate, w_up, w_down):
    tok_rows, width_d = tokens.shape
    chosen = expert_ids.shape[1]
    groups = lax.axis_size("expert")
    local_experts = w_gate.shape[0]
    experts = local_experts * groups
    cap = 3 * tok_rows * chosen // (2 * experts)
    slot_list = slot_numbers(expert_ids, experts, cap)
    pair_count = tok_rows * chosen
    owner = jnp.full((experts * cap,), pair_count, jnp.int32)
    owner = owner.at[slot_list].set(jnp.arange(pair_count, dtype=jnp.int32))
    token_index = owner // chosen
    token_pad = jnp.concatenate([tokens, jnp.zeros((1, width_d), jnp.bfloat16)], axis=0)
    grad_pad = jnp.concatenate([grad_out, jnp.zeros((1, width_d), jnp.bfloat16)], axis=0)
    weight_pad = jnp.concatenate([route_weights.reshape(-1), jnp.zeros((1,), jnp.float32)], axis=0)
    x_send = token_pad[token_index]
    g_send = (weight_pad[owner][:, None] * grad_pad[token_index].astype(jnp.float32)).astype(
        jnp.bfloat16
    )
    x_recv, g_recv = (
        lax.all_to_all(x_send, "expert", split_axis=0, concat_axis=0, tiled=True),
        lax.all_to_all(g_send, "expert", split_axis=0, concat_axis=0, tiled=True),
    )
    grid_shape = (groups, local_experts, cap, width_d)
    x_slots = x_recv.reshape(grid_shape)
    g_slots = g_recv.reshape(grid_shape)
    gate_pre = jnp.einsum("secd,efd->secf", x_slots, w_gate, preferred_element_type=jnp.float32)
    up_pre = jnp.einsum("secd,efd->secf", x_slots, w_up, preferred_element_type=jnp.float32)
    sigmoid_gate = jax.nn.sigmoid(gate_pre)
    silu_gate = gate_pre * sigmoid_gate
    act = (silu_gate * up_pre).astype(jnp.bfloat16)
    d_hidden = jnp.einsum("secd,efd->secf", g_slots, w_down, preferred_element_type=jnp.float32)
    d_gate = (d_hidden * up_pre * sigmoid_gate * (1.0 + gate_pre * (1.0 - sigmoid_gate))).astype(
        jnp.bfloat16
    )
    d_up = (d_hidden * silu_gate).astype(jnp.bfloat16)
    grad_down = jnp.einsum(
        "secf,secd->efd", act, g_slots, preferred_element_type=jnp.float32
    ).astype(jnp.bfloat16)
    grad_gate = jnp.einsum(
        "secf,secd->efd", d_gate, x_slots, preferred_element_type=jnp.float32
    ).astype(jnp.bfloat16)
    grad_up = jnp.einsum(
        "secf,secd->efd", d_up, x_slots, preferred_element_type=jnp.float32
    ).astype(jnp.bfloat16)
    partial_value = jnp.einsum("secf,efd->secd", d_gate, w_gate, preferred_element_type=jnp.float32)
    partial_value = partial_value + jnp.einsum(
        "secf,efd->secd", d_up, w_up, preferred_element_type=jnp.float32
    )
    partial_value = partial_value.reshape(groups * local_experts * cap, width_d)
    summed = lax.psum_scatter(
        partial_value.astype(jnp.bfloat16), "tensor", scatter_dimension=1, tiled=True
    )
    returned = lax.all_to_all(summed, "expert", split_axis=0, concat_axis=0, tiled=True)
    picked = returned[slot_list].astype(jnp.float32).reshape(tok_rows, chosen, returned.shape[1])
    grad_tokens = jnp.sum(picked, axis=1).astype(jnp.bfloat16)
    return (grad_tokens, grad_gate, grad_up, grad_down)


def solution(mesh):
    return jax.shard_map(
        shards,
        mesh=mesh,
        in_specs=(
            P("expert", None),
            P("expert", None),
            P("expert", None),
            P("expert", None),
            P("expert", "tensor", None),
            P("expert", "tensor", None),
            P("expert", "tensor", None),
        ),
        out_specs=(
            P("expert", "tensor"),
            P("expert", "tensor", None),
            P("expert", "tensor", None),
            P("expert", "tensor", None),
        ),
        check_vma=False,
    )
```

profile of v0, /device:TPU:0, one launch (start us, length us, event | category | flops | bytes accessed | tf_op | source)
XLA Modules:
  0.0 601.1 jit_solution(2090817988252071818)
XLA Ops:
  9.3 9.0 %reduce-window.6 = s32[32,8,128]{2,1,0:T(8,128)S(1)} reduce-window(s32[32,8,128]{2,1,0:T(8,128)S(1)} %fusion.39, s32[]{:T(128)} %constant.16.clone.1), window={size=1x1x128 pad=0_0x0_0x127_0}, to_apply=%region_0.0 | reduce-window | flops 4161536 | bytes 262148 | tf_op jit(solution)/shard_map/reduce-window
  18.9 4.3 scatter_custom_fusion
  25.6 23.5 %gather_fusion.2 = bf16[1536,4096]{1,0:T(8,128)(2,1)} fusion(bf16[129,4096]{1,0:T(8,128)(2,1)} %concatenate.11, s32[2048]{0:T(1024)S(1)} %get-tuple-element.8), kind=kCustom, calls=%fused_computation.2 | custom fusion | bytes 25171968 | tf_op jit(solution)/shard_map/gather | solution.py:30
  49.0 8.3 %all-to-all-start.1 = ((bf16[16,96,4096]{2,1,0:T(8,128)(2,1)}), bf16[16,96,4096]{2,1,0:T(8,128)(2,1)}, u32[]{:S(2)}, u32[]{:S(2)}) async-start(bf16[16,96,4096]{2,1,0:T(8,128)(2,1)} %bitcast.107), calls=%async_computation.1 | async-start | bytes 25165824 | tf_op jit(solution)/shard_map/all_to_all | solution.py:35
  57.6 8.4 %gather_fusion = f32[1536]{0:T(1024)S(1)} fusion(f32[1025]{0:T(1024)S(1)} %pad_maximum_fusion, s32[2048]{0:T(1024)S(1)} %get-tuple-element.9), kind=kCustom, calls=%fused_computation | custom fusion | bytes 18432 | tf_op jit(solution)/shard_map/gather | solution.py:31
  68.4 23.4 %gather_fusion.1 = bf16[1536,4096]{1,0:T(8,128)(2,1)} fusion(bf16[129,4096]{1,0:T(8,128)(2,1)} %concatenate.10, s32[2048]{0:T(1024)S(1)} %get-tuple-element.8), kind=kCustom, calls=%fused_computation.1 | custom fusion | bytes 25171968 | tf_op jit(solution)/shard_map/gather | solution.py:31
  91.8 11.7 %fusion = bf16[16,96,4096]{2,1,0:T(8,128)(2,1)} fusion(bf16[16,96,4096]{2,1,0:T(8,128)(2,1)} %bitcast.108, f32[16,96]{1,0:T(8,128)S(1)} %mul.55), kind=kLoop, calls=%fused_computation.6 | loop fusion | flops 18874368 | bytes 25171968 | tf_op jit(solution)/shard_map/convert_element_type | solution.py:31
  103.5 140.7 %all-to-all-done.1 = bf16[16,96,4096]{2,1,0:T(8,128)(2,1)} async-done(((bf16[16,96,4096]{2,1,0:T(8,128)(2,1)}), bf16[16,96,4096]{2,1,0:T(8,128)(2,1)}, u32[]{:S(2)}, u32[]{:S(2)}) %all-to-all-start.1) | async-done | bytes 12582944 | tf_op jit(solution)/shard_map/all_to_all | solution.py:35
  244.2 5.0 all-to-all-start
  249.4 9.3 %fusion.10 = f32[2,16,48,192]{3,2,1,0:T(8,128)} fusion(bf16[16,2,48,4096]{3,2,1,0:T(8,128)(2,1)} %bitcast.10, bf16[2,192,4096]{2,1,0:T(8,128)(2,1)S(1)} %copy-done), kind=kOutput, calls=%fused_computation.17 | convolution fusion | flops 2415919104 | bytes 16908288 | tf_op jit(solution)/shard_map/secd,efd->secf/dot_general | solution.py:41
  258.7 9.2 %fusion.12 = f32[2,16,48,192]{3,2,1,0:T(8,128)} fusion(bf16[16,2,48,4096]{3,2,1,0:T(8,128)(2,1)} %bitcast.10, bf16[2,192,4096]{2,1,0:T(8,128)(2,1)S(1)} %copy-done.1), kind=kOutput, calls=%fused_computation.19 | convolution fusion | flops 2415919104 | bytes 16908288 | tf_op jit(solution)/shard_map/secd,efd->secf/dot_general | solution.py:42
  267.9 164.3 %all-to-all-done = bf16[16,96,4096]{2,1,0:T(8,128)(2,1)} async-done(((bf16[16,96,4096]{2,1,0:T(8,128)(2,1)}), bf16[16,96,4096]{2,1,0:T(8,128)(2,1)}, u32[]{:S(2)}, u32[]{:S(2)}) %all-to-all-start) | async-done | bytes 12582944 | tf_op jit(solution)/shard_map/all_to_all | solution.py:36
  432.2 11.4 %fusion.34 = (bf16[16,2,48,192]{3,2,0,1:T(8,128)(2,1)}, bf16[16,2,48,192]{3,2,0,1:T(8,128)(2,1)}) fusion(f32[2,16,48,192]{3,2,1,0:T(8,128)} %fusion.10, f32[2,16,48,192]{3,2,1,0:T(8,128)} %fusion.12, bf16[2,192,4096]{2,1,0:T(8,128)(2,1)} %param.13, bf16[16,2,48,4096]{3,2,1,0:T(8,128)(2,1)} %bitcast.5), kind=kOutput, calls=%fused_computation.44 | convolution fusion | flops 2419752960 | bytes 19267584 | tf_op jit(solution)/shard_map/secd,efd->secf/dot_general | solution.py:46
  443.6 11.2 %fusion.20 = f32[2,16,48,4096]{3,2,1,0:T(8,128)} fusion(bf16[16,2,48,192]{3,2,0,1:T(8,128)(2,1)} %get-tuple-element.5, bf16[2,192,4096]{2,1,0:T(8,128)(2,1)S(1)} %copy-done), kind=kOutput, calls=%fused_computation.24 | convolution fusion | flops 2415919104 | bytes 28901376 | tf_op jit(solution)/shard_map/secf,efd->secd/dot_general | solution.py:60
  454.8 15.8 %fusion.1 = bf16[16,2,48,4096]{3,2,0,1:T(8,128)(2,1)} fusion(f32[2,16,48,4096]{3,2,1,0:T(8,128)} %fusion.20, bf16[16,2,48,192]{3,2,0,1:T(8,128)(2,1)} %get-tuple-element.4, bf16[2,192,4096]{2,1,0:T(8,128)(2,1)} %param.12), kind=kOutput, calls=%fused_computation.8 | convolution fusion | flops 2428502016 | bytes 41484288 | tf_op jit(solution)/shard_map/secf,efd->secd/dot_general | solution.py:61
  470.6 10.7 %copy.20 = bf16[16,2,48,4096]{3,2,1,0:T(8,128)(2,1)} copy(bf16[16,2,48,4096]{3,2,0,1:T(8,128)(2,1)} %fusion.1) | data formatting | bytes 25165824 | tf_op jit(solution)/shard_map/convert_element_type | solution.py:66
  481.3 9.2 %bitcast_convert_fusion.1 = bf16[2,192,4096]{2,1,0:T(8,128)(2,1)} fusion(bf16[16,2,48,192]{3,2,0,1:T(8,128)(2,1)} %get-tuple-element.4, bf16[16,2,48,4096]{3,2,1,0:T(8,128)(2,1)} %bitcast.10), kind=kOutput, calls=%fused_computation.22 | convolution fusion | flops 2417491968 | bytes 16318464 | tf_op jit(solution)/shard_map/secf,secd->efd/dot_general | solution.py:57
  490.6 9.5 %bitcast_convert_fusion.2 = bf16[2,192,4096]{2,1,0:T(8,128)(2,1)} fusion(bf16[16,2,48,192]{3,2,0,1:T(8,128)(2,1)S(1)} %copy-done.2, bf16[16,2,48,4096]{3,2,1,0:T(8,128)(2,1)} %bitcast.10), kind=kOutput, calls=%fused_computation.23 | convolution fusion | flops 2417491968 | bytes 16318464 | tf_op jit(solution)/shard_map/secf,secd->efd/dot_general | solution.py:54
  500.1 54.3 %reduce-scatter.2.cloned.1.call-done = bf16[1536,512]{1,0:T(8,128)(2,1)} async-done(((bf16[1536,4096]{1,0:T(8,128)(2,1)}), bf16[1536,512]{1,0:T(8,128)(2,1)}) %reduce-scatter.2.cloned.1.call-update) | async-done | bytes 1572880 | tf_op jit(solution)/shard_map/reduce_scatter | solution.py:65
  554.4 7.0 %all-to-all-start.2 = ((bf16[16,96,512]{2,1,0:T(8,128)(2,1)}), bf16[16,96,512]{2,1,0:T(8,128)(2,1)}, u32[]{:S(2)}, u32[]{:S(2)}) async-start(bf16[16,96,512]{2,1,0:T(8,128)(2,1)} %bitcast.110), calls=%async_computation.3 | async-start | bytes 3145728 | tf_op jit(solution)/shard_map/all_to_all | solution.py:68
  561.5 10.0 %bitcast_convert_fusion = bf16[2,192,4096]{2,1,0:T(8,128)(2,1)} fusion(bf16[16,2,48,4096]{3,2,1,0:T(8,128)(2,1)} %bitcast.5, f32[2,16,48,192]{3,2,1,0:T(8,128)} %fusion.12, f32[2,16,48,192]{3,2,1,0:T(8,128)} %fusion.10), kind=kOutput, calls=%fused_computation.21 | convolution fusion | flops 2419261440 | bytes 18087936 | tf_op jit(solution)/shard_map/secf,secd->efd/dot_general | solution.py:51
  571.5 13.5 %all-to-all-done.2 = bf16[16,96,512]{2,1,0:T(8,128)(2,1)} async-done(((bf16[16,96,512]{2,1,0:T(8,128)(2,1)}), bf16[16,96,512]{2,1,0:T(8,128)(2,1)}, u32[]{:S(2)}, u32[]{:S(2)}) %all-to-all-start.2) | async-done | bytes 1572896 | tf_op jit(solution)/shard_map/all_to_all | solution.py:68
  584.9 6.7 %gather_fusion.3 = bf16[1024,512]{1,0:T(8,128)(2,1)} fusion(bf16[1536,512]{1,0:T(8,128)(2,1)} %bitcast.21, s32[1024]{0:T(1024)S(1)} %broadcast_clamp_fusion), kind=kCustom, calls=%fused_computation.3 | custom fusion | bytes 2101248 | tf_op jit(solution)/shard_map/gather | solution.py:69
  591.6 2.6 bitcast_reduce_fusion
  (35 shorter events, 7.8 us)
Async XLA Ops:
  7.2 242.2 %copy-start = (bf16[2,192,4096]{2,1,0:T(8,128)(2,1)S(1)}, bf16[2,192,4096]{2,1,0:T(8,128)(2,1)}, u32[]{:S(2)}) copy-start(bf16[2,192,4096]{2,1,0:T(8,128)(2,1)} %param.11) | copy-start | bytes 9437188
  49.0 8.3 %copy-start.3 = (f32[128,8]{0,1:T(8,128)S(1)}, f32[128,8]{0,1:T(8,128)}, u32[]{:S(2)}) copy-start(f32[128,8]{0,1:T(8,128)} %param.9) | copy-start | bytes 12292
  49.0 195.1 %all-to-all-start.1 = ((bf16[16,96,4096]{2,1,0:T(8,128)(2,1)}), bf16[16,96,4096]{2,1,0:T(8,128)(2,1)}, u32[]{:S(2)}, u32[]{:S(2)}) async-start(bf16[16,96,4096]{2,1,0:T(8,128)(2,1)} %bitcast.107), calls=%async_computation.1 | async-start | bytes 25165824 | tf_op jit(solution)/shard_map/all_to_all | solution.py:35
  244.2 188.0 %all-to-all-start = ((bf16[16,96,4096]{2,1,0:T(8,128)(2,1)}), bf16[16,96,4096]{2,1,0:T(8,128)(2,1)}, u32[]{:S(2)}, u32[]{:S(2)}) async-start(bf16[16,96,4096]{2,1,0:T(8,128)(2,1)} %fusion), calls=%async_computation | async-start | bytes 25165824 | tf_op jit(solution)/shard_map/all_to_all | solution.py:36
  249.1 305.3 %reduce-scatter.2.cloned.1.call-start = ((), (), s32[]{:S(2)}) async-start(), calls=%async_computation.4 | async-start | bytes 14155776 | tf_op jit(solution)/shard_map/reduce_scatter | solution.py:65
  249.4 9.3 %copy-start.1 = (bf16[2,192,4096]{2,1,0:T(8,128)(2,1)S(1)}, bf16[2,192,4096]{2,1,0:T(8,128)(2,1)}, u32[]{:S(2)}) copy-start(bf16[2,192,4096]{2,1,0:T(8,128)(2,1)} %param.12) | copy-start | bytes 9437188
  481.3 9.2 %copy-start.2 = (bf16[16,2,48,192]{3,2,0,1:T(8,128)(2,1)S(1)}, bf16[16,2,48,192]{3,2,0,1:T(8,128)(2,1)}, u32[]{:S(2)}) copy-start(bf16[16,2,48,192]{3,2,0,1:T(8,128)(2,1)} %get-tuple-element.5) | copy-start | bytes 1769476
  554.4 30.5 %all-to-all-start.2 = ((bf16[16,96,512]{2,1,0:T(8,128)(2,1)}), bf16[16,96,512]{2,1,0:T(8,128)(2,1)}, u32[]{:S(2)}, u32[]{:S(2)}) async-start(bf16[16,96,512]{2,1,0:T(8,128)(2,1)} %bitcast.110), calls=%async_computation.3 | async-start | bytes 3145728 | tf_op jit(solution)/shard_map/all_to_all | solution.py:68
Sparse Core Ops, SparseCore 0:
  481.4 72.9 reduce-scatter.1
where the time goes:
time: 604 us; the launch traced here: 601 us
  waiting for transfers between devices  373 us (62%)
  matrix products  85.7 us (14%)
  local copies, waits for them, and re-layouts  83.5 us (14%)
  other arithmetic  24.4 us (4%)
  starting transfers between devices  20.5 us (3%)
  between operations  14.2 us (2%)
    all_to_all x1, waiting for transfers between devices, shards(): lax.all_to_all(g_send, 'expert', split_axis=0, concat_axis=0, tiled=True)  164 us
    all_to_all x1, waiting for transfers between devices, shards(): lax.all_to_all(x_send, 'expert', split_axis=0, concat_axis=0, tiled=True)  141 us
    reduce_scatter x1, waiting for transfers between devices, shards(): lax.psum_scatter(partial_value.astype(jnp.bfloat16), 'tensor', scatter_di...  54.3 us
    gather x1, local copies, waits for them, and re-layouts, shards(): x_send = token_pad[token_index]  23.5 us
    gather x1, local copies, waits for them, and re-layouts, shards(): grad_pad[token_index].astype(jnp.float32)  23.4 us
    dot_general x1, matrix products, shards(): jnp.einsum('secf,efd->secd', d_up, w_up, preferred_element_type=jnp.float32)  15.8 us
    all_to_all x1, waiting for transfers between devices, shards(): lax.all_to_all(summed, 'expert', split_axis=0, concat_axis=0, tiled=True)  13.5 us
  transfers between devices with their start and end apart: 4, of which 4 were waited for; matrix products, arithmetic and copies ran while one was open for 16% of the time, Pallas kernels for 0%

commit v1 on v0

v1 whole, which is shorter than its diff:
```python
import jax
import jax.numpy as jnp
from jax import lax
from jax.experimental import pallas as pl
from jax.experimental.pallas import tpu as pltpu
from jax.sharding import Mesh
from jax.sharding import PartitionSpec as P

BF = jnp.bfloat16
F32 = jnp.float32
CAP = 48
ZY = ("z", "y")
VMEM = pl.BlockSpec(memory_space=pltpu.VMEM)
SMEM = pl.BlockSpec(memory_space=pltpu.SMEM)
SWAP = [(0, 1), (1, 0)]


def params(mib):
    return pltpu.CompilerParams(vmem_limit_bytes=mib * 1024 * 1024)


def cost(flops, nbytes):
    return pl.CostEstimate(flops=int(flops), bytes_accessed=int(nbytes), transcendentals=0)


def nt(a, b):
    return lax.dot_general(a, b, (((1,), (1,)), ((), ())), preferred_element_type=F32)


def tn(a, b):
    return lax.dot_general(a, b, (((0,), (0,)), ((), ())), preferred_element_type=F32)


def places_kernel(c_ref, ids_ref, wts_ref, out_ref):
    rows, top = ids_ref.shape
    lane = lax.broadcasted_iota(jnp.int32, (rows, 128), 1)
    expert = 2 * lane + c_ref[0]
    hit = jnp.zeros((rows, 128), F32)
    wt = jnp.zeros((rows, 128), F32)
    for k in range(top):
        same = ids_ref[:, k : k + 1] == expert
        hit = hit + same.astype(F32)
        wt = wt + jnp.where(same, wts_ref[:, k : k + 1], 0.0)
    r = lax.broadcasted_iota(jnp.int32, (rows, rows), 0)
    q = lax.broadcasted_iota(jnp.int32, (rows, rows), 1)
    before = jnp.dot((q < r).astype(BF), hit.astype(BF), preferred_element_type=F32)
    pos = jnp.where(hit > 0.5, before, -1.0)
    out_ref[:, 0:rows] = pos.T[0:16, :]
    out_ref[:, rows : 2 * rows] = wt.T[0:16, :]


def chosen(row, count):
    p = lax.broadcasted_iota(jnp.int32, (CAP, count), 0).astype(F32)
    return row == p


def forward_kernel(pw_ref, ag_ref, wgu_ref, wd_ref, xo_ref, go_ref, act_ref, dgu_ref, xs, gs, pre, dh):
    step = pl.program_id(0)
    hidden = wd_ref.shape[0]
    picks, scales = [], []
    for i in range(2):
        row = pw_ref[pl.ds(2 * step + i, 1), :]
        pick = chosen(row[:, 0:128], 128)
        scales.append(jnp.sum(jnp.where(pick, row[:, 128:256], 0.0), axis=1, keepdims=True))
        wide = pick.astype(F32)
        none = jnp.zeros((CAP, 128), F32)
        picks.append(jnp.concatenate([wide, none] if i == 0 else [none, wide], axis=1))
    pick = jnp.concatenate(picks, axis=0).astype(BF)
    scale = jnp.concatenate(scales, axis=0)
    at = pl.ds(pl.multiple_of(step * 2 * CAP, 2 * CAP), 2 * CAP)
    for t in range(8):
        both = jnp.concatenate([ag_ref[t], ag_ref[8 + t]], axis=0)
        got = jnp.dot(pick, both, preferred_element_type=F32)
        x = got[:, 0:512].astype(BF)
        g = (got[:, 512:1024] * scale).astype(BF)
        cols = slice(t * 512, (t + 1) * 512)
        xs[at, cols] = x
        gs[at, cols] = g
        xo_ref[:, cols] = x
        go_ref[:, cols] = g

    @pl.when(step % 4 == 3)
    def _():
        rows = pl.ds(pl.multiple_of((step // 4) * 8 * CAP, 8 * CAP), 8 * CAP)

        @pl.loop(0, 3)
        def _(n):
            pre[n] = nt(xs[rows, :], wgu_ref[pl.ds(pl.multiple_of(n * 256, 256), 256), :])

        dh[...] = nt(gs[rows, :], wd_ref[...])
        both = jnp.concatenate([pre[0], pre[1], pre[2]], axis=1)
        gate, up = both[:, 0:hidden], both[:, hidden : 2 * hidden]
        sig = jax.nn.sigmoid(gate)
        silu = gate * sig
        d = dh[...]
        act_ref[rows, :] = (silu * up).astype(BF)
        dgu_ref[rows, 0:hidden] = (d * up * sig * (1.0 + gate * (1.0 - sig))).astype(BF)
        dgu_ref[rows, hidden : 2 * hidden] = (d * silu).astype(BF)


def partial_kernel(dgu_ref, wgu_ref, out_ref):
    out_ref[0] = jnp.dot(dgu_ref[...], wgu_ref[...], preferred_element_type=F32).astype(BF)


def weight_kernel(c_ref, dgu_ref, act_ref, xs_ref, gs_ref, gg_ref, gu_ref, gd_ref, sg_ref, su_ref, sd_ref, dt, at):
    f = gg_ref.shape[1]

    @pl.when(pl.program_id(0) == 0)
    def _():
        dt[...] = dgu_ref[...].astype(F32).T.astype(BF)
        at[...] = act_ref[...].astype(F32).T.astype(BF)

    gu = jnp.dot(dt[...], xs_ref[...], preferred_element_type=F32).astype(BF)
    gd = jnp.dot(at[...], gs_ref[...], preferred_element_type=F32).astype(BF)
    gg_ref[0] = gu[0:f]
    sg_ref[...] = gu[f : 2 * f]
    gu_ref[0] = gu[2 * f : 3 * f]
    su_ref[...] = gu[3 * f : 4 * f]
    gd_ref[0] = gd[0:f]
    sd_ref[...] = gd[f : 2 * f]


def combine_kernel(c_ref, pw_ref, ret_ref, keep_ref, send_ref):
    picks = [chosen(pw_ref[e : e + 1, 0:128], 128).astype(F32) for e in range(16)]
    pick = jnp.concatenate(picks, axis=0).T.astype(BF)
    total = jnp.dot(pick, ret_ref[...], preferred_element_type=F32)
    low = c_ref[0] == 0
    left, right = total[:, 0:512], total[:, 512:1024]
    keep_ref[...] = jnp.where(low, left, right)
    send_ref[...] = jnp.where(low, right, left)


def swap(v):
    return lax.ppermute(v, "c", SWAP)


def shards(tokens, expert_ids, route_weights, grad_out, w_gate, w_up, w_down):
    rows, width = tokens.shape
    f = w_gate.shape[1]
    slots = 16 * CAP
    c = lax.axis_index("c")
    t = lax.axis_index("x") * 2 + c
    cs = jnp.reshape(c, (1,)).astype(jnp.int32)

    own = jnp.concatenate(
        [lax.dynamic_slice_in_dim(v, t * 512, 512, 1) for v in (tokens, grad_out)], axis=1
    )
    gathered = lax.all_gather(own, ("z", "y", "x", "c"), axis=0, tiled=False)

    pw_own = pl.pallas_call(
        places_kernel,
        out_shape=jax.ShapeDtypeStruct((16, 2 * rows), F32),
        in_specs=[SMEM, VMEM, VMEM],
        out_specs=VMEM,
        name="places",
    )(cs, expert_ids, route_weights)
    pw = lax.all_to_all(pw_own, ZY, split_axis=0, concat_axis=0, tiled=True)

    mine = [lax.dynamic_index_in_dim(w, c, 0, False) for w in (w_gate, w_up, w_down)]
    other = [swap(lax.dynamic_index_in_dim(w, 1 - c, 0, False)) for w in (w_gate, w_up, w_down)]
    wgu = jnp.concatenate([mine[0], other[0], mine[1], other[1]], axis=0)
    wd = jnp.concatenate([mine[2], other[2]], axis=0)

    xs, gs, act, dgu = pl.pallas_call(
        forward_kernel,
        grid=(8,),
        out_shape=(
            jax.ShapeDtypeStruct((slots, width), BF),
            jax.ShapeDtypeStruct((slots, width), BF),
            jax.ShapeDtypeStruct((slots, 2 * f), BF),
            jax.ShapeDtypeStruct((slots, 4 * f), BF),
        ),
        in_specs=[VMEM, pl.BlockSpec((16, rows, 1024), lambda b: (b, 0, 0)), VMEM, VMEM],
        out_specs=(
            pl.BlockSpec((2 * CAP, width), lambda b: (b, 0)),
            pl.BlockSpec((2 * CAP, width), lambda b: (b, 0)),
            VMEM,
            VMEM,
        ),
        scratch_shapes=[
            pltpu.VMEM((slots, width), BF),
            pltpu.VMEM((slots, width), BF),
            pltpu.VMEM((3, 8 * CAP, 256), F32),
            pltpu.VMEM((8 * CAP, 2 * f), F32),
        ],
        compiler_params=params(56),
        cost_estimate=cost(2 * slots * width * 6 * f, 60e6),
        name="forward",
    )(pw, gathered, wgu, wd)

    partial_value = pl.pallas_call(
        partial_kernel,
        grid=(8,),
        out_shape=jax.ShapeDtypeStruct((4, slots, 1024), BF),
        in_specs=[VMEM, pl.BlockSpec((4 * f, 512), lambda j: (0, j))],
        out_specs=pl.BlockSpec((1, slots, 512), lambda j: (j // 2, 0, j % 2)),
        compiler_params=params(32),
        cost_estimate=cost(2 * slots * width * 4 * f, 14e6),
        name="partial",
    )(dgu, wgu)
    summed = lax.psum_scatter(
        partial_value.reshape(4 * slots, 1024), "x", scatter_dimension=0, tiled=True
    )

    whole = jax.ShapeDtypeStruct((2, f, width), BF)
    piece = jax.ShapeDtypeStruct((f, width), BF)
    gg, gu, gd, sg, su, sd = pl.pallas_call(
        weight_kernel,
        grid_spec=pltpu.PrefetchScalarGridSpec(
            num_scalar_prefetch=1,
            grid=(8,),
            in_specs=[
                VMEM,
                VMEM,
                pl.BlockSpec((slots, 512), lambda j, cr: (0, j)),
                pl.BlockSpec((slots, 512), lambda j, cr: (0, j)),
            ],
            out_specs=[pl.BlockSpec((1, f, 512), lambda j, cr: (cr[0], 0, j))] * 3
            + [pl.BlockSpec((f, 512), lambda j, cr: (0, j))] * 3,
            scratch_shapes=[pltpu.VMEM((4 * f, slots), BF), pltpu.VMEM((2 * f, slots), BF)],
        ),
        out_shape=[whole] * 3 + [piece] * 3,
        compiler_params=params(40),
        cost_estimate=cost(2 * slots * width * 6 * f, 24e6),
        name="weights",
    )(cs, dgu, act, xs, gs)
    grads = [
        lax.dynamic_update_index_in_dim(g, swap(s), 1 - c, 0)
        for g, s in ((gg, sg), (gu, su), (gd, sd))
    ]

    returned = lax.all_to_all(summed, ZY, split_axis=0, concat_axis=0, tiled=True)
    half = jax.ShapeDtypeStruct((rows, 512), F32)
    keep, send = pl.pallas_call(
        combine_kernel,
        out_shape=(half, half),
        in_specs=[SMEM, VMEM, VMEM],
        out_specs=(VMEM, VMEM),
        compiler_params=params(32),
        name="combine",
    )(cs, pw_own, returned)
    grad_tokens = (keep + swap(send)).astype(BF)
    return (grad_tokens, *grads)


def solution(mesh):
    fine = Mesh(mesh.devices.reshape(4, 4, 4, 2), ("z", "y", "x", "c"))
    rows = P(ZY, None)
    weights = P(ZY, ("x", "c"), None)
    return jax.shard_map(
        shards,
        mesh=fine,
        in_specs=(rows, rows, rows, rows, weights, weights, weights),
        out_specs=(P(ZY, ("x", "c")), weights, weights, weights),
        check_vma=False,
    )
```

time: 604 us -> 272 us (0.45)
  waiting for transfers between devices: 373 us -> 139 us
  matrix products: 85.7 us -> 0 us
  local copies, waits for them, and re-layouts: 83.5 us -> 28.3 us
  Pallas kernels: 0 us -> 54 us
  blocking collectives: 0 us -> 15.5 us
  other arithmetic: 24.4 us -> 10.4 us
  starting transfers between devices: 20.5 us -> 8.41 us
    all_to_all x3 -> x1, waiting for transfers between devices: 318 us -> 19.1 us  [shards(): lax.all_to_all(summed, ZY, split_axis=0, concat_axis=0, tiled=True)]
    dot_general x8 -> x0, matrix products: 85.7 us -> none  [the longest x1 15.8 us: shards(): jnp.einsum('secf,efd->secd', d_up, w_up, preferred_element_type=jnp.float32)]
    all_gather x0 -> x1, waiting for transfers between devices: none -> 74 us  [shards(): gathered = lax.all_gather(own, ('z', 'y', 'x', 'c'), axis=0, tiled=False)]
    gather x4 -> x0, local copies, waits for them, and re-layouts: 62 us -> none  [the longest x1 23.5 us: shards(): x_send = token_pad[token_index]]
    pallas_call x0 -> x5, Pallas kernels: none -> 54 us  [the longest x1 32.3 us: shards(): pl.pallas_call(forward_kernel, grid=(8,), out_shape=(jax.ShapeDtypeStruct...]
    all_to_all x0 -> x1, blocking collectives: none -> 15.5 us  [shards(): pw = lax.all_to_all(pw_own, ZY, split_axis=0, concat_axis=0, tiled=True)]
    all_to_all x3 -> x1, starting transfers between devices: 20.3 us -> 6.98 us  [shards(): lax.all_to_all(summed, ZY, split_axis=0, concat_axis=0, tiled=True)]
    convert_element_type x2 -> x1, other arithmetic: 11.7 us -> 0.7 us  [shards(): grad_tokens = (keep + swap(send)).astype(BF)]
  transfers between devices with their start and end apart: 4 -> 10, of which waited for: 4 -> 3; matrix products, arithmetic and copies ran while one was open for 16% -> 10% of each run, Pallas kernels for 0% -> 5%
where the time goes in v1:
time: 272 us; the launch traced here: 270 us
  waiting for transfers between devices  139 us (51%)
  Pallas kernels  54 us (20%)
  local copies, waits for them, and re-layouts  28.3 us (10%)
  blocking collectives  15.5 us (6%)
  between operations  14.2 us (5%)
  other arithmetic  10.4 us (4%)
  starting transfers between devices  8.41 us (3%)
    all_gather x1, waiting for transfers between devices, shards(): gathered = lax.all_gather(own, ('z', 'y', 'x', 'c'), axis=0, tiled=False)  74 us
    reduce_scatter x1, waiting for transfers between devices, shards(): lax.psum_scatter(partial_value.reshape(4 * slots, 1024), 'x', scatter_dim...  45.5 us
    pallas_call x1, Pallas kernels, shards(): pl.pallas_call(forward_kernel, grid=(8,), out_shape=(jax.ShapeDtypeStruct...  32.3 us
    all_to_all x1, waiting for transfers between devices, shards(): lax.all_to_all(summed, ZY, split_axis=0, concat_axis=0, tiled=True)  19.1 us
    all_to_all x1, blocking collectives, shards(): pw = lax.all_to_all(pw_own, ZY, split_axis=0, concat_axis=0, tiled=True)  15.5 us
    pallas_call x1, Pallas kernels, shards(): pl.pallas_call(weight_kernel, grid_spec=pltpu.PrefetchScalarGridSpec(num_...  12 us
    unnamed x25, local copies, waits for them, and re-layouts  11.6 us
    dynamic_update_slice x3, local copies, waits for them, and re-layouts, shards(): lax.dynamic_update_index_in_dim(g, swap(s), 1 - c, 0)  8.12 us
  transfers between devices with their start and end apart: 10, of which 3 were waited for; matrix products, arithmetic and copies ran while one was open for 10% of the time, Pallas kernels for 5%

profile of v1, /device:TPU:0, one launch (start us, length us, event | category | flops | bytes accessed | tf_op | source)
XLA Modules:
  0.0 269.5 jit_solution(8002412447108463423)
XLA Ops:
  7.2 1.0 constant_dynamic-slice_fusion
  8.2 0.7 pad_maximum_fusion.2
  9.0 3.5 %dynamic-slice_bitcast_fusion.5 = (bf16[192,4096]{1,0:T(8,128)(2,1)S(1)}, bf16[192,4096]{1,0:T(8,128)(2,1)}) fusion(bf16[2,192,4096]{2,1,0:T(8,128)(2,1)} %param.11, s32[]{:T(128)S(6)} %select_n.20, s32[]{:T(128)S(6)} %select_n.21), kind=kLoop, calls=%fused_computation.10 | loop fusion | bytes 6291464 | tf_op jit(solution)/shard_map/jit(dynamic_index_in_dim)/squeeze | solution.py:159
  12.5 2.0 dynamic-slice_bitcast_fusion.1
  15.5 1.4 dynamic-slice_bitcast_fusion.3
  18.4 2.0 places.1.pw_ref
  21.1 15.5 %all_to_all.22 = f32[16,1,256]{2,1,0:T(1,128)S(1)} all-to-all(f32[16,1,256]{2,1,0:T(1,128)S(1)} %copy.15), channel_id=1, replica_groups=mesh['z'=4,'y'=4,'x'=4,'c'=2] {'z','y'}, dimensions={0} | all-to-all | bytes 32768 | tf_op jit(solution)/shard_map/all_to_all | solution.py:157
  37.3 3.9 %pad_maximum_fusion.1.wd_ref = bf16[384,4096]{1,0:T(8,128)(2,1)} fusion(bf16[192,4096]{1,0:T(8,128)(2,1)} %collective-permute-done.2, bf16[192,4096]{1,0:T(8,128)(2,1)} %get-tuple-element.28), kind=kLoop, calls=%fused_computation.1 | loop fusion | flops 6291456 | bytes 6291456 | tf_op jit(solution)/shard_map/concatenate | solution.py:162
  41.2 5.1 %pad_maximum_fusion.wgu_ref = bf16[768,4096]{1,0:T(8,128)(2,1)} fusion(bf16[192,4096]{1,0:T(8,128)(2,1)} %collective-permute-done.1, bf16[192,4096]{1,0:T(8,128)(2,1)S(1)} %get-tuple-element.32, bf16[192,4096]{1,0:T(8,128)(2,1)} %collective-permute-done, bf16[192,4096]{1,0:T(8,128)(2,1)S(1)} %get-tuple-element.30), kind=kLoop, calls=%fused_computation | loop fusion | flops 25165824 | bytes 12582912 | tf_op jit(solution)/shard_map/concatenate | solution.py:161
  46.3 74.0 %all-gather.3.cloned.1.call-done = bf16[16384,1024]{1,0:T(8,128)(2,1)} async-done(((bf16[128,1024]{1,0:T(8,128)(2,1)}), bf16[16384,1024]{1,0:T(8,128)(2,1)}) %all-gather.3.cloned.1.call-update) | async-done | bytes 33554448 | tf_op jit(solution)/shard_map/all_gather | solution.py:148
  120.2 32.3 %forward.1 = (bf16[768,4096]{1,0:T(8,128)(2,1)}, bf16[768,4096]{1,0:T(8,128)(2,1)}, bf16[768,384]{1,0:T(8,128)(2,1)}, bf16[768,768]{1,0:T(8,128)(2,1)}) custom-call(f32[16,256]{1,0:T(8,128)} %bitcast.32, bf16[128,128,1024]{2,1,0:T(8,128)(2,1)} %bitcast.30, bf16[768,4096]{1,0:T(8,128)(2,1)} %pad_maximum_fusion.wgu_ref, bf16[384,4096]{1,0:T(8,128)(2,1)} %pad_maximum_fusion.1.wd_ref), custom_call_target="tpu_custom_call" | custom-call | flops 7247757312 | bytes 60000000 | tf_op jit(solution)/shard_map/forward/pallas_call | solution.py:164
  152.6 1.3 copy-done.4
  153.8 7.3 %partial.1 = bf16[4,768,1024]{2,1,0:T(8,128)(2,1)S(1)} custom-call(bf16[768,768]{1,0:T(8,128)(2,1)S(1)} %copy-done.4, bf16[768,4096]{1,0:T(8,128)(2,1)S(1)} %copy-done), custom_call_target="tpu_custom_call" | custom-call | flops 4831838208 | bytes 14000000 | tf_op jit(solution)/shard_map/partial/pallas_call | solution.py:191
  161.2 2.6 copy-done.1
  163.8 1.2 copy-done.5
  165.1 2.8 %copy-done.3 = bf16[768,4096]{1,0:T(8,128)(2,1)S(1)} copy-done((bf16[768,4096]{1,0:T(8,128)(2,1)S(1)}, bf16[768,4096]{1,0:T(8,128)(2,1)}, u32[]{:S(2)}) %copy-start.3) | copy-done | bytes 6291480
  167.9 1.1 copy-done.6
  168.9 12.0 %weights.1 = (bf16[2,192,4096]{2,1,0:T(8,128)(2,1)}, bf16[2,192,4096]{2,1,0:T(8,128)(2,1)}, bf16[2,192,4096]{2,1,0:T(8,128)(2,1)}, bf16[192,4096]{1,0:T(8,128)(2...) custom-call(s32[1]{0:T(128)} %bitcast.c_ref, bf16[768,768]{1,0:T(8,128)(2,1)S(1)} %copy-done.5, ...), custom_call_target="tpu_custom_call" | custom-call | flops 7247757312 | bytes 24000000 | tf_op jit(solution)/shard_map/weights/pallas_call | solution.py:207
  181.7 45.5 %reduce-scatter.2.cloned.1.call-done = bf16[768,1024]{1,0:T(8,128)(2,1)} async-done(((bf16[3072,1024]{1,0:T(8,128)(2,1)}), bf16[768,1024]{1,0:T(8,128)(2,1)}) %reduce-scatter.2.cloned.1.call-update) | async-done | bytes 1572880 | tf_op jit(solution)/shard_map/reduce_scatter | solution.py:201
  227.2 7.0 %all-to-all-start.1 = ((bf16[16,48,1024]{2,1,0:T(8,128)(2,1)}), bf16[16,48,1024]{2,1,0:T(8,128)(2,1)S(1)}, u32[]{:S(2)}, u32[]{:S(2)}) async-start(bf16[16,48,1024]{2,1,0:T(8,128)(2,1)} %bitcast.31), calls=%async_computation.2 | async-start | bytes 3145728 | tf_op jit(solution)/shard_map/all_to_all | solution.py:232
  234.2 2.7 %bitcast_dynamic-update-slice_fusion.2 = bf16[2,192,4096]{2,1,0:T(8,128)(2,1)} fusion(bf16[2,192,4096]{2,1,0:T(8,128)(2,1)} %get-tuple-element.22, s32[]{:T(128)S(6)} %select_n.21, bf16[192,4096]{1,0:T(8,128)(2,1)} %collective-permute-done.4), kind=kLoop, calls=%fused_computation.4 | loop fusion | bytes 3145732 | tf_op jit(solution)/shard_map/jit(dynamic_update_index_in_dim)/dynamic_update_slice | solution.py:228
  237.0 2.7 %bitcast_dynamic-update-slice_fusion.1 = bf16[2,192,4096]{2,1,0:T(8,128)(2,1)} fusion(bf16[2,192,4096]{2,1,0:T(8,128)(2,1)} %get-tuple-element.24, s32[]{:T(128)S(6)} %select_n.21, bf16[192,4096]{1,0:T(8,128)(2,1)} %collective-permute-done.5), kind=kLoop, calls=%fused_computation.3 | loop fusion | bytes 3145732 | tf_op jit(solution)/shard_map/jit(dynamic_update_index_in_dim)/dynamic_update_slice | solution.py:228
  239.7 19.1 %all-to-all-done.1 = bf16[16,48,1024]{2,1,0:T(8,128)(2,1)S(1)} async-done(((bf16[16,48,1024]{2,1,0:T(8,128)(2,1)}), bf16[16,48,1024]{2,1,0:T(8,128)(2,1)S(1)}, u32[]{:S(2)}, u32[]{:S(2)}) %all-to-all-start.1) | async-done | bytes 1572896 | tf_op jit(solution)/shard_map/all_to_all | solution.py:232
  259.3 2.7 %bitcast_dynamic-update-slice_fusion = bf16[2,192,4096]{2,1,0:T(8,128)(2,1)} fusion(bf16[2,192,4096]{2,1,0:T(8,128)(2,1)} %get-tuple-element.26, s32[]{:T(128)S(6)} %select_n.21, bf16[192,4096]{1,0:T(8,128)(2,1)} %collective-permute-done.6), kind=kLoop, calls=%fused_computation.2 | loop fusion | bytes 3145732 | tf_op jit(solution)/shard_map/jit(dynamic_update_index_in_dim)/dynamic_update_slice | solution.py:228
  (41 shorter events, 5.9 us)
Async XLA Ops:
  7.2 113.1 %all-gather.3.cloned.1.call-start = ((), (), s32[]{:S(2)}) async-start(), calls=%async_computation.4 | async-start | bytes 33816576 | tf_op jit(solution)/shard_map/all_gather | solution.py:148
  9.0 218.3 %reduce-scatter.2.cloned.1.call-start = ((), (), s32[]{:S(2)}) async-start(), calls=%async_computation.3 | async-start | bytes 7864320 | tf_op jit(solution)/shard_map/reduce_scatter | solution.py:201
  9.0 3.5 %copy-start.7 = (bf16[2,192,4096]{2,1,0:T(8,128)(2,1)S(1)}, bf16[2,192,4096]{2,1,0:T(8,128)(2,1)}, u32[]{:S(2)}) copy-start(bf16[2,192,4096]{2,1,0:T(8,128)(2,1)} %param.13) | copy-start | bytes 9437188
  12.5 3.0 %copy-start.8 = (bf16[2,192,4096]{2,1,0:T(8,128)(2,1)S(1)}, bf16[2,192,4096]{2,1,0:T(8,128)(2,1)}, u32[]{:S(2)}) copy-start(bf16[2,192,4096]{2,1,0:T(8,128)(2,1)} %param.12) | copy-start | bytes 9437188
  12.5 28.7 %collective-permute-start = (bf16[192,4096]{1,0:T(8,128)(2,1)}, bf16[192,4096]{1,0:T(8,128)(2,1)}, u32[]{:S(2)}, u32[]{:S(2)}) collective-permute-start(bf16[192,4096]{1,0:T(8,128)(2,1)} %get-tuple-element.31), channel_id=1, source_target_pairs={{0,1},{1,0},{2,3},{3,2},{4,5},{5,4},{6,7},{7,6},{8,9},{9,8},{10,11... | collective-permute-start | bytes 4718600 | tf_op jit(solution)/shard_map/ppermute | solution.py:134
  14.5 2.4 copy-start.9
  14.5 3.2 %copy-start.10 = (f32[128,8]{0,1:T(8,128)S(1)}, f32[128,8]{0,1:T(8,128)}, u32[]{:S(2)}) copy-start(f32[128,8]{0,1:T(8,128)} %param.9) | copy-start | bytes 12292
  14.5 22.7 %collective-permute-start.2 = (bf16[192,4096]{1,0:T(8,128)(2,1)}, bf16[192,4096]{1,0:T(8,128)(2,1)}, u32[]{:S(2)}, u32[]{:S(2)}) collective-permute-start(bf16[192,4096]{1,0:T(8,128)(2,1)} %get-tuple-element.29), channel_id=1, source_target_pairs={{0,1},{1,0},{2,3},{3,2},{4,5},{5,4},{6,7},{7,6},{8,9},{9,8},{10,11... | collective-permute-start | bytes 4718600 | tf_op jit(solution)/shard_map/ppermute | solution.py:134
  17.0 24.2 %collective-permute-start.1 = (bf16[192,4096]{1,0:T(8,128)(2,1)}, bf16[192,4096]{1,0:T(8,128)(2,1)}, u32[]{:S(2)}, u32[]{:S(2)}) collective-permute-start(bf16[192,4096]{1,0:T(8,128)(2,1)} %get-tuple-element.33), channel_id=1, source_target_pairs={{0,1},{1,0},{2,3},{3,2},{4,5},{5,4},{6,7},{7,6},{8,9},{9,8},{10,11... | collective-permute-start | bytes 4718600 | tf_op jit(solution)/shard_map/ppermute | solution.py:134
  120.2 32.3 %copy-start = (bf16[768,4096]{1,0:T(8,128)(2,1)S(1)}, bf16[768,4096]{1,0:T(8,128)(2,1)}, u32[]{:S(2)}) copy-start(bf16[768,4096]{1,0:T(8,128)(2,1)} %pad_maximum_fusion.wgu_ref) | copy-start | bytes 18874372
  152.6 1.3 copy-start.4
  161.2 2.6 copy-start.1
  163.8 1.3 copy-start.5
  165.1 2.8 %copy-start.3 = (bf16[768,4096]{1,0:T(8,128)(2,1)S(1)}, bf16[768,4096]{1,0:T(8,128)(2,1)}, u32[]{:S(2)}) copy-start(bf16[768,4096]{1,0:T(8,128)(2,1)} %get-tuple-element.20.xs_ref) | copy-start | bytes 18874372
  167.9 1.1 copy-start.6
  180.9 53.3 %collective-permute-start.4 = (bf16[192,4096]{1,0:T(8,128)(2,1)}, bf16[192,4096]{1,0:T(8,128)(2,1)}, u32[]{:S(2)}, u32[]{:S(2)}) collective-permute-start(bf16[192,4096]{1,0:T(8,128)(2,1)} %get-tuple-element.23), channel_id=1, source_target_pairs={{0,1},{1,0},{2,3},{3,2},{4,5},{5,4},{6,7},{7,6},{8,9},{9,8},{10,11... | collective-permute-start | bytes 4718600 | tf_op jit(solution)/shard_map/ppermute | solution.py:134
  181.2 55.8 %collective-permute-start.5 = (bf16[192,4096]{1,0:T(8,128)(2,1)}, bf16[192,4096]{1,0:T(8,128)(2,1)}, u32[]{:S(2)}, u32[]{:S(2)}) collective-permute-start(bf16[192,4096]{1,0:T(8,128)(2,1)} %get-tuple-element.25), channel_id=1, source_target_pairs={{0,1},{1,0},{2,3},{3,2},{4,5},{5,4},{6,7},{7,6},{8,9},{9,8},{10,11... | collective-permute-start | bytes 4718600 | tf_op jit(solution)/shard_map/ppermute | solution.py:134
  181.4 77.9 %collective-permute-start.6 = (bf16[192,4096]{1,0:T(8,128)(2,1)S(1)}, bf16[192,4096]{1,0:T(8,128)(2,1)}, u32[]{:S(2)}, u32[]{:S(2)}) collective-permute-start(bf16[192,4096]{1,0:T(8,128)(2,1)S(1)} %get-tuple-element.27), channel_id=1, source_target_pairs={{0,1},{1,0},{2,3},{3,2},{4,5},{5,4},{6,7},{7,6},{8,9},{9,8},{10,11... | collective-permute-start | bytes 4718600 | tf_op jit(solution)/shard_map/ppermute | solution.py:134
  227.2 31.5 %all-to-all-start.1 = ((bf16[16,48,1024]{2,1,0:T(8,128)(2,1)}), bf16[16,48,1024]{2,1,0:T(8,128)(2,1)S(1)}, u32[]{:S(2)}, u32[]{:S(2)}) async-start(bf16[16,48,1024]{2,1,0:T(8,128)(2,1)} %bitcast.31), calls=%async_computation.2 | async-start | bytes 3145728 | tf_op jit(solution)/shard_map/all_to_all | solution.py:232
  234.2 24.5 %copy-start.2 = (f32[16,256]{1,0:T(8,128)S(1)}, f32[16,256]{1,0:T(8,128)}, u32[]{:S(2)}) copy-start(f32[16,256]{1,0:T(8,128)} %places.1.pw_ref) | copy-start | bytes 49156
  259.2 2.8 %collective-permute-start.3 = (f32[128,512]{1,0:T(8,128)S(1)}, f32[128,512]{1,0:T(8,128)S(1)}, u32[]{:S(2)}, u32[]{:S(2)}) collective-permute-start(f32[128,512]{1,0:T(8,128)S(1)} %get-tuple-element.18), channel_id=1, source_target_pairs={{0,1},{1,0},{2,3},{3,2},{4,5},{5,4},{6,7},{7,6},{8,9},{9,8},{10,11... | collective-permute-start | bytes 786440 | tf_op jit(solution)/shard_map/ppermute | solution.py:134
Sparse Core Ops, SparseCore 0:
  11.0 109.1 all-gather.2
  163.9 63.2 reduce-scatter.1

commit v2 on v0

v2 whole, which is shorter than its diff:
```python
import jax
import jax.numpy as jnp
from jax import lax
from jax.experimental import pallas as pl
from jax.experimental.pallas import tpu as pltpu
from jax.sharding import Mesh
from jax.sharding import PartitionSpec as P

BF = jnp.bfloat16
F32 = jnp.float32
CAP = 48
ZY = ("z", "y")
ZYX = ("z", "y", "x")
VMEM = pl.BlockSpec(memory_space=pltpu.VMEM)
SMEM = pl.BlockSpec(memory_space=pltpu.SMEM)
SWAP = [(0, 1), (1, 0)]


def params(mib):
    return pltpu.CompilerParams(vmem_limit_bytes=mib * 1024 * 1024)


def cost(flops, nbytes):
    return pl.CostEstimate(flops=int(flops), bytes_accessed=int(nbytes), transcendentals=0)


def nt(a, b):
    return lax.dot_general(a, b, (((1,), (1,)), ((), ())), preferred_element_type=F32)


def mm(a, b):
    return jnp.dot(a, b, preferred_element_type=F32)


def swap(v):
    return lax.ppermute(v, "c", SWAP)


def like(shape, dtype=BF):
    return jax.ShapeDtypeStruct(shape, dtype)


def prefetched(grid, in_specs, out_specs, scratch=()):
    return pltpu.PrefetchScalarGridSpec(
        num_scalar_prefetch=1, grid=grid, in_specs=in_specs, out_specs=out_specs, scratch_shapes=list(scratch)
    )


def places_kernel(ids_ref, wts_ref, out_ref):
    rows, top = ids_ref.shape
    lane = lax.broadcasted_iota(jnp.int32, (rows, 128), 1)
    hit = jnp.zeros((rows, 128), F32)
    wt = jnp.zeros((rows, 128), F32)
    for k in range(top):
        same = ids_ref[:, k : k + 1] == lane
        hit = hit + same.astype(F32)
        wt = wt + jnp.where(same, wts_ref[:, k : k + 1], 0.0)
    r = lax.broadcasted_iota(jnp.int32, (rows, rows), 0)
    q = lax.broadcasted_iota(jnp.int32, (rows, rows), 1)
    before = mm((q < r).astype(BF), hit.astype(BF))
    pos = jnp.where(hit > 0.5, before, -1.0)
    out_ref[:, 0:rows] = pos.T[0:32, :]
    out_ref[:, rows : 2 * rows] = wt.T[0:32, :]


def chosen(row):
    p = lax.broadcasted_iota(jnp.int32, (CAP, row.shape[1]), 0).astype(F32)
    return row == p


def outgoing_kernel(c_ref, g_ref, u_ref, d_ref, out_ref):
    out_ref[0:2] = g_ref[...]
    out_ref[2:4] = u_ref[...]
    out_ref[4:6] = d_ref[...]


def assemble_kernel(c_ref, g_ref, u_ref, d_ref, in_ref, wgu_ref, wd_ref):
    f = g_ref.shape[1]

    def place(low, high):
        for e in range(2):
            wgu_ref[e, low : low + f] = g_ref[e]
            wgu_ref[e, high : high + f] = in_ref[e]
            wgu_ref[e, 2 * f + low : 3 * f + low] = u_ref[e]
            wgu_ref[e, 2 * f + high : 3 * f + high] = in_ref[2 + e]
            wd_ref[e, low : low + f] = d_ref[e]
            wd_ref[e, high : high + f] = in_ref[4 + e]

    @pl.when(c_ref[0] == 0)
    def _():
        place(0, f)

    @pl.when(c_ref[0] == 1)
    def _():
        place(f, 0)


def select_kernel(pw_ref, ag_ref, xs_ref, gs_ref):
    step = pl.program_id(0)
    none = jnp.zeros((CAP, 128), F32)
    picks, scales = [], []
    for e in range(2):
        for i in range(2):
            row = pw_ref[pl.ds(4 * step + 2 * i + e, 1), :]
            pick = chosen(row[:, 0:128])
            scales.append(jnp.sum(jnp.where(pick, row[:, 128:256], 0.0), axis=1, keepdims=True))
            wide = pick.astype(F32)
            picks.append(jnp.concatenate([wide, none] if i == 0 else [none, wide], axis=1))
    pick = jnp.concatenate(picks, axis=0).astype(BF)
    scale = jnp.concatenate(scales, axis=0)
    for x in range(4):
        both = jnp.concatenate([ag_ref[x], ag_ref[4 + x]], axis=0)
        got = mm(pick, both)
        cols = slice(x * 512, (x + 1) * 512)
        xv = got[:, 0:512].astype(BF)
        gv = (got[:, 512:1024] * scale).astype(BF)
        for e in range(2):
            xs_ref[e, :, cols] = xv[e * 2 * CAP : (e + 1) * 2 * CAP]
            gs_ref[e, :, cols] = gv[e * 2 * CAP : (e + 1) * 2 * CAP]


def hidden_kernel(e_ref, xs_ref, gs_ref, wgu_ref, wd_ref, out_ref):
    n = wgu_ref.shape[1]
    a = nt(xs_ref[0], wgu_ref[0])
    b = nt(gs_ref[0], wd_ref[0])

    @pl.when(pl.program_id(0) == 0)
    def _():
        out_ref[:, 0:n] = a
        out_ref[:, n:] = b

    @pl.when(pl.program_id(0) > 0)
    def _():
        out_ref[:, 0:n] += a
        out_ref[:, n:] += b


def act_kernel(h_ref, r_ref, out_ref):
    n = out_ref.shape[1] // 3
    h = h_ref[...] + r_ref[...]
    gate, up, d = h[:, 0:n], h[:, n : 2 * n], h[:, 2 * n :]
    sig = jax.nn.sigmoid(gate)
    silu = gate * sig
    out_ref[:, 0:n] = (d * up * sig * (1.0 + gate * (1.0 - sig))).astype(BF)
    out_ref[:, n : 2 * n] = (d * silu).astype(BF)
    out_ref[:, 2 * n :] = (silu * up).astype(BF)


def partial_kernel(e_ref, ad_ref, wgu_ref, *rest):
    out_ref = rest[-1]
    n = wgu_ref.shape[1]
    got = mm(ad_ref[:, 0:n], wgu_ref[0]).astype(BF)
    out_ref[:, 0, 0] = got.reshape(16, CAP, 512)


def weight_kernel(c_ref, mine_ref, theirs_ref, xs_ref, gs_ref, gg_ref, gu_ref, gd_ref, send_ref, dt):
    f = gg_ref.shape[1]
    first = pl.program_id(1) == 0

    @pl.when(first & (pl.program_id(0) == 0))
    def _():
        dt[...] = mine_ref[...].astype(F32).T.astype(BF)

    @pl.when(first & (pl.program_id(0) == 1))
    def _():
        dt[...] = theirs_ref[...].astype(F32).T.astype(BF)

    c = c_ref[0]
    outs = (gg_ref, gu_ref, gd_ref)
    for i in range(3):
        rows = xs_ref if i < 2 else gs_ref
        keep = pl.ds(pl.multiple_of(2 * f * i + f * c, f), f)
        away = pl.ds(pl.multiple_of(2 * f * i + f * (1 - c), f), f)
        outs[i][0] = mm(dt[keep, :], rows[0]).astype(BF)
        send_ref[0, i] = mm(dt[away, :], rows[0]).astype(BF)


def settle_kernel(c_ref, in_ref, a_ref, b_ref, d_ref, gg_ref, gu_ref, gd_ref):
    for e in range(2):
        gg_ref[e] = in_ref[e, 0]
        gu_ref[e] = in_ref[e, 1]
        gd_ref[e] = in_ref[e, 2]


def combine_kernel(c_ref, pw_ref, ret_ref, out_ref):
    low = c_ref[0] == 0
    picks = []
    for e in range(16):
        a, b = pw_ref[2 * e : 2 * e + 1, 0:128], pw_ref[2 * e + 1 : 2 * e + 2, 0:128]
        picks.append(chosen(jnp.where(low, a, b)).astype(F32))
        picks.append(chosen(jnp.where(low, b, a)).astype(F32))
    pick = jnp.concatenate(picks, axis=0).T.astype(BF)
    total = mm(pick, ret_ref[:, 0].reshape(32 * CAP, 512))
    for x in range(1, 4):
        total = total + mm(pick, ret_ref[:, x].reshape(32 * CAP, 512))
    out_ref[...] = total.astype(BF)


def shards(tokens, expert_ids, route_weights, grad_out, w_gate, w_up, w_down):
    rows, width = tokens.shape
    f = w_gate.shape[1]
    slots = 16 * CAP
    half = width // 2
    c = lax.axis_index("c")
    x = lax.axis_index("x")
    cs = jnp.reshape(c, (1,)).astype(jnp.int32)
    others = 1 - cs

    at = x * 1024 + c * 512
    own = jnp.concatenate([lax.dynamic_slice_in_dim(v, at, 512, 1) for v in (tokens, grad_out)], axis=1)
    gathered = lax.all_gather(own, ZYX, axis=0, tiled=False)

    pw_own = pl.pallas_call(
        places_kernel, out_shape=like((32, 2 * rows), F32), in_specs=[VMEM, VMEM], out_specs=VMEM, name="places"
    )(expert_ids, route_weights)
    pw = lax.all_to_all(pw_own, ZY, split_axis=0, concat_axis=0, tiled=True)

    strip = (2, f, 512)
    outgoing = pl.pallas_call(
        outgoing_kernel,
        grid_spec=prefetched(
            (4,),
            [pl.BlockSpec(strip, lambda j, cr: (0, 0, 2 * j + 1 - cr[0]))] * 3,
            pl.BlockSpec((6, f, 512), lambda j, cr: (0, 0, j)),
        ),
        out_shape=like((6, f, half)),
        cost_estimate=cost(0, 9.4e6),
        name="outgoing",
    )(cs, w_gate, w_up, w_down)
    incoming = swap(outgoing)
    wgu, wd = pl.pallas_call(
        assemble_kernel,
        grid_spec=prefetched(
            (4,),
            [pl.BlockSpec(strip, lambda j, cr: (0, 0, 2 * j + cr[0]))] * 3
            + [pl.BlockSpec((6, f, 512), lambda j, cr: (0, 0, j))],
            [
                pl.BlockSpec((2, 4 * f, 512), lambda j, cr: (0, 0, j)),
                pl.BlockSpec((2, 2 * f, 512), lambda j, cr: (0, 0, j)),
            ],
        ),
        out_shape=(like((2, 4 * f, half)), like((2, 2 * f, half))),
        compiler_params=params(32),
        cost_estimate=cost(0, 19e6),
        name="assemble",
    )(cs, w_gate, w_up, w_down, incoming)

    xs, gs = pl.pallas_call(
        select_kernel,
        grid=(8,),
        out_shape=(like((2, slots, half)), like((2, slots, half))),
        in_specs=[VMEM, pl.BlockSpec((8, rows, 1024), lambda b: (b, 0, 0))],
        out_specs=(
            pl.BlockSpec((2, 2 * CAP, half), lambda b: (0, b, 0)),
            pl.BlockSpec((2, 2 * CAP, half), lambda b: (0, b, 0)),
        ),
        compiler_params=params(32),
        cost_estimate=cost(3.2e9, 30e6),
        name="select",
    )(pw, gathered)

    def hidden(which):
        return pl.pallas_call(
            hidden_kernel,
            grid_spec=prefetched(
                (4,),
                [
                    pl.BlockSpec((1, slots, 512), lambda j, er: (er[0], 0, j)),
                    pl.BlockSpec((1, slots, 512), lambda j, er: (er[0], 0, j)),
                    pl.BlockSpec((1, 4 * f, 512), lambda j, er: (er[0], 0, j)),
                    pl.BlockSpec((1, 2 * f, 512), lambda j, er: (er[0], 0, j)),
                ],
                pl.BlockSpec((slots, 6 * f), lambda j, er: (0, 0)),
            ),
            out_shape=like((slots, 6 * f), F32),
            compiler_params=params(40),
            cost_estimate=cost(2 * slots * half * 6 * f, 15e6),
            name="hidden",
        )(which, xs, gs, wgu, wd)

    received = swap(hidden(others))
    mine = pl.pallas_call(
        act_kernel,
        grid=(4,),
        out_shape=like((slots, 6 * f)),
        in_specs=[pl.BlockSpec((slots // 4, 6 * f), lambda j: (j, 0))] * 2,
        out_specs=pl.BlockSpec((slots // 4, 6 * f), lambda j: (j, 0)),
        compiler_params=params(32),
        cost_estimate=cost(1e7, 9e6),
        name="act",
    )(hidden(cs), received)
    theirs = swap(mine)

    def partial(which, place, ad, into):
        specs = [VMEM, pl.BlockSpec((1, 4 * f, 512), lambda j, er: (er[0], 0, j))]
        out = like((16, 4, 2, CAP, 512))
        return pl.pallas_call(
            partial_kernel,
            grid_spec=prefetched(
                (4,),
                specs + [pl.BlockSpec(memory_space=pl.ANY)] * len(into),
                pl.BlockSpec((16, 1, 1, CAP, 512), lambda j, er: (0, j, place, 0, 0)),
            ),
            out_shape=out,
            input_output_aliases={3: 0} if into else {},
            compiler_params=params(32),
            cost_estimate=cost(2 * slots * half * 4 * f, 8e6),
            name="partial",
        )(which, ad, wgu, *into)

    sent = partial(others, 1, theirs, [partial(cs, 0, mine, [])])
    returned = lax.all_to_all(sent.reshape(64, 2, CAP, 512), ZYX, split_axis=0, concat_axis=0, tiled=True)

    pick = lambda i, cr: jnp.where(i == 0, cr[0], 1 - cr[0])
    gg, gu, gd, send = pl.pallas_call(
        weight_kernel,
        grid_spec=prefetched(
            (2, 4),
            [
                VMEM,
                VMEM,
                pl.BlockSpec((1, slots, 512), lambda i, j, cr: (pick(i, cr), 0, j)),
                pl.BlockSpec((1, slots, 512), lambda i, j, cr: (pick(i, cr), 0, j)),
            ],
            [pl.BlockSpec((1, f, 512), lambda i, j, cr: (pick(i, cr), 0, 2 * j + cr[0]))] * 3
            + [pl.BlockSpec((1, 3, f, 512), lambda i, j, cr: (pick(i, cr), 0, 0, j))],
            [pltpu.VMEM((6 * f, slots), BF)],
        ),
        out_shape=[like((2, f, width))] * 3 + [like((2, 3, f, half))],
        compiler_params=params(40),
        cost_estimate=cost(4 * slots * half * 6 * f, 24e6),
        name="weights",
    )(cs, mine, theirs, xs, gs)
    strips = pl.BlockSpec(strip, lambda j, cr: (0, 0, 2 * j + 1 - cr[0]))
    grads = pl.pallas_call(
        settle_kernel,
        grid_spec=prefetched(
            (4,),
            [pl.BlockSpec((2, 3, f, 512), lambda j, cr: (0, 0, 0, j))] + [pl.BlockSpec(memory_space=pl.ANY)] * 3,
            [strips] * 3,
        ),
        out_shape=[like((2, f, width))] * 3,
        input_output_aliases={2: 0, 3: 1, 4: 2},
        cost_estimate=cost(0, 9.4e6),
        name="settle",
    )(cs, swap(send), gg, gu, gd)

    grad_tokens = pl.pallas_call(
        combine_kernel,
        out_shape=like((rows, 512)),
        in_specs=[SMEM, VMEM, VMEM],
        out_specs=VMEM,
        compiler_params=params(40),
        cost_estimate=cost(1e9, 6.5e6),
        name="combine",
    )(cs, pw_own, returned.reshape(16, 4, 2 * CAP, 512))
    return (grad_tokens, *grads)


def solution(mesh):
    fine = Mesh(mesh.devices.reshape(4, 4, 4, 2), ("z", "y", "x", "c"))
    rows = P(ZY, None)
    weights = P(ZY, ("x", "c"), None)
    return jax.shard_map(
        shards,
        mesh=fine,
        in_specs=(rows, rows, rows, rows, weights, weights, weights),
        out_specs=(P(ZY, ("x", "c")), weights, weights, weights),
        check_vma=False,
    )
```

time: 604 us -> 277 us (0.46)
  waiting for transfers between devices: 373 us -> 140 us
  matrix products: 85.7 us -> 0 us
  Pallas kernels: 0 us -> 75.2 us
  local copies, waits for them, and re-layouts: 83.5 us -> 24.3 us
  other arithmetic: 24.4 us -> 0.73 us
    all_to_all x3 -> x2, waiting for transfers between devices: 318 us -> 59.9 us  [the longest x1 52.3 us: shards(): lax.all_to_all(sent.reshape(64, 2, CAP, 512), ZYX, split_axis=0, concat_a...]
    dot_general x8 -> x0, matrix products: 85.7 us -> none  [the longest x1 15.8 us: shards(): jnp.einsum('secf,efd->secd', d_up, w_up, preferred_element_type=jnp.float32)]
    pallas_call x0 -> x12, Pallas kernels: none -> 75.2 us  [the longest x2 19 us: hidden(): pl.pallas_call(hidden_kernel, grid_spec=prefetched((4,), [pl.BlockSpec((1...]
    all_gather x0 -> x1, waiting for transfers between devices: none -> 72.1 us  [shards(): gathered = lax.all_gather(own, ZYX, axis=0, tiled=False)]
    gather x4 -> x0, local copies, waits for them, and re-layouts: 62 us -> none  [the longest x1 23.5 us: shards(): x_send = token_pad[token_index]]
    reduce_scatter x1 -> x0, waiting for transfers between devices: 54.3 us -> none  [shards(): lax.psum_scatter(partial_value.astype(jnp.bfloat16), 'tensor', scatter_di...]
    unnamed x10 -> x36, local copies, waits for them, and re-layouts: 1.02 us -> 21.9 us
    convert_element_type x2 -> x0, other arithmetic: 11.7 us -> none  [the longest x1 11.7 us: shards(): (weight_pad[owner][:, None] * grad_pad[token_index].astype(jnp.float32))....]
  transfers between devices with their start and end apart: 4 -> 7, of which waited for: 4 -> 4; matrix products, arithmetic and copies ran while one was open for 16% -> 1% of each run, Pallas kernels for 0% -> 16%
where the time goes in v2:
time: 277 us; the launch traced here: 272 us
  waiting for transfers between devices  140 us (51%)
  Pallas kernels  75.2 us (27%)
  local copies, waits for them, and re-layouts  24.3 us (9%)
  starting transfers between devices  17.5 us (6%)
  between operations  14.2 us (5%)
    all_gather x1, waiting for transfers between devices, shards(): gathered = lax.all_gather(own, ZYX, axis=0, tiled=False)  72.1 us
    all_to_all x1, waiting for transfers between devices, shards(): lax.all_to_all(sent.reshape(64, 2, CAP, 512), ZYX, split_axis=0, concat_a...  52.3 us
    unnamed x36, local copies, waits for them, and re-layouts  21.9 us
    pallas_call x2, Pallas kernels, hidden(): pl.pallas_call(hidden_kernel, grid_spec=prefetched((4,), [pl.BlockSpec((1...  19 us
    pallas_call x1, Pallas kernels, shards(): pl.pallas_call(weight_kernel, grid_spec=prefetched((2, 4), [VMEM, VMEM, p...  12.9 us
    pallas_call x1, Pallas kernels, shards(): pl.pallas_call(select_kernel, grid=(8,), out_shape=(like((2, slots, half)...  10.5 us
    all_to_all x1, starting transfers between devices, shards(): lax.all_to_all(sent.reshape(64, 2, CAP, 512), ZYX, split_axis=0, concat_a...  8.87 us
    all_to_all x1, starting transfers between devices, shards(): pw = lax.all_to_all(pw_own, ZY, split_axis=0, concat_axis=0, tiled=True)  8.13 us
  transfers between devices with their start and end apart: 7, of which 4 were waited for; matrix products, arithmetic and copies ran while one was open for 1% of the time, Pallas kernels for 16%

profile of v2, /device:TPU:0, one launch (start us, length us, event | category | flops | bytes accessed | tf_op | source)
XLA Modules:
  0.0 271.9 jit_solution(14090540965175634715)
XLA Ops:
  9.0 5.3 %outgoing.1 = bf16[6,192,2048]{2,1,0:T(8,128)(2,1)} custom-call(s32[1]{0:T(128)} %bitcast.c_ref.e_ref, bf16[2,192,4096]{2,1,0:T(8,128)(2,1)} %g_ref.3, bf16[2,192,4096]{2,1,0:T(8,128)(2,1)} %u_ref.3, bf16[2,192,4096]{2,1,0:T(8,128)(2,1)} %d_ref.3), custom_call_target="tpu_custom_call" | custom-call | bytes 9400000 | tf_op jit(solution)/shard_map/outgoing/pallas_call | solution.py:219
  15.8 2.0 places.1.pw_ref
  19.2 8.1 %all-to-all-start = ((f32[16,2,256]{2,1,0:T(2,128)}), f32[16,2,256]{2,1,0:T(2,128)S(1)}, u32[]{:S(2)}, u32[]{:S(2)}) async-start(f32[16,2,256]{2,1,0:T(2,128)} %all_to_all.10), calls=%async_computation | async-start | bytes 65536 | tf_op jit(solution)/shard_map/all_to_all | solution.py:216
  27.3 7.6 %all-to-all-done = f32[16,2,256]{2,1,0:T(2,128)S(1)} async-done(((f32[16,2,256]{2,1,0:T(2,128)}), f32[16,2,256]{2,1,0:T(2,128)S(1)}, u32[]{:S(2)}, u32[]{:S(2)}) %all-to-all-start) | async-done | bytes 32800 | tf_op jit(solution)/shard_map/all_to_all | solution.py:216
  35.0 1.9 copy-done.6
  38.8 5.8 %assemble.1 = (bf16[2,768,2048]{2,1,0:T(8,128)(2,1)}, bf16[2,384,2048]{2,1,0:T(8,128)(2,1)S(1)}) custom-call(s32[1]{0:T(128)} %bitcast.c_ref.e_ref, bf16[2,192,4096]{2,1,0:T(8,128)(2,1)S(1)} %copy-done.5, bf16[2,192,4096]{2,1,0:T(8,128)(2,1)S(1)} %copy-done.6, bf16[2,192,4096]{2,1,0:T(8,128)(2,1)S(1)} %copy-done.7, ...), custom_call_target="tpu_custom_call" | custom-call | bytes 19000000 | tf_op jit(solution)/shard_map/assemble/pallas_call | solution.py:231
  46.2 72.1 %all-gather.3.cloned.1.call-done = bf16[8192,1024]{1,0:T(8,128)(2,1)} async-done(((bf16[128,1024]{1,0:T(8,128)(2,1)}), bf16[8192,1024]{1,0:T(8,128)(2,1)}) %all-gather.3.cloned.1.call-update) | async-done | bytes 16777232 | tf_op jit(solution)/shard_map/all_gather | solution.py:211
  118.4 10.5 %select.1 = (bf16[2,768,2048]{2,1,0:T(8,128)(2,1)S(1)}, bf16[2,768,2048]{2,1,0:T(8,128)(2,1)S(1)}) custom-call(f32[32,256]{1,0:T(8,128)S(1)} %all_to_all.12.pw_ref, bf16[64,128,1024]{2,1,0:T(8,128)(2,1)} %bitcast.7), custom_call_target="tpu_custom_call" | custom-call | flops 3200000000 | bytes 30000000 | tf_op jit(solution)/shard_map/select/pallas_call | solution.py:248
  128.8 2.6 copy-done.4
  131.5 11.1 %hidden.3 = f32[768,1152]{1,0:T(8,128)} custom-call(s32[1]{0:T(128)S(6)} %sub.3.e_ref, bf16[2,768,2048]{2,1,0:T(8,128)(2,1)S(1)} %get-tuple-element.15.xs_ref, bf16[2,768,2048]{2,1,0:T(8,128)(2,1)} %copy-done.4, bf16[2,768,2048]{2,1,0:T(8,128)(2,1)} %get-tuple-element.17.wgu_ref, bf16[2,384,2048]{2,1,0:T(8,128)(2,1)S(1)} %copy-done.9), custom_call_target="tpu_custom_call" | custom-call | flops 3623878656 | bytes 15000000 | tf_op jit(solution)/shard_map/hidden/pallas_call | solution.py:263
  142.6 2.9 %copy-done.2 = bf16[2,768,2048]{2,1,0:T(8,128)(2,1)S(1)} copy-done((bf16[2,768,2048]{2,1,0:T(8,128)(2,1)S(1)}, bf16[2,768,2048]{2,1,0:T(8,128)(2,1)}, u32[]{:S(2)}) %copy-start.2) | copy-done | bytes 6291480
  147.5 7.9 %hidden.2.h_ref = f32[768,1152]{1,0:T(8,128)S(1)} custom-call(s32[1]{0:T(128)} %bitcast.c_ref.e_ref, bf16[2,768,2048]{2,1,0:T(8,128)(2,1)S(1)} %copy-done.2, bf16[2,768,2048]{2,1,0:T(8,128)(2,1)} %copy-done.4, bf16[2,768,2048]{2,1,0:T(8,128)(2,1)} %get-tuple-element.17.wgu_ref, bf16[2,384,2048]{2,1,0:T(8,128)(2,1)S(1)} %copy-done.10), custom_call_target="tpu_custom_call" | custom-call | flops 3623878656 | bytes 15000000 | tf_op jit(solution)/shard_map/hidden/pallas_call | solution.py:263
  155.4 3.1 %act.1.ad_ref.mine_ref = bf16[768,1152]{1,0:T(8,128)(2,1)S(1)} custom-call(f32[768,1152]{1,0:T(8,128)S(1)} %hidden.2.h_ref, f32[768,1152]{1,0:T(8,128)} %collective-permute-done.1.r_ref), custom_call_target="tpu_custom_call" | custom-call | flops 10000000 | bytes 9000000 | tf_op jit(solution)/shard_map/act/pallas_call | solution.py:282
  158.9 3.6 %partial.2.rest_0_ = bf16[16,4,2,48,512]{4,3,2,1,0:T(8,128)(2,1)S(1)} custom-call(s32[1]{0:T(128)} %bitcast.c_ref.e_ref, bf16[768,1152]{1,0:T(8,128)(2,1)S(1)} %act.1.ad_ref.mine_ref, bf16[2,768,2048]{2,1,0:T(8,128)(2,1)S(1)} %bitcast.5), custom_call_target="tpu_custom_call" | custom-call | flops 2415919104 | bytes 8000000 | tf_op jit(solution)/shard_map/partial/pallas_call | solution.py:297
  162.5 3.6 %partial.3 = bf16[16,4,2,48,512]{4,3,2,1,0:T(8,128)(2,1)S(1)} custom-call(s32[1]{0:T(128)S(6)} %sub.3.e_ref, bf16[768,1152]{1,0:T(8,128)(2,1)S(1)} %collective-permute-done.2.ad_ref.theirs_ref, bf16[2,768,2048]{2,1,0:T(8,128)(2,1)S(1)} %bitcast.5, bf16[16,4,2,48,512]{4,3,2,1,0:T(8,128)(2,1)S(1)} %partial.2.rest_0_), custom_call_target="tpu_custom_call", output_to_operand_aliasing={{}: (3, {})} | custom-call | flops 2415919104 | bytes 8000000 | tf_op jit(solution)/shard_map/partial/pallas_call | solution.py:297
  166.1 2.6 copy-done
  168.6 8.9 %all-to-all-start.1 = ((bf16[64,2,48,512]{3,2,1,0:T(8,128)(2,1)}), bf16[64,2,48,512]{3,2,1,0:T(8,128)(2,1)}, u32[]{:S(2)}, u32[]{:S(2)}) async-start(bf16[64,2,48,512]{3,2,1,0:T(8,128)(2,1)} %bitcast.6), calls=%async_computation.1 | async-start | bytes 12582912 | tf_op jit(solution)/shard_map/all_to_all | solution.py:312
  177.5 2.8 %copy-done.3 = bf16[2,768,2048]{2,1,0:T(8,128)(2,1)S(1)} copy-done((bf16[2,768,2048]{2,1,0:T(8,128)(2,1)S(1)}, bf16[2,768,2048]{2,1,0:T(8,128)(2,1)}, u32[]{:S(2)}) %copy-start.3) | copy-done | bytes 6291480
  180.3 12.9 %weights.1 = (bf16[2,192,4096]{2,1,0:T(8,128)(2,1)}, bf16[2,192,4096]{2,1,0:T(8,128)(2,1)}, bf16[2,192,4096]{2,1,0:T(8,128)(2,1)}, bf16[2,3,192,2048]{3,2,1,0:T(8,128)(2,1)S(1)}) custom-call(s32[1]{0:T(128)} %bitcast.c_ref.e_ref, bf16[768,1152]{1,0:T(8,128)(2,1)S(1)} %act.1.ad_ref.mine_ref, bf16[768,1152]{1,0:T(8,128)(2,1)S(1)} %collective-permute-done.2.ad_ref.theirs_ref, ...), custom_call_target="tpu_custom_call" | custom-call | flops 7247757312 | bytes 24000000 | tf_op jit(solution)/shard_map/weights/pallas_call | solution.py:315
  193.2 7.9 %collective-permute-done.3.in_ref = bf16[2,3,192,2048]{3,2,1,0:T(8,128)(2,1)S(1)} collective-permute-done((bf16[2,3,192,2048]{3,2,1,0:T(8,128)(2,1)S(1)}, bf16[2,3,192,2048]{3,2,1,0:T(8,128)(2,1)S(1)}, u32[]{:S(2)}, u32[]{:S(2)}) %collective-permute-start.3) | collective-permute-done | bytes 4718624 | tf_op jit(solution)/shard_map/ppermute | solution.py:36
  201.1 2.1 copy-done.12
  203.2 5.0 %settle.1 = (bf16[2,192,4096]{2,1,0:T(8,128)(2,1)}, bf16[2,192,4096]{2,1,0:T(8,128)(2,1)}, bf16[2,192,4096]{2,1,0:T(8,128)(2,1)}) custom-call(s32[1]{0:T(128)} %bitcast.c_ref.e_ref, bf16[2,3,192,2048]{3,2,1,0:T(8,128)(2,1)} %copy-done.12, bf16[2,192,4096]{2,1,0:T(8,128)(2,1)} %get-tuple-element.20.a_ref, ...), custom_call_target="tpu_custom_call", output_to_operand_aliasing={{0}: (2, {}), {1}: (3, {}), {2}: (4, {})} | custom-call | bytes 9400000 | tf_op jit(solution)/shard_map/settle/pallas_call | solution.py:335
  208.3 52.3 %all-to-all-done.1 = bf16[64,2,48,512]{3,2,1,0:T(8,128)(2,1)} async-done(((bf16[64,2,48,512]{3,2,1,0:T(8,128)(2,1)}), bf16[64,2,48,512]{3,2,1,0:T(8,128)(2,1)}, u32[]{:S(2)}, u32[]{:S(2)}) %all-to-all-start.1) | async-done | bytes 6291488 | tf_op jit(solution)/shard_map/all_to_all | solution.py:312
  260.5 4.5 %combine.1 = bf16[128,512]{1,0:T(8,128)(2,1)} custom-call(s32[1]{0:T(128)} %bitcast.c_ref.e_ref, f32[32,256]{1,0:T(8,128)S(1)} %copy-done.11, bf16[16,4,96,512]{3,2,1,0:T(8,128)(2,1)} %bitcast.3.ret_ref), custom_call_target="tpu_custom_call" | custom-call | flops 1000000000 | bytes 6500000 | tf_op jit(solution)/shard_map/combine/pallas_call | solution.py:348
  (44 shorter events, 10.6 us)
Async XLA Ops:
  7.2 111.2 %all-gather.3.cloned.1.call-start = ((), (), s32[]{:S(2)}) async-start(), calls=%async_computation.2 | async-start | bytes 17039360 | tf_op jit(solution)/shard_map/all_gather | solution.py:211
  9.0 5.4 %copy-start.13 = (s32[128,8]{0,1:T(8,128)S(1)}, s32[128,8]{0,1:T(8,128)}, u32[]{:S(2)}) copy-start(s32[128,8]{0,1:T(8,128)} %param.8) | copy-start | bytes 12292
  9.0 6.1 %copy-start.14 = (f32[128,8]{0,1:T(8,128)S(1)}, f32[128,8]{0,1:T(8,128)}, u32[]{:S(2)}) copy-start(f32[128,8]{0,1:T(8,128)} %param.9) | copy-start | bytes 12292
  9.0 26.0 %copy-start.5 = (bf16[2,192,4096]{2,1,0:T(8,128)(2,1)S(1)}, bf16[2,192,4096]{2,1,0:T(8,128)(2,1)}, u32[]{:S(2)}) copy-start(bf16[2,192,4096]{2,1,0:T(8,128)(2,1)} %g_ref.3) | copy-start | bytes 9437188
  14.3 20.6 %collective-permute-start = (bf16[6,192,2048]{2,1,0:T(8,128)(2,1)}, bf16[6,192,2048]{2,1,0:T(8,128)(2,1)}, u32[]{:S(2)}, u32[]{:S(2)}) collective-permute-start(bf16[6,192,2048]{2,1,0:T(8,128)(2,1)} %outgoing.1), channel_id=1, source_target_pairs={{0,1},{1,0},{2,3},{3,2},{4,5},{5,4},{6,7},{7,6},{8,9},{9,8},{10,11... | collective-permute-start | bytes 14155784 | tf_op jit(solution)/shard_map/ppermute | solution.py:36
  19.2 15.7 %all-to-all-start = ((f32[16,2,256]{2,1,0:T(2,128)}), f32[16,2,256]{2,1,0:T(2,128)S(1)}, u32[]{:S(2)}, u32[]{:S(2)}) async-start(f32[16,2,256]{2,1,0:T(2,128)} %all_to_all.10), calls=%async_computation | async-start | bytes 65536 | tf_op jit(solution)/shard_map/all_to_all | solution.py:216
  35.0 1.9 copy-start.6
  36.9 1.9 copy-start.7
  44.6 1.7 copy-start.8
  118.3 13.1 %copy-start.9 = (bf16[2,384,2048]{2,1,0:T(8,128)(2,1)S(1)}, bf16[2,384,2048]{2,1,0:T(8,128)(2,1)}, u32[]{:S(2)}) copy-start(bf16[2,384,2048]{2,1,0:T(8,128)(2,1)} %copy-done.8) | copy-start | bytes 9437188
  128.8 2.6 copy-start.4
  131.5 11.2 %copy-start.1 = (bf16[2,768,2048]{2,1,0:T(8,128)(2,1)}, bf16[2,768,2048]{2,1,0:T(8,128)(2,1)S(1)}, u32[]{:S(2)}) copy-start(bf16[2,768,2048]{2,1,0:T(8,128)(2,1)S(1)} %get-tuple-element.15.xs_ref) | copy-start | bytes 18874372
  131.5 27.4 %slice-start = ((s8[6291456]{0:T(1024)(128)(4,1)}), s8[4194304]{0:T(1024)(128)(4,1)S(1)}, s32[]{:S(2)}) async-start(s8[6291456]{0:T(1024)(128)(4,1)} %bitcast.4), calls=%async_computation.3 | async-start | bytes 8388608
  142.6 16.3 %slice-start.1 = ((s8[6291456]{0:T(1024)(128)(4,1)}), s8[2097152]{0:T(1024)(128)(4,1)S(1)}, s32[]{:S(2)}) async-start(s8[6291456]{0:T(1024)(128)(4,1)} %bitcast.4), calls=%async_computation.4 | async-start | bytes 4194304
  142.6 12.7 %collective-permute-start.1 = (f32[768,1152]{1,0:T(8,128)}, f32[768,1152]{1,0:T(8,128)}, u32[]{:S(2)}, u32[]{:S(2)}) collective-permute-start(f32[768,1152]{1,0:T(8,128)} %hidden.3), channel_id=1, source_target_pairs={{0,1},{1,0},{2,3},{3,2},{4,5},{5,4},{6,7},{7,6},{8,9},{9,8},{10,11... | collective-permute-start | bytes 10616840 | tf_op jit(solution)/shard_map/ppermute | solution.py:36
  142.6 2.9 %copy-start.2 = (bf16[2,768,2048]{2,1,0:T(8,128)(2,1)S(1)}, bf16[2,768,2048]{2,1,0:T(8,128)(2,1)}, u32[]{:S(2)}) copy-start(bf16[2,768,2048]{2,1,0:T(8,128)(2,1)} %copy-done.1) | copy-start | bytes 18874372
  145.6 1.9 copy-start.10
  158.4 4.0 %collective-permute-start.2 = (bf16[768,1152]{1,0:T(8,128)(2,1)S(1)}, bf16[768,1152]{1,0:T(8,128)(2,1)S(1)}, u32[]{:S(2)}, u32[]{:S(2)}) collective-permute-start(bf16[768,1152]{1,0:T(8,128)(2,1)S(1)} %act.1.ad_ref.mine_ref), channel_id=1, source_target_pairs={{0,1},{1,0},{2,3},{3,2},{4,5},{5,4},{6,7},{7,6},{8,9},{9,8},{10,11... | collective-permute-start | bytes 5308424 | tf_op jit(solution)/shard_map/ppermute | solution.py:36
  166.0 2.6 copy-start
  168.6 91.9 %all-to-all-start.1 = ((bf16[64,2,48,512]{3,2,1,0:T(8,128)(2,1)}), bf16[64,2,48,512]{3,2,1,0:T(8,128)(2,1)}, u32[]{:S(2)}, u32[]{:S(2)}) async-start(bf16[64,2,48,512]{3,2,1,0:T(8,128)(2,1)} %bitcast.6), calls=%async_computation.1 | async-start | bytes 12582912 | tf_op jit(solution)/shard_map/all_to_all | solution.py:312
  177.5 2.8 %copy-start.3 = (bf16[2,768,2048]{2,1,0:T(8,128)(2,1)S(1)}, bf16[2,768,2048]{2,1,0:T(8,128)(2,1)}, u32[]{:S(2)}) copy-start(bf16[2,768,2048]{2,1,0:T(8,128)(2,1)} %copy-done.1) | copy-start | bytes 18874372
  193.2 7.9 %collective-permute-start.3 = (bf16[2,3,192,2048]{3,2,1,0:T(8,128)(2,1)S(1)}, bf16[2,3,192,2048]{3,2,1,0:T(8,128)(2,1)S(1)}, u32[]{:S(2)}, u32[]{:S(2)}) collective-permute-start(bf16[2,3,192,2048]{3,2,1,0:T(8,128)(2,1)S(1)} %get-tuple-element.19), channel_id=1, source_target_pairs={{0,1},{1,0},{2,3},{3,2},{4,5},{5,4},{6,7},{7,6},{8,9},{9,8},{10,11... | collective-permute-start | bytes 14155784 | tf_op jit(solution)/shard_map/ppermute | solution.py:36
  201.1 2.1 copy-start.12
  203.2 57.3 %copy-start.11 = (f32[32,256]{1,0:T(8,128)S(1)}, f32[32,256]{1,0:T(8,128)}, u32[]{:S(2)}) copy-start(f32[32,256]{1,0:T(8,128)} %places.1.pw_ref) | copy-start | bytes 98308
Sparse Core Ops, SparseCore 0:
  11.5 106.8 all-gather.2

commit v3 on v2

--- a/solution.py
+++ b/solution.py
@@ -21,7 +21,7 @@
 
 
 def cost(flops, nbytes):
-    return pl.CostEstimate(flops=int(flops), bytes_accessed=int(nbytes), transcendentals=0)
+    return pl.CostEstimate(flops=int(flops / 1e3), bytes_accessed=int(nbytes / 1e3), transcendentals=0)
 
 
 def nt(a, b):
@@ -34,6 +34,31 @@
 
 def swap(v):
     return lax.ppermute(v, "c", SWAP)
+
+
+def pairs(to):
+    spot = lambda z, y, x, c: ((z % 4 * 4 + y % 4) * 4 + x % 4) * 2 + c
+    places = [(z, y, x, c) for z in range(4) for y in range(4) for x in range(4) for c in range(2)]
+    return [(spot(*p), spot(*to(*p))) for p in places]
+
+
+def first(s):
+    return pairs(lambda z, y, x, c: (z + s, y, x, c) if c == 0 else (z, y + s, x, c))
+
+
+def second(s):
+    return pairs(lambda z, y, x, c: (z, y + s, x, c) if c == 0 else (z + s, y, x, c))
+
+
+along = pairs(lambda z, y, x, c: (z, y, x + 1 if c == 0 else x - 1, c))
+
+
+def hop(v, to):
+    return lax.ppermute(v, ("z", "y", "x", "c"), to)
+
+
+def together(*v):
+    return lax.optimization_barrier(v)
 
 
 def like(shape, dtype=BF):
@@ -46,21 +71,28 @@
     )
 
 
-def places_kernel(ids_ref, wts_ref, out_ref):
-    rows, top = ids_ref.shape
-    lane = lax.broadcasted_iota(jnp.int32, (rows, 128), 1)
-    hit = jnp.zeros((rows, 128), F32)
-    wt = jnp.zeros((rows, 128), F32)
+def pack_kernel(at_ref, ids_ref, wts_ref, t0, t1, g0, g1, g2, g3, out_ref):
+    top, rows = ids_ref.shape
+    expert = lax.broadcasted_iota(jnp.int32, (32, rows), 0)
+    hit = jnp.zeros((32, rows), F32)
+    wt = jnp.zeros((32, rows), F32)
     for k in range(top):
-        same = ids_ref[:, k : k + 1] == lane
+        same = ids_ref[k : k + 1, :] == expert
         hit = hit + same.astype(F32)
-        wt = wt + jnp.where(same, wts_ref[:, k : k + 1], 0.0)
+        wt = wt + jnp.where(same, wts_ref[k : k + 1, :], 0.0)
     r = lax.broadcasted_iota(jnp.int32, (rows, rows), 0)
     q = lax.broadcasted_iota(jnp.int32, (rows, rows), 1)
-    before = mm((q < r).astype(BF), hit.astype(BF))
+    before = mm(hit.astype(BF), (r < q).astype(BF))
     pos = jnp.where(hit > 0.5, before, -1.0)
-    out_ref[:, 0:rows] = pos.T[0:32, :]
-    out_ref[:, rows : 2 * rows] = wt.T[0:32, :]
+    high = wt.astype(BF)
+    rest = wt - high.astype(F32)
+    mid = rest.astype(BF)
+    low = (rest - mid.astype(F32)).astype(BF)
+    out_ref[:, 0:512] = t0[...]
+    out_ref[:, 512:1024] = t1[...]
+    out_ref[:, 1024:1152] = jnp.concatenate([pos.astype(BF), high, mid, low], axis=0)
+    for i, ref in enumerate((g0, g1, g2, g3)):
+        out_ref[:, 1152 + i * 512 : 1664 + i * 512] = ref[...]
 
 
 def chosen(row):
@@ -95,50 +127,47 @@
         place(f, 0)
 
 
-def select_kernel(pw_ref, ag_ref, xs_ref, gs_ref):
-    step = pl.program_id(0)
-    none = jnp.zeros((CAP, 128), F32)
+def picked(info_ref, meta, held):
+    held[...] = meta.astype(F32)
     picks, scales = [], []
-    for e in range(2):
-        for i in range(2):
-            row = pw_ref[pl.ds(4 * step + 2 * i + e, 1), :]
-            pick = chosen(row[:, 0:128])
-            scales.append(jnp.sum(jnp.where(pick, row[:, 128:256], 0.0), axis=1, keepdims=True))
-            wide = pick.astype(F32)
-            picks.append(jnp.concatenate([wide, none] if i == 0 else [none, wide], axis=1))
-    pick = jnp.concatenate(picks, axis=0).astype(BF)
-    scale = jnp.concatenate(scales, axis=0)
-    for x in range(4):
-        both = jnp.concatenate([ag_ref[x], ag_ref[4 + x]], axis=0)
-        got = mm(pick, both)
-        cols = slice(x * 512, (x + 1) * 512)
-        xv = got[:, 0:512].astype(BF)
-        gv = (got[:, 512:1024] * scale).astype(BF)
-        for e in range(2):
-            xs_ref[e, :, cols] = xv[e * 2 * CAP : (e + 1) * 2 * CAP]
-            gs_ref[e, :, cols] = gv[e * 2 * CAP : (e + 1) * 2 * CAP]
-
-
-def hidden_kernel(e_ref, xs_ref, gs_ref, wgu_ref, wd_ref, out_ref):
-    n = wgu_ref.shape[1]
-    a = nt(xs_ref[0], wgu_ref[0])
-    b = nt(gs_ref[0], wd_ref[0])
-
-    @pl.when(pl.program_id(0) == 0)
-    def _():
-        out_ref[:, 0:n] = a
-        out_ref[:, n:] = b
-
-    @pl.when(pl.program_id(0) > 0)
-    def _():
-        out_ref[:, 0:n] += a
-        out_ref[:, n:] += b
-
-
-def act_kernel(h_ref, r_ref, out_ref):
+    for k in range(2):
+        row = info_ref[0] + k
+        pick = chosen(held[pl.ds(row, 1), :])
+        wt = held[pl.ds(32 + row, 1), :] + held[pl.ds(64 + row, 1), :] + held[pl.ds(96 + row, 1), :]
+        picks.append(pick.astype(F32))
+        scales.append(jnp.sum(jnp.where(pick, wt, 0.0), axis=1, keepdims=True))
+    return jnp.concatenate(picks, axis=0).astype(BF), jnp.concatenate(scales, axis=0)
+
+
+def select_x_kernel(info_ref, near_ref, far_ref, *rest):
+    out_ref, held = rest[-2:]
+    w = out_ref.shape[2] // 2
+    pick, _ = picked(info_ref, near_ref[0, :, w:], held)
+    for i, ref in enumerate((near_ref, far_ref)):
+        got = mm(pick, ref[0, :, 0:w]).astype(BF)
+        side = info_ref[1] if i == 0 else 1 - info_ref[1]
+        cols = pl.ds(pl.multiple_of(side * w, w), w)
+        out_ref[0, :, cols] = got[0:CAP]
+        out_ref[1, :, cols] = got[CAP:]
+
+
+def select_g_kernel(info_ref, near_ref, g_ref, *rest):
+    out_ref, held = rest[-2:]
+    pick, scale = picked(info_ref, near_ref[0], held)
+    got = (mm(pick, g_ref[0]) * scale).astype(BF)
+    out_ref[0] = got[0:CAP]
+    out_ref[1] = got[CAP:]
+
+
+def hidden_kernel(e_ref, v_ref, w_ref, out_ref):
+    out_ref[...] = nt(v_ref[0], w_ref[0])
+
+
+def act_kernel(a_ref, b_ref, d_ref, e_ref, out_ref):
     n = out_ref.shape[1] // 3
-    h = h_ref[...] + r_ref[...]
-    gate, up, d = h[:, 0:n], h[:, n : 2 * n], h[:, 2 * n :]
+    h = a_ref[...] + b_ref[...]
+    gate, up = h[:, 0:n], h[:, n:]
+    d = d_ref[...] + e_ref[...]
     sig = jax.nn.sigmoid(gate)
     silu = gate * sig
     out_ref[:, 0:n] = (d * up * sig * (1.0 + gate * (1.0 - sig))).astype(BF)
@@ -184,9 +213,10 @@
 
 def combine_kernel(c_ref, pw_ref, ret_ref, out_ref):
     low = c_ref[0] == 0
+    places = pw_ref[0:32, 1024:1152].astype(F32)
     picks = []
     for e in range(16):
-        a, b = pw_ref[2 * e : 2 * e + 1, 0:128], pw_ref[2 * e + 1 : 2 * e + 2, 0:128]
+        a, b = places[2 * e : 2 * e + 1], places[2 * e + 1 : 2 * e + 2]
         picks.append(chosen(jnp.where(low, a, b)).astype(F32))
         picks.append(chosen(jnp.where(low, b, a)).astype(F32))
     pick = jnp.concatenate(picks, axis=0).T.astype(BF)
@@ -206,14 +236,26 @@
     cs = jnp.reshape(c, (1,)).astype(jnp.int32)
     others = 1 - cs
 
-    at = x * 1024 + c * 512
-    own = jnp.concatenate([lax.dynamic_slice_in_dim(v, at, 512, 1) for v in (tokens, grad_out)], axis=1)
-    gathered = lax.all_gather(own, ZYX, axis=0, tiled=False)
-
-    pw_own = pl.pallas_call(
-        places_kernel, out_shape=like((32, 2 * rows), F32), in_specs=[VMEM, VMEM], out_specs=VMEM, name="places"
-    )(expert_ids, route_weights)
-    pw = lax.all_to_all(pw_own, ZY, split_axis=0, concat_axis=0, tiled=True)
+    z, y = lax.axis_index("z"), lax.axis_index("y")
+    side = x % 2
+
+    piece = lambda k: pl.BlockSpec((rows, 512), lambda i, ar: (0, ar[k]))
+    flat = lambda v: pl.BlockSpec(v.shape, lambda i, ar: (0, 0))
+    ids, wts = expert_ids.T, route_weights.T
+    own = pl.pallas_call(
+        pack_kernel,
+        grid_spec=prefetched(
+            (1,),
+            [flat(ids), flat(wts)] + [piece(k) for k in range(6)],
+            pl.BlockSpec((rows, 3200), lambda i, ar: (0, 0)),
+        ),
+        out_shape=like((rows, 3200)),
+        cost_estimate=cost(1e7, 2e6),
+        name="pack",
+    )(
+        jnp.stack([2 * k + c for k in (2 * side, 2 * side + 1, 0, 1, 2, 3)]).astype(jnp.int32),
+        *(ids, wts, tokens, tokens, grad_out, grad_out, grad_out, grad_out),
+    )
 
     strip = (2, f, 512)
     outgoing = pl.pallas_call(
@@ -227,7 +269,20 @@
         cost_estimate=cost(0, 9.4e6),
         name="outgoing",
     )(cs, w_gate, w_up, w_down)
+
+    up, down = hop(own, first(1)), hop(own, first(-1))
+    up, down, outgoing = together(up, down, outgoing)
+    far = jnp.concatenate([hop(up[:64], first(1)), hop(down[64:], first(-1))], axis=0)
     incoming = swap(outgoing)
+    line = [own, up, down, far]
+    xg = jnp.stack([v[:, :1152] for v in line])
+    gg = jnp.stack([v[:, 1152:] for v in line])
+    xm, xr, xg_far = hop(xg, second(1)), hop(xg, second(-1)), hop(xg, along)
+    gg, xm, xr, xg_far, incoming = together(gg, xm, xr, xg_far, incoming)
+    gm, gr = hop(gg, second(1)), hop(gg, second(-1))
+    xd0, xd1 = hop(xm[:2], second(1)), hop(xr[2:], second(-1))
+    xm_far = hop(xm, along)
+
     wgu, wd = pl.pallas_call(
         assemble_kernel,
         grid_spec=prefetched(
@@ -240,55 +295,96 @@
             ],
         ),
         out_shape=(like((2, 4 * f, half)), like((2, 2 * f, half))),
-        compiler_params=params(32),
+        compiler_params=params(24),
         cost_estimate=cost(0, 19e6),
         name="assemble",
     )(cs, w_gate, w_up, w_down, incoming)
 
-    xs, gs = pl.pallas_call(
-        select_kernel,
-        grid=(8,),
-        out_shape=(like((2, slots, half)), like((2, slots, half))),
-        in_specs=[VMEM, pl.BlockSpec((8, rows, 1024), lambda b: (b, 0, 0))],
-        out_specs=(
-            pl.BlockSpec((2, 2 * CAP, half), lambda b: (0, b, 0)),
-            pl.BlockSpec((2, 2 * CAP, half), lambda b: (0, b, 0)),
-        ),
-        compiler_params=params(32),
-        cost_estimate=cost(3.2e9, 30e6),
-        name="select",
-    )(pw, gathered)
-
-    def hidden(which):
+    offsets = (0, -1, 1, 2)
+    table = []
+    for b in offsets:
+        for a in offsets:
+            oz, oy = jnp.where(c == 0, a, b), jnp.where(c == 0, b, a)
+            table.append((z + oz + 4) % 4 * 4 + (y + oy + 4) % 4)
+    info = jnp.stack([2 * (z * 4 + y), side] + table).astype(jnp.int32)
+
+    def select(kernel, start, near, other, into):
+        is_x = kernel is select_x_kernel
+        if is_x:
+            specs = [pl.BlockSpec((1, rows, 1152), lambda i, fo: (i, 0, 0))] * 2
+        else:
+            specs = [
+                pl.BlockSpec((1, rows, 128), lambda i, fo: (i, 0, 8)),
+                pl.BlockSpec((1, rows, half), lambda i, fo: (i, 0, 0)),
+            ]
+        n = near.shape[0]
+        return pl.pallas_call(
+            kernel,
+            grid_spec=prefetched(
+                (n,),
+                specs + [pl.BlockSpec(memory_space=pl.ANY)] * len(into),
+                pl.BlockSpec((2, CAP, half), lambda i, fo: (0, fo[2 + start + i], 0)),
+                [pltpu.VMEM((rows, rows), F32)],
+            ),
+            out_shape=like((2, slots, half)),
+            input_output_aliases={3: 0} if into else {},
+            compiler_params=params(24),
+            cost_estimate=cost(2 * n * 2 * CAP * rows * half, n * 1.4e6),
+            name="select",
+        )(info, near, other, *into)
+
+    xs = select(select_x_kernel, 0, xg, xg_far, [])
+    gs = select(select_g_kernel, 0, xg, gg, [])
+    xm_far, xr_go, xs, gs, wgu, wd = together(xm_far, xr, xs, gs, wgu, wd)
+    xr_far = hop(xr_go, along)
+    gm, gr, xd0, xd1, xr_far = together(gm, gr, xd0, xd1, xr_far)
+    gd0, gd1 = hop(gm[:2], second(1)), hop(gr[2:], second(-1))
+    xd0_far = hop(xd0, along)
+    xs = select(select_x_kernel, 4, xm, xm_far, [xs])
+    gs = select(select_g_kernel, 4, xm, gm, [gs])
+    xd0_far, xd1, xs, gs = together(xd0_far, xd1, xs, gs)
+    xd1_far = hop(xd1, along)
+    xs = select(select_x_kernel, 8, xr, xr_far, [xs])
+    xs = select(select_x_kernel, 12, xd0, xd0_far, [xs])
+    gs = select(select_g_kernel, 8, xr, gr, [gs])
+    xs = select(select_x_kernel, 14, xd1, xd1_far, [xs])
+    gd0, gd1, xs, gs = together(gd0, gd1, xs, gs)
+    gs = select(select_g_kernel, 12, xd0, gd0, [gs])
+    gs = select(select_g_kernel, 14, xd1, gd1, [gs])
+
+    def hidden(which, v, w, chunk):
+        n = w.shape[1]
         return pl.pallas_call(
             hidden_kernel,
             grid_spec=prefetched(
-                (4,),
+                (n // chunk,),
                 [
-                    pl.BlockSpec((1, slots, 512), lambda j, er: (er[0], 0, j)),
-                    pl.BlockSpec((1, slots, 512), lambda j, er: (er[0], 0, j)),
-                    pl.BlockSpec((1, 4 * f, 512), lambda j, er: (er[0], 0, j)),
-                    pl.BlockSpec((1, 2 * f, 512), lambda j, er: (er[0], 0, j)),
+                    pl.BlockSpec((1, slots, half), lambda j, er: (er[0], 0, 0)),
+                    pl.BlockSpec((1, chunk, half), lambda j, er: (er[0], j, 0)),
                 ],
-                pl.BlockSpec((slots, 6 * f), lambda j, er: (0, 0)),
+                pl.BlockSpec((slots, chunk), lambda j, er: (0, j)),
             ),
-            out_shape=like((slots, 6 * f), F32),
-            compiler_params=params(40),
-            cost_estimate=cost(2 * slots * half * 6 * f, 15e6),
+            out_shape=like((slots, n), F32),
+            compiler_params=params(24),
+            cost_estimate=cost(2 * slots * half * n, 9e6),
             name="hidden",
-        )(which, xs, gs, wgu, wd)
-
-    received = swap(hidden(others))
+        )(which, v, w)
+
+    pre_in = swap(hidden(others, xs, wgu, 256))
+    pre = hidden(cs, xs, wgu, 256)
+    dh_in = swap(hidden(others, gs, wd, 128))
+    dh = hidden(cs, gs, wd, 128)
+    quarter = lambda n: pl.BlockSpec((slots // 4, n), lambda j: (j, 0))
     mine = pl.pallas_call(
         act_kernel,
         grid=(4,),
         out_shape=like((slots, 6 * f)),
-        in_specs=[pl.BlockSpec((slots // 4, 6 * f), lambda j: (j, 0))] * 2,
-        out_specs=pl.BlockSpec((slots // 4, 6 * f), lambda j: (j, 0)),
-        compiler_params=params(32),
+        in_specs=[quarter(4 * f), quarter(4 * f), quarter(2 * f), quarter(2 * f)],
+        out_specs=quarter(6 * f),
+        compiler_params=params(24),
         cost_estimate=cost(1e7, 9e6),
         name="act",
-    )(hidden(cs), received)
+    )(pre, pre_in, dh, dh_in)
     theirs = swap(mine)
 
     def partial(which, place, ad, into):
@@ -303,7 +399,7 @@
             ),
             out_shape=out,
             input_output_aliases={3: 0} if into else {},
-            compiler_params=params(32),
+            compiler_params=params(24),
             cost_estimate=cost(2 * slots * half * 4 * f, 8e6),
             name="partial",
         )(which, ad, wgu, *into)
@@ -327,7 +423,7 @@
             [pltpu.VMEM((6 * f, slots), BF)],
         ),
         out_shape=[like((2, f, width))] * 3 + [like((2, 3, f, half))],
-        compiler_params=params(40),
+        compiler_params=params(24),
         cost_estimate=cost(4 * slots * half * 6 * f, 24e6),
         name="weights",
     )(cs, mine, theirs, xs, gs)
@@ -350,10 +446,10 @@
         out_shape=like((rows, 512)),
         in_specs=[SMEM, VMEM, VMEM],
         out_specs=VMEM,
-        compiler_params=params(40),
+        compiler_params=params(24),
         cost_estimate=cost(1e9, 6.5e6),
         name="combine",
-    )(cs, pw_own, returned.reshape(16, 4, 2 * CAP, 512))
+    )(cs, own, returned.reshape(16, 4, 2 * CAP, 512))
     return (grad_tokens, *grads)
 
 

time: 277 us -> 244 us (0.88); the launches traced: 272 us -> 243 us
  waiting for transfers between devices: 140 us -> 111 us
  starting transfers between devices: 17.5 us -> 33.3 us
  between operations: 14.2 us -> 1.16 us
    all_gather x1 -> x0, waiting for transfers between devices: 72.1 us -> none  [shards(): gathered = lax.all_gather(own, ZYX, axis=0, tiled=False)]
    ppermute x0 -> x17, waiting for transfers between devices: none -> 48.2 us  [hop(): return lax.ppermute(v, ('z', 'y', 'x', 'c'), to)]
    ppermute x0 -> x17, starting transfers between devices: none -> 24.3 us  [hop(): return lax.ppermute(v, ('z', 'y', 'x', 'c'), to)]
    all_to_all x1 -> x0, starting transfers between devices: 8.13 us -> none  [shards(): pw = lax.all_to_all(pw_own, ZY, split_axis=0, concat_axis=0, tiled=True)]
    all_to_all x1 -> x0, waiting for transfers between devices: 7.6 us -> none  [shards(): pw = lax.all_to_all(pw_own, ZY, split_axis=0, concat_axis=0, tiled=True)]
    pallas_call x4 -> x15, Pallas kernels: 31.5 us -> 36.4 us  [the longest x10 21 us: select(): pl.pallas_call(kernel, grid_spec=prefetched((n,), specs + [pl.BlockSpec(m...]
    slice x0 -> x6, local copies, waits for them, and re-layouts: none -> 3.86 us  [the longest x2 2.64 us: shards(): gd0, gd1 = (hop(gm[:2], second(1)), hop(gr[2:], second(-1)))]
    pallas_call x1, Pallas kernels: 5.79 us -> 2.26 us  [shards(): pl.pallas_call(assemble_kernel, grid_spec=prefetched((4,), [pl.BlockSpec(...]
  transfers between devices with their start and end apart: 7 -> 23, of which waited for: 4 -> 13; matrix products, arithmetic and copies ran while one was open for 1% -> 2% of each run, Pallas kernels for 16% -> 24%
where the time goes in v3:
time: 244 us; the launch traced here: 243 us
  waiting for transfers between devices  111 us (45%)
  Pallas kernels  73.4 us (30%)
  starting transfers between devices  33.3 us (14%)
  local copies, waits for them, and re-layouts  23.5 us (10%)
    all_to_all x1, waiting for transfers between devices, shards(): lax.all_to_all(sent.reshape(64, 2, CAP, 512), ZYX, split_axis=0, concat_a...  55.1 us
    ppermute x17, waiting for transfers between devices, hop(): return lax.ppermute(v, ('z', 'y', 'x', 'c'), to)  48.2 us
    ppermute x17, starting transfers between devices, hop(): return lax.ppermute(v, ('z', 'y', 'x', 'c'), to)  24.3 us
    pallas_call x10, Pallas kernels, select(): pl.pallas_call(kernel, grid_spec=prefetched((n,), specs + [pl.BlockSpec(m...  21 us
    unnamed x49, local copies, waits for them, and re-layouts  18.5 us
    pallas_call x4, Pallas kernels, hidden(): pl.pallas_call(hidden_kernel, grid_spec=prefetched((n // chunk,), [pl.Blo...  12.5 us
    pallas_call x1, Pallas kernels, shards(): pl.pallas_call(weight_kernel, grid_spec=prefetched((2, 4), [VMEM, VMEM, p...  12.2 us
    all_to_all x1, starting transfers between devices, shards(): lax.all_to_all(sent.reshape(64, 2, CAP, 512), ZYX, split_axis=0, concat_a...  8.08 us
  transfers between devices with their start and end apart: 23, of which 13 were waited for; matrix products, arithmetic and copies ran while one was open for 2% of the time, Pallas kernels for 24%

profile of v3, /device:TPU:0, one launch (start us, length us, event | category | flops | bytes accessed | tf_op | source)
XLA Modules:
  0.0 243.0 jit_solution(15983565676503917004)
XLA Ops:
  1.3 2.9 %pack.1.pw_ref = bf16[128,3200]{1,0:T(8,128)(2,1)} custom-call(s32[6]{0:T(128)} %stack.111.at_ref, s32[8,128]{1,0:T(8,128)} %bitcast.47, f32[8,128]{1,0:T(8,128)} %bitcast.48, bf16[128,4096]{1,0:T(8,128)(2,1)} %t1.1, bf16[128,4096]{1,0:T(8,128)(2,1)} %t1.1, bf16[128,4096]{1,0:T(8,128)(2,1)} %g3.1, bf16[128,4096]{1,0:T(8,128)(2,1)} %g3.1, ...), custom_call_target="tpu_custom_call" | custom-call | flops 10000 | bytes 2000 | tf_op jit(solution)/shard_map/pack/pallas_call | solution.py:245
  8.4 5.0 %outgoing.1 = bf16[6,192,2048]{2,1,0:T(8,128)(2,1)} custom-call(s32[1]{0:T(128)} %bitcast.c_ref.e_ref, bf16[2,192,4096]{2,1,0:T(8,128)(2,1)} %g_ref.3, bf16[2,192,4096]{2,1,0:T(8,128)(2,1)} %u_ref.3, bf16[2,192,4096]{2,1,0:T(8,128)(2,1)} %d_ref.3), custom_call_target="tpu_custom_call" | custom-call | bytes 9400 | tf_op jit(solution)/shard_map/outgoing/pallas_call | solution.py:261
  13.5 5.5 %collective-permute-done = bf16[128,3200]{1,0:T(8,128)(2,1)S(1)} collective-permute-done((bf16[128,3200]{1,0:T(8,128)(2,1)}, bf16[128,3200]{1,0:T(8,128)(2,1)S(1)}, u32[]{:S(2)}, u32[]{:S(2)}) %collective-permute-start) | collective-permute-done | bytes 819232 | tf_op jit(solution)/shard_map/ppermute | solution.py:57
  22.6 5.8 %collective-permute-done.2 = bf16[64,3200]{1,0:T(8,128)(2,1)S(1)} collective-permute-done((bf16[64,3200]{1,0:T(8,128)(2,1)S(1)}, bf16[64,3200]{1,0:T(8,128)(2,1)S(1)}, u32[]{:S(2)}, u32[]{:S(2)}) %collective-permute-start.2) | collective-permute-done | bytes 409632 | tf_op jit(solution)/shard_map/ppermute | solution.py:57
  34.5 12.3 %collective-permute-done.4.near_ref = bf16[4,128,1152]{2,1,0:T(8,128)(2,1)} collective-permute-done((bf16[4,128,1152]{2,1,0:T(8,128)(2,1)S(1)}, bf16[4,128,1152]{2,1,0:T(8,128)(2,1)}, u32[]{:S(2)}, u32[]{:S(2)}) %collective-permute-start.4) | collective-permute-done | bytes 1179680 | tf_op jit(solution)/shard_map/ppermute | solution.py:57
  53.8 2.9 %collective-permute-start.9 = (bf16[4,128,2048]{2,1,0:T(8,128)(2,1)S(1)}, bf16[4,128,2048]{2,1,0:T(8,128)(2,1)}, u32[]{:S(2)}, u32[]{:S(2)}) collective-permute-start(bf16[4,128,2048]{2,1,0:T(8,128)(2,1)S(1)} %pad_maximum_fusion.g_ref), channel_id=1, source_target_pairs={{0,24},{1,97},{2,26},{3,99},{4,28},{5,101},{6,30},{7,103},{8,0},{9... | collective-permute-start | bytes 6291464 | tf_op jit(solution)/shard_map/ppermute | solution.py:57
  66.1 4.7 %collective-permute-done.12.far_ref = bf16[4,128,1152]{2,1,0:T(8,128)(2,1)} collective-permute-done((bf16[4,128,1152]{2,1,0:T(8,128)(2,1)}, bf16[4,128,1152]{2,1,0:T(8,128)(2,1)}, u32[]{:S(2)}, u32[]{:S(2)}) %collective-permute-start.12) | collective-permute-done | bytes 1179680 | tf_op jit(solution)/shard_map/ppermute | solution.py:57
  75.4 11.6 %collective-permute-done.10.near_ref = bf16[2,128,1152]{2,1,0:T(8,128)(2,1)S(1)} collective-permute-done((bf16[2,128,1152]{2,1,0:T(8,128)(2,1)S(1)}, bf16[2,128,1152]{2,1,0:T(8,128)(2,1)S(1)}, u32[]{:S(2)}, u32[]{:S(2)}) %collective-permute-start.10) | collective-permute-done | bytes 589856 | tf_op jit(solution)/shard_map/ppermute | solution.py:57
  94.6 3.6 %select.78.rest_0_ = bf16[2,768,2048]{2,1,0:T(8,128)(2,1)S(1)} custom-call(s32[18]{0:T(128)S(1)} %stack.140.info_ref, bf16[4,128,1152]{2,1,0:T(8,128)(2,1)} %collective-permute-done.4.near_ref, bf16[4,128,1152]{2,1,0:T(8,128)(2,1)} %collective-permute-done.12.far_ref, bf16[2,768,2048]{2,1,0:T(8,128)(2,1)S(1)} %select.76.rest_0_), custom_call_target="tpu_custom_call", output_to_operand_aliasing={{}: (3, {})} | custom-call | flops 201326 | bytes 5600 | tf_op jit(solution)/shard_map/select/pallas_call | solution.py:321
  98.2 3.6 %select.79.rest_0_ = bf16[2,768,2048]{2,1,0:T(8,128)(2,1)S(1)} custom-call(s32[18]{0:T(128)S(1)} %stack.140.info_ref, bf16[4,128,1152]{2,1,0:T(8,128)(2,1)} %collective-permute-done.4.near_ref, bf16[4,128,2048]{2,1,0:T(8,128)(2,1)} %collective-permute-done.8.g_ref, bf16[2,768,2048]{2,1,0:T(8,128)(2,1)S(1)} %select.77.rest_0_), custom_call_target="tpu_custom_call", output_to_operand_aliasing={{}: (3, {})} | custom-call | flops 201326 | bytes 5600 | tf_op jit(solution)/shard_map/select/pallas_call | solution.py:321
  106.3 3.7 %select.83.rest_0_ = bf16[2,768,2048]{2,1,0:T(8,128)(2,1)S(1)} custom-call(s32[18]{0:T(128)S(1)} %stack.140.info_ref, bf16[4,128,1152]{2,1,0:T(8,128)(2,1)S(1)} %copy-done.10, bf16[4,128,2048]{2,1,0:T(8,128)(2,1)} %collective-permute-done.9.g_ref, bf16[2,768,2048]{2,1,0:T(8,128)(2,1)S(1)} %select.79.rest_0_), custom_call_target="tpu_custom_call", output_to_operand_aliasing={{}: (3, {})} | custom-call | flops 201326 | bytes 5600 | tf_op jit(solution)/shard_map/select/pallas_call | solution.py:321
  110.0 3.2 %collective-permute-done.17.far_ref = bf16[2,128,1152]{2,1,0:T(8,128)(2,1)S(1)} collective-permute-done((bf16[2,128,1152]{2,1,0:T(8,128)(2,1)S(1)}, bf16[2,128,1152]{2,1,0:T(8,128)(2,1)S(1)}, u32[]{:S(2)}, u32[]{:S(2)}) %collective-permute-start.17) | collective-permute-done | bytes 589856 | tf_op jit(solution)/shard_map/ppermute | solution.py:57
  114.4 3.2 %hidden.5 = f32[768,768]{1,0:T(8,128)S(1)} custom-call(s32[1]{0:T(128)S(6)} %sub.3.e_ref, bf16[2,768,2048]{2,1,0:T(8,128)(2,1)S(1)} %select.82.v_ref.xs_ref, bf16[2,768,2048]{2,1,0:T(8,128)(2,1)S(1)} %bitcast.45), custom_call_target="tpu_custom_call" | custom-call | flops 2415919 | bytes 9000 | tf_op jit(solution)/shard_map/hidden/pallas_call | solution.py:357
  120.2 3.0 %hidden.7 = f32[768,384]{1,0:T(8,128)S(1)} custom-call(s32[1]{0:T(128)S(6)} %sub.3.e_ref, bf16[2,768,2048]{2,1,0:T(8,128)(2,1)S(1)} %select.85.v_ref.gs_ref, bf16[2,384,2048]{2,1,0:T(8,128)(2,1)S(1)} %get-tuple-element.68.w_ref), custom_call_target="tpu_custom_call" | custom-call | flops 1207959 | bytes 9000 | tf_op jit(solution)/shard_map/hidden/pallas_call | solution.py:357
  123.8 3.0 %hidden.6.d_ref = f32[768,384]{1,0:T(8,128)S(1)} custom-call(s32[1]{0:T(128)} %bitcast.c_ref.e_ref, bf16[2,768,2048]{2,1,0:T(8,128)(2,1)S(1)} %select.85.v_ref.gs_ref, bf16[2,384,2048]{2,1,0:T(8,128)(2,1)S(1)} %get-tuple-element.68.w_ref), custom_call_target="tpu_custom_call" | custom-call | flops 1207959 | bytes 9000 | tf_op jit(solution)/shard_map/hidden/pallas_call | solution.py:357
  126.8 3.2 %hidden.4.a_ref = f32[768,768]{1,0:T(8,128)S(1)} custom-call(s32[1]{0:T(128)} %bitcast.c_ref.e_ref, bf16[2,768,2048]{2,1,0:T(8,128)(2,1)S(1)} %select.82.v_ref.xs_ref, bf16[2,768,2048]{2,1,0:T(8,128)(2,1)S(1)} %bitcast.45), custom_call_target="tpu_custom_call" | custom-call | flops 2415919 | bytes 9000 | tf_op jit(solution)/shard_map/hidden/pallas_call | solution.py:357
  131.0 3.6 %partial.2.rest_0_ = bf16[16,4,2,48,512]{4,3,2,1,0:T(8,128)(2,1)S(1)} custom-call(s32[1]{0:T(128)} %bitcast.c_ref.e_ref, bf16[768,1152]{1,0:T(8,128)(2,1)S(1)} %act.1.ad_ref.mine_ref, bf16[2,768,2048]{2,1,0:T(8,128)(2,1)S(1)} %bitcast.45), custom_call_target="tpu_custom_call" | custom-call | flops 2415919 | bytes 8000 | tf_op jit(solution)/shard_map/partial/pallas_call | solution.py:393
  134.7 3.6 %partial.3 = bf16[16,4,2,48,512]{4,3,2,1,0:T(8,128)(2,1)S(1)} custom-call(s32[1]{0:T(128)S(6)} %sub.3.e_ref, bf16[768,1152]{1,0:T(8,128)(2,1)S(1)} %collective-permute-done.20.ad_ref.theirs_ref, bf16[2,768,2048]{2,1,0:T(8,128)(2,1)S(1)} %bitcast.45, bf16[16,4,2,48,512]{4,3,2,1,0:T(8,128)(2,1)S(1)} %partial.2.rest_0_), custom_call_target="tpu_custom_call", output_to_operand_aliasing={{}: (3, {})} | custom-call | flops 2415919 | bytes 8000 | tf_op jit(solution)/shard_map/partial/pallas_call | solution.py:393
  140.9 8.1 %all-to-all-start = ((bf16[64,2,48,512]{3,2,1,0:T(8,128)(2,1)}), bf16[64,2,48,512]{3,2,1,0:T(8,128)(2,1)}, u32[]{:S(2)}, u32[]{:S(2)}) async-start(bf16[64,2,48,512]{3,2,1,0:T(8,128)(2,1)} %bitcast.46), calls=%async_computation | async-start | bytes 12582912 | tf_op jit(solution)/shard_map/all_to_all | solution.py:408
  156.1 12.2 %weights.1 = (bf16[2,192,4096]{2,1,0:T(8,128)(2,1)}, bf16[2,192,4096]{2,1,0:T(8,128)(2,1)}, bf16[2,192,4096]{2,1,0:T(8,128)(2,1)}, bf16[2,3,192,2048]{3,2,1,0:T(8,128)(2,1)S(1)}) custom-call(s32[1]{0:T(128)} %bitcast.c_ref.e_ref, bf16[768,1152]{1,0:T(8,128)(2,1)S(1)} %act.1.ad_ref.mine_ref, bf16[768,1152]{1,0:T(8,128)(2,1)S(1)} %copy-done.14, ...), custom_call_target="tpu_custom_call" | custom-call | flops 7247757 | bytes 24000 | tf_op jit(solution)/shard_map/weights/pallas_call | solution.py:411
  168.4 7.8 %collective-permute-done.21.in_ref = bf16[2,3,192,2048]{3,2,1,0:T(8,128)(2,1)S(1)} collective-permute-done((bf16[2,3,192,2048]{3,2,1,0:T(8,128)(2,1)S(1)}, bf16[2,3,192,2048]{3,2,1,0:T(8,128)(2,1)S(1)}, u32[]{:S(2)}, u32[]{:S(2)}) %collective-permute-start.21) | collective-permute-done | bytes 4718624 | tf_op jit(solution)/shard_map/ppermute | solution.py:36
  178.3 5.1 %settle.1 = (bf16[2,192,4096]{2,1,0:T(8,128)(2,1)}, bf16[2,192,4096]{2,1,0:T(8,128)(2,1)}, bf16[2,192,4096]{2,1,0:T(8,128)(2,1)}) custom-call(s32[1]{0:T(128)} %bitcast.c_ref.e_ref, bf16[2,3,192,2048]{3,2,1,0:T(8,128)(2,1)} %copy-done.19, bf16[2,192,4096]{2,1,0:T(8,128)(2,1)} %get-tuple-element.70.a_ref, ...), custom_call_target="tpu_custom_call", output_to_operand_aliasing={{0}: (2, {}), {1}: (3, {}), {2}: (4, {})} | custom-call | bytes 9400 | tf_op jit(solution)/shard_map/settle/pallas_call | solution.py:431
  183.4 55.1 %all-to-all-done = bf16[64,2,48,512]{3,2,1,0:T(8,128)(2,1)} async-done(((bf16[64,2,48,512]{3,2,1,0:T(8,128)(2,1)}), bf16[64,2,48,512]{3,2,1,0:T(8,128)(2,1)}, u32[]{:S(2)}, u32[]{:S(2)}) %all-to-all-start) | async-done | bytes 6291488 | tf_op jit(solution)/shard_map/all_to_all | solution.py:408
  238.5 4.5 %combine.1 = bf16[128,512]{1,0:T(8,128)(2,1)} custom-call(s32[1]{0:T(128)} %bitcast.c_ref.e_ref, bf16[128,3200]{1,0:T(8,128)(2,1)S(1)} %copy-done.12, bf16[16,4,96,512]{3,2,1,0:T(8,128)(2,1)} %bitcast.35.ret_ref), custom_call_target="tpu_custom_call" | custom-call | flops 1000000 | bytes 6500 | tf_op jit(solution)/shard_map/combine/pallas_call | solution.py:444
  (112 shorter events, 64.5 us)
Async XLA Ops:
  4.3 14.7 %collective-permute-start = (bf16[128,3200]{1,0:T(8,128)(2,1)}, bf16[128,3200]{1,0:T(8,128)(2,1)S(1)}, u32[]{:S(2)}, u32[]{:S(2)}) collective-permute-start(bf16[128,3200]{1,0:T(8,128)(2,1)} %pack.1.pw_ref), channel_id=1, source_target_pairs={{0,32},{1,9},{2,34},{3,11},{4,36},{5,13},{6,38},{7,15},{8,40},{9,1... | collective-permute-start | bytes 2457608 | tf_op jit(solution)/shard_map/ppermute | solution.py:57
  6.3 12.7 %collective-permute-start.1 = (bf16[128,3200]{1,0:T(8,128)(2,1)}, bf16[128,3200]{1,0:T(8,128)(2,1)S(1)}, u32[]{:S(2)}, u32[]{:S(2)}) collective-permute-start(bf16[128,3200]{1,0:T(8,128)(2,1)} %pack.1.pw_ref), channel_id=1, source_target_pairs={{0,96},{1,25},{2,98},{3,27},{4,100},{5,29},{6,102},{7,31},{8,104},... | collective-permute-start | bytes 2457608 | tf_op jit(solution)/shard_map/ppermute | solution.py:57
  19.0 32.0 %collective-permute-start.7 = (bf16[6,192,2048]{2,1,0:T(8,128)(2,1)}, bf16[6,192,2048]{2,1,0:T(8,128)(2,1)S(1)}, u32[]{:S(2)}, u32[]{:S(2)}) collective-permute-start(bf16[6,192,2048]{2,1,0:T(8,128)(2,1)} %outgoing.1), channel_id=1, source_target_pairs={{0,1},{1,0},{2,3},{3,2},{4,5},{5,4},{6,7},{7,6},{8,9},{9,8},{10,11... | collective-permute-start | bytes 14155784 | tf_op jit(solution)/shard_map/ppermute | solution.py:36
  19.1 9.2 %collective-permute-start.2 = (bf16[64,3200]{1,0:T(8,128)(2,1)S(1)}, bf16[64,3200]{1,0:T(8,128)(2,1)S(1)}, u32[]{:S(2)}, u32[]{:S(2)}) collective-permute-start(bf16[64,3200]{1,0:T(8,128)(2,1)S(1)} %slice.45), channel_id=1, source_target_pairs={{0,32},{1,9},{2,34},{3,11},{4,36},{5,13},{6,38},{7,15},{8,40},{9,1... | collective-permute-start | bytes 1228808 | tf_op jit(solution)/shard_map/ppermute | solution.py:57
  21.0 8.0 %collective-permute-start.3 = (bf16[64,3200]{1,0:T(8,128)(2,1)S(1)}, bf16[64,3200]{1,0:T(8,128)(2,1)S(1)}, u32[]{:S(2)}, u32[]{:S(2)}) collective-permute-start(bf16[64,3200]{1,0:T(8,128)(2,1)S(1)} %slice.46), channel_id=1, source_target_pairs={{0,96},{1,25},{2,98},{3,27},{4,100},{5,29},{6,102},{7,31},{8,104},... | collective-permute-start | bytes 1228808 | tf_op jit(solution)/shard_map/ppermute | solution.py:57
  29.2 17.6 %collective-permute-start.4 = (bf16[4,128,1152]{2,1,0:T(8,128)(2,1)S(1)}, bf16[4,128,1152]{2,1,0:T(8,128)(2,1)}, u32[]{:S(2)}, u32[]{:S(2)}) collective-permute-start(bf16[4,128,1152]{2,1,0:T(8,128)(2,1)S(1)} %pad_maximum_fusion.1.near_ref), channel_id=1, source_target_pairs={{0,8},{1,33},{2,10},{3,35},{4,12},{5,37},{6,14},{7,39},{8,16},{9,4... | collective-permute-start | bytes 3538952 | tf_op jit(solution)/shard_map/ppermute | solution.py:57
  30.9 16.2 %collective-permute-start.5 = (bf16[4,128,1152]{2,1,0:T(8,128)(2,1)S(1)}, bf16[4,128,1152]{2,1,0:T(8,128)(2,1)S(1)}, u32[]{:S(2)}, u32[]{:S(2)}) collective-permute-start(bf16[4,128,1152]{2,1,0:T(8,128)(2,1)S(1)} %pad_maximum_fusion.1.near_ref), channel_id=1, source_target_pairs={{0,24},{1,97},{2,26},{3,99},{4,28},{5,101},{6,30},{7,103},{8,0},{9... | collective-permute-start | bytes 3538952 | tf_op jit(solution)/shard_map/ppermute | solution.py:57
  32.5 17.4 %collective-permute-start.6 = (bf16[4,128,1152]{2,1,0:T(8,128)(2,1)S(1)}, bf16[4,128,1152]{2,1,0:T(8,128)(2,1)S(1)}, u32[]{:S(2)}, u32[]{:S(2)}) collective-permute-start(bf16[4,128,1152]{2,1,0:T(8,128)(2,1)S(1)} %pad_maximum_fusion.1.near_ref), channel_id=1, source_target_pairs={{0,2},{1,7},{2,4},{3,1},{4,6},{5,3},{6,0},{7,5},{8,10},{9,15},{10,... | collective-permute-start | bytes 3538952 | tf_op jit(solution)/shard_map/ppermute | solution.py:57
  53.2 17.7 %collective-permute-start.12 = (bf16[4,128,1152]{2,1,0:T(8,128)(2,1)}, bf16[4,128,1152]{2,1,0:T(8,128)(2,1)}, u32[]{:S(2)}, u32[]{:S(2)}) collective-permute-start(bf16[4,128,1152]{2,1,0:T(8,128)(2,1)} %collective-permute-done.4.near_ref), channel_id=1, source_target_pairs={{0,2},{1,7},{2,4},{3,1},{4,6},{5,3},{6,0},{7,5},{8,10},{9,15},{10,... | collective-permute-start | bytes 3538952 | tf_op jit(solution)/shard_map/ppermute | solution.py:57
  53.4 33.6 %collective-permute-start.8 = (bf16[4,128,2048]{2,1,0:T(8,128)(2,1)S(1)}, bf16[4,128,2048]{2,1,0:T(8,128)(2,1)}, u32[]{:S(2)}, u32[]{:S(2)}) collective-permute-start(bf16[4,128,2048]{2,1,0:T(8,128)(2,1)S(1)} %pad_maximum_fusion.g_ref), channel_id=1, source_target_pairs={{0,8},{1,33},{2,10},{3,35},{4,12},{5,37},{6,14},{7,39},{8,16},{9,4... | collective-permute-start | bytes 6291464 | tf_op jit(solution)/shard_map/ppermute | solution.py:57
  53.8 33.2 %collective-permute-start.9 = (bf16[4,128,2048]{2,1,0:T(8,128)(2,1)S(1)}, bf16[4,128,2048]{2,1,0:T(8,128)(2,1)}, u32[]{:S(2)}, u32[]{:S(2)}) collective-permute-start(bf16[4,128,2048]{2,1,0:T(8,128)(2,1)S(1)} %pad_maximum_fusion.g_ref), channel_id=1, source_target_pairs={{0,24},{1,97},{2,26},{3,99},{4,28},{5,101},{6,30},{7,103},{8,0},{9... | collective-permute-start | bytes 6291464 | tf_op jit(solution)/shard_map/ppermute | solution.py:57
  70.9 17.4 %collective-permute-start.13 = (bf16[4,128,1152]{2,1,0:T(8,128)(2,1)S(1)}, bf16[4,128,1152]{2,1,0:T(8,128)(2,1)S(1)}, u32[]{:S(2)}, u32[]{:S(2)}) collective-permute-start(bf16[4,128,1152]{2,1,0:T(8,128)(2,1)S(1)} %copy-done.10), channel_id=1, source_target_pairs={{0,2},{1,7},{2,4},{3,1},{4,6},{5,3},{6,0},{7,5},{8,10},{9,15},{10,... | collective-permute-start | bytes 3538952 | tf_op jit(solution)/shard_map/ppermute | solution.py:57
  72.1 14.9 %collective-permute-start.10 = (bf16[2,128,1152]{2,1,0:T(8,128)(2,1)S(1)}, bf16[2,128,1152]{2,1,0:T(8,128)(2,1)S(1)}, u32[]{:S(2)}, u32[]{:S(2)}) collective-permute-start(bf16[2,128,1152]{2,1,0:T(8,128)(2,1)S(1)} %slice.52), channel_id=1, source_target_pairs={{0,8},{1,33},{2,10},{3,35},{4,12},{5,37},{6,14},{7,39},{8,16},{9,4... | collective-permute-start | bytes 1769480 | tf_op jit(solution)/shard_map/ppermute | solution.py:57
  72.5 14.5 %collective-permute-start.11 = (bf16[2,128,1152]{2,1,0:T(8,128)(2,1)S(1)}, bf16[2,128,1152]{2,1,0:T(8,128)(2,1)S(1)}, u32[]{:S(2)}, u32[]{:S(2)}) collective-permute-start(bf16[2,128,1152]{2,1,0:T(8,128)(2,1)S(1)} %slice.53), channel_id=1, source_target_pairs={{0,24},{1,97},{2,26},{3,99},{4,28},{5,101},{6,30},{7,103},{8,0},{9... | collective-permute-start | bytes 1769480 | tf_op jit(solution)/shard_map/ppermute | solution.py:57
  88.3 13.6 %collective-permute-start.16 = (bf16[2,128,1152]{2,1,0:T(8,128)(2,1)S(1)}, bf16[2,128,1152]{2,1,0:T(8,128)(2,1)S(1)}, u32[]{:S(2)}, u32[]{:S(2)}) collective-permute-start(bf16[2,128,1152]{2,1,0:T(8,128)(2,1)S(1)} %collective-permute-done.10.near_ref), channel_id=1, source_target_pairs={{0,2},{1,7},{2,4},{3,1},{4,6},{5,3},{6,0},{7,5},{8,10},{9,15},{10,... | collective-permute-start | bytes 1769480 | tf_op jit(solution)/shard_map/ppermute | solution.py:57
  89.9 24.5 %collective-permute-start.14 = (bf16[2,128,2048]{2,1,0:T(8,128)(2,1)S(1)}, bf16[2,128,2048]{2,1,0:T(8,128)(2,1)S(1)}, u32[]{:S(2)}, u32[]{:S(2)}) collective-permute-start(bf16[2,128,2048]{2,1,0:T(8,128)(2,1)S(1)} %slice.54), channel_id=1, source_target_pairs={{0,8},{1,33},{2,10},{3,35},{4,12},{5,37},{6,14},{7,39},{8,16},{9,4... | collective-permute-start | bytes 3145736 | tf_op jit(solution)/shard_map/ppermute | solution.py:57
  92.0 22.4 %collective-permute-start.15 = (bf16[2,128,2048]{2,1,0:T(8,128)(2,1)S(1)}, bf16[2,128,2048]{2,1,0:T(8,128)(2,1)S(1)}, u32[]{:S(2)}, u32[]{:S(2)}) collective-permute-start(bf16[2,128,2048]{2,1,0:T(8,128)(2,1)S(1)} %slice.55), channel_id=1, source_target_pairs={{0,24},{1,97},{2,26},{3,99},{4,28},{5,101},{6,30},{7,103},{8,0},{9... | collective-permute-start | bytes 3145736 | tf_op jit(solution)/shard_map/ppermute | solution.py:57
  101.9 11.3 %collective-permute-start.17 = (bf16[2,128,1152]{2,1,0:T(8,128)(2,1)S(1)}, bf16[2,128,1152]{2,1,0:T(8,128)(2,1)S(1)}, u32[]{:S(2)}, u32[]{:S(2)}) collective-permute-start(bf16[2,128,1152]{2,1,0:T(8,128)(2,1)S(1)} %collective-permute-done.11.near_ref), channel_id=1, source_target_pairs={{0,2},{1,7},{2,4},{3,1},{4,6},{5,3},{6,0},{7,5},{8,10},{9,15},{10,... | collective-permute-start | bytes 1769480 | tf_op jit(solution)/shard_map/ppermute | solution.py:57
  117.7 12.4 %collective-permute-start.18 = (f32[768,768]{1,0:T(8,128)S(1)}, f32[768,768]{1,0:T(8,128)S(1)}, u32[]{:S(2)}, u32[]{:S(2)}) collective-permute-start(f32[768,768]{1,0:T(8,128)S(1)} %hidden.5), channel_id=1, source_target_pairs={{0,1},{1,0},{2,3},{3,2},{4,5},{5,4},{6,7},{7,6},{8,9},{9,8},{10,11... | collective-permute-start | bytes 7077896 | tf_op jit(solution)/shard_map/ppermute | solution.py:36
  123.2 6.8 %collective-permute-start.19 = (f32[768,384]{1,0:T(8,128)S(1)}, f32[768,384]{1,0:T(8,128)S(1)}, u32[]{:S(2)}, u32[]{:S(2)}) collective-permute-start(f32[768,384]{1,0:T(8,128)S(1)} %hidden.7), channel_id=1, source_target_pairs={{0,1},{1,0},{2,3},{3,2},{4,5},{5,4},{6,7},{7,6},{8,9},{9,8},{10,11... | collective-permute-start | bytes 3538952 | tf_op jit(solution)/shard_map/ppermute | solution.py:36
  130.9 3.8 %collective-permute-start.20 = (bf16[768,1152]{1,0:T(8,128)(2,1)S(1)}, bf16[768,1152]{1,0:T(8,128)(2,1)S(1)}, u32[]{:S(2)}, u32[]{:S(2)}) collective-permute-start(bf16[768,1152]{1,0:T(8,128)(2,1)S(1)} %act.1.ad_ref.mine_ref), channel_id=1, source_target_pairs={{0,1},{1,0},{2,3},{3,2},{4,5},{5,4},{6,7},{7,6},{8,9},{9,8},{10,11... | collective-permute-start | bytes 5308424 | tf_op jit(solution)/shard_map/ppermute | solution.py:36
  140.9 97.6 %all-to-all-start = ((bf16[64,2,48,512]{3,2,1,0:T(8,128)(2,1)}), bf16[64,2,48,512]{3,2,1,0:T(8,128)(2,1)}, u32[]{:S(2)}, u32[]{:S(2)}) async-start(bf16[64,2,48,512]{3,2,1,0:T(8,128)(2,1)} %bitcast.46), calls=%async_computation | async-start | bytes 12582912 | tf_op jit(solution)/shard_map/all_to_all | solution.py:408
  168.3 7.9 %collective-permute-start.21 = (bf16[2,3,192,2048]{3,2,1,0:T(8,128)(2,1)S(1)}, bf16[2,3,192,2048]{3,2,1,0:T(8,128)(2,1)S(1)}, u32[]{:S(2)}, u32[]{:S(2)}) collective-permute-start(bf16[2,3,192,2048]{3,2,1,0:T(8,128)(2,1)S(1)} %get-tuple-element.69), channel_id=1, source_target_pairs={{0,1},{1,0},{2,3},{3,2},{4,5},{5,4},{6,7},{7,6},{8,9},{9,8},{10,11... | collective-permute-start | bytes 14155784 | tf_op jit(solution)/shard_map/ppermute | solution.py:36
  178.3 60.2 %copy-start.12 = (bf16[128,3200]{1,0:T(8,128)(2,1)S(1)}, bf16[128,3200]{1,0:T(8,128)(2,1)}, u32[]{:S(2)}) copy-start(bf16[128,3200]{1,0:T(8,128)(2,1)} %pack.1.pw_ref) | copy-start | bytes 2457604
  (23 other events, 133.3 us)

commit v4 on v3

--- a/solution.py
+++ b/solution.py
@@ -176,10 +176,11 @@
 
 
 def partial_kernel(e_ref, ad_ref, wgu_ref, *rest):
-    out_ref = rest[-1]
+    ring_ref, rows_ref = rest[-2:]
     n = wgu_ref.shape[1]
     got = mm(ad_ref[:, 0:n], wgu_ref[0]).astype(BF)
-    out_ref[:, 0, 0] = got.reshape(16, CAP, 512)
+    ring_ref[0, 0] = got[:, 0:256]
+    rows_ref[:, 0] = got[:, 256:512].reshape(16, CAP, 256)
 
 
 def weight_kernel(c_ref, mine_ref, theirs_ref, xs_ref, gs_ref, gg_ref, gu_ref, gd_ref, send_ref, dt):
@@ -211,7 +212,7 @@
         gd_ref[e] = in_ref[e, 2]
 
 
-def combine_kernel(c_ref, pw_ref, ret_ref, out_ref):
+def gathering(c_ref, pw_ref):
     low = c_ref[0] == 0
     places = pw_ref[0:32, 1024:1152].astype(F32)
     picks = []
@@ -219,11 +220,18 @@
         a, b = places[2 * e : 2 * e + 1], places[2 * e + 1 : 2 * e + 2]
         picks.append(chosen(jnp.where(low, a, b)).astype(F32))
         picks.append(chosen(jnp.where(low, b, a)).astype(F32))
-    pick = jnp.concatenate(picks, axis=0).T.astype(BF)
-    total = mm(pick, ret_ref[:, 0].reshape(32 * CAP, 512))
-    for x in range(1, 4):
-        total = total + mm(pick, ret_ref[:, x].reshape(32 * CAP, 512))
-    out_ref[...] = total.astype(BF)
+    return jnp.concatenate(picks, axis=0).T.astype(BF)
+
+
+def rows_kernel(c_ref, pw_ref, ret_ref, out_ref):
+    total = mm(gathering(c_ref, pw_ref), ret_ref[...].reshape(32 * CAP, 1024))
+    for j in range(4):
+        out_ref[lax.rem(j - c_ref[1] + 4, 4)] = total[:, j * 256 : (j + 1) * 256]
+
+
+def combine_kernel(c_ref, pw_ref, ret_ref, a_ref, b_ref, d_ref, e_ref, out_ref):
+    out_ref[:, 0:256] = mm(gathering(c_ref, pw_ref), ret_ref[...].reshape(32 * CAP, 256)).astype(BF)
+    out_ref[:, 256:512] = (a_ref[...] + b_ref[...] + d_ref[...] + e_ref[...]).astype(BF)
 
 
 def shards(tokens, expert_ids, route_weights, grad_out, w_gate, w_up, w_down):
@@ -389,23 +397,29 @@
 
     def partial(which, place, ad, into):
         specs = [VMEM, pl.BlockSpec((1, 4 * f, 512), lambda j, er: (er[0], 0, j))]
-        out = like((16, 4, 2, CAP, 512))
         return pl.pallas_call(
             partial_kernel,
             grid_spec=prefetched(
                 (4,),
                 specs + [pl.BlockSpec(memory_space=pl.ANY)] * len(into),
-                pl.BlockSpec((16, 1, 1, CAP, 512), lambda j, er: (0, j, place, 0, 0)),
+                [
+                    pl.BlockSpec((1, 1, slots, 256), lambda j, er: (lax.rem(j - er[1] + 4, 4), place, 0, 0)),
+                    pl.BlockSpec((16, 1, CAP, 256), lambda j, er: (0, place, 0, j)),
+                ],
             ),
-            out_shape=out,
-            input_output_aliases={3: 0} if into else {},
+            out_shape=(like((4, 2, slots, 256)), like((16, 2, CAP, 1024))),
+            input_output_aliases={3: 0, 4: 1} if into else {},
             compiler_params=params(24),
             cost_estimate=cost(2 * slots * half * 4 * f, 8e6),
             name="partial",
-        )(which, ad, wgu, *into)
-
-    sent = partial(others, 1, theirs, [partial(cs, 0, mine, [])])
-    returned = lax.all_to_all(sent.reshape(64, 2, CAP, 512), ZYX, split_axis=0, concat_axis=0, tiled=True)
+        )(jnp.concatenate([which, xx]), ad, wgu, *into)
+
+    shift = lambda v, k: lax.ppermute(v, "x", [(i, (i + k) % 4) for i in range(4)])
+    xx = jnp.reshape(x, (1,)).astype(jnp.int32)
+    ring, by_rows = partial(others, 1, theirs, partial(cs, 0, mine, []))
+    r1, r2, r3 = shift(ring[1], 1), shift(ring[2], 2), shift(ring[3], -1)
+    by_rows, mine, theirs = together(by_rows, mine, theirs)
+    row_sums = lax.all_to_all(by_rows, ZY, split_axis=0, concat_axis=0, tiled=True)
 
     pick = lambda i, cr: jnp.where(i == 0, cr[0], 1 - cr[0])
     gg, gu, gd, send = pl.pallas_call(
@@ -427,6 +441,11 @@
         cost_estimate=cost(4 * slots * half * 6 * f, 24e6),
         name="weights",
     )(cs, mine, theirs, xs, gs)
+    r1, r2, r3, gg, gu, gd, send = together(r1, r2, r3, gg, gu, gd, send)
+    kept = sum(v.astype(F32) for v in (ring[0], r1, r2, r3)).astype(BF)
+    kept = kept.reshape(2, 16, CAP, 256).transpose(1, 0, 2, 3)
+    row_sums, kept, gg, gu, gd, send = together(row_sums, kept, gg, gu, gd, send)
+    returned = lax.all_to_all(kept, ZY, split_axis=0, concat_axis=0, tiled=True)
     strips = pl.BlockSpec(strip, lambda j, cr: (0, 0, 2 * j + 1 - cr[0]))
     grads = pl.pallas_call(
         settle_kernel,
@@ -441,15 +460,27 @@
         name="settle",
     )(cs, swap(send), gg, gu, gd)
 
-    grad_tokens = pl.pallas_call(
-        combine_kernel,
-        out_shape=like((rows, 512)),
+    cx = jnp.concatenate([cs, xx])
+    sums = pl.pallas_call(
+        rows_kernel,
+        out_shape=like((4, rows, 256), F32),
         in_specs=[SMEM, VMEM, VMEM],
         out_specs=VMEM,
         compiler_params=params(24),
         cost_estimate=cost(1e9, 6.5e6),
+        name="rows",
+    )(cx, own, row_sums)
+    s1, s2, s3 = shift(sums[1], 1), shift(sums[2], 2), shift(sums[3], -1)
+    s1, s2, s3, *grads = together(s1, s2, s3, *grads)
+    grad_tokens = pl.pallas_call(
+        combine_kernel,
+        out_shape=like((rows, 512)),
+        in_specs=[SMEM] + [VMEM] * 6,
+        out_specs=VMEM,
+        compiler_params=params(24),
+        cost_estimate=cost(1e9, 6.5e6),
         name="combine",
-    )(cs, own, returned.reshape(16, 4, 2 * CAP, 512))
+    )(cx, own, returned, sums[0], s1, s2, s3)
     return (grad_tokens, *grads)
 
 

time: 244 us -> 220 us (0.902)
  waiting for transfers between devices: 111 us -> 68.3 us
  starting transfers between devices: 33.3 us -> 44.5 us
  other arithmetic: 0.44 us -> 3.35 us
  Pallas kernels: 73.4 us -> 76.1 us
    all_to_all x1 -> x2, waiting for transfers between devices: 55.1 us -> 8.74 us  [the longest x1 6.57 us: shards(): lax.all_to_all(by_rows, ZY, split_axis=0, concat_axis=0, tiled=True)]
    ppermute x0 -> x6, waiting for transfers between devices: none -> 14.8 us  [shards(): lax.ppermute(v, 'x', [(i, (i + k) % 4) for i in range(4)])]
    ppermute x0 -> x6, starting transfers between devices: none -> 8.85 us  [shards(): lax.ppermute(v, 'x', [(i, (i + k) % 4) for i in range(4)])]
    ppermute x5, waiting for transfers between devices: 7.84 us -> 0.01 us  [swap(): return lax.ppermute(v, 'c', SWAP)]
    ppermute x17, waiting for transfers between devices: 48.2 us -> 44.8 us  [hop(): return lax.ppermute(v, ('z', 'y', 'x', 'c'), to)]
    pallas_call x1, Pallas kernels: 4.47 us -> 1.52 us  [shards(): pl.pallas_call(combine_kernel, out_shape=like((rows, 512)), in_specs=[SME...]
    pallas_call x0 -> x1, Pallas kernels: none -> 2.53 us  [shards(): pl.pallas_call(rows_kernel, out_shape=like((4, rows, 256), F32), in_specs...]
    all_to_all x1 -> x2, starting transfers between devices: 8.08 us -> 10.2 us  [the longest x1 5.82 us: shards(): lax.all_to_all(by_rows, ZY, split_axis=0, concat_axis=0, tiled=True)]
  transfers between devices with their start and end apart: 23 -> 30, of which waited for: 13 -> 16; matrix products, arithmetic and copies ran while one was open for 2% -> 5% of each run, Pallas kernels for 24% -> 29%
where the time goes in v4:
time: 220 us; the launch traced here: 219 us
  Pallas kernels  76.1 us (35%)
  waiting for transfers between devices  68.3 us (31%)
  starting transfers between devices  44.5 us (20%)
  local copies, waits for them, and re-layouts  25.6 us (12%)
  other arithmetic  3.35 us (2%)
    ppermute x17, waiting for transfers between devices, hop(): return lax.ppermute(v, ('z', 'y', 'x', 'c'), to)  44.8 us
    ppermute x17, starting transfers between devices, hop(): return lax.ppermute(v, ('z', 'y', 'x', 'c'), to)  24.5 us
    pallas_call x10, Pallas kernels, select(): pl.pallas_call(kernel, grid_spec=prefetched((n,), specs + [pl.BlockSpec(m...  23.1 us
    unnamed x49, local copies, waits for them, and re-layouts  17.7 us
    ppermute x6, waiting for transfers between devices, shards(): lax.ppermute(v, 'x', [(i, (i + k) % 4) for i in range(4)])  14.8 us
    pallas_call x4, Pallas kernels, hidden(): pl.pallas_call(hidden_kernel, grid_spec=prefetched((n // chunk,), [pl.Blo...  12.5 us
    pallas_call x1, Pallas kernels, shards(): pl.pallas_call(weight_kernel, grid_spec=prefetched((2, 4), [VMEM, VMEM, p...  12.2 us
    ppermute x6, starting transfers between devices, shards(): lax.ppermute(v, 'x', [(i, (i + k) % 4) for i in range(4)])  8.85 us
  transfers between devices with their start and end apart: 30, of which 16 were waited for; matrix products, arithmetic and copies ran while one was open for 5% of the time, Pallas kernels for 29%

profile of v4, /device:TPU:0, one launch (start us, length us, event | category | flops | bytes accessed | tf_op | source)
XLA Modules:
  0.0 219.0 jit_solution(11637246428773387549)
XLA Ops:
  1.3 2.9 %pack.1.pw_ref = bf16[128,3200]{1,0:T(8,128)(2,1)} custom-call(s32[6]{0:T(128)} %stack.111.at_ref, s32[8,128]{1,0:T(8,128)} %bitcast.67, f32[8,128]{1,0:T(8,128)} %bitcast.68, bf16[128,4096]{1,0:T(8,128)(2,1)} %t1.1, bf16[128,4096]{1,0:T(8,128)(2,1)} %t1.1, bf16[128,4096]{1,0:T(8,128)(2,1)} %g3.1, bf16[128,4096]{1,0:T(8,128)(2,1)} %g3.1, ...), custom_call_target="tpu_custom_call" | custom-call | flops 10000 | bytes 2000 | tf_op jit(solution)/shard_map/pack/pallas_call | solution.py:253
  8.4 5.1 %outgoing.1 = bf16[6,192,2048]{2,1,0:T(8,128)(2,1)} custom-call(s32[1]{0:T(128)} %bitcast.c_ref.e_ref, bf16[2,192,4096]{2,1,0:T(8,128)(2,1)} %g_ref.3, bf16[2,192,4096]{2,1,0:T(8,128)(2,1)} %u_ref.3, bf16[2,192,4096]{2,1,0:T(8,128)(2,1)} %d_ref.3), custom_call_target="tpu_custom_call" | custom-call | bytes 9400 | tf_op jit(solution)/shard_map/outgoing/pallas_call | solution.py:269
  13.5 5.5 %collective-permute-done = bf16[128,3200]{1,0:T(8,128)(2,1)S(1)} collective-permute-done((bf16[128,3200]{1,0:T(8,128)(2,1)}, bf16[128,3200]{1,0:T(8,128)(2,1)S(1)}, u32[]{:S(2)}, u32[]{:S(2)}) %collective-permute-start) | collective-permute-done | bytes 819232 | tf_op jit(solution)/shard_map/ppermute | solution.py:57
  22.7 5.8 %collective-permute-done.2 = bf16[64,3200]{1,0:T(8,128)(2,1)S(1)} collective-permute-done((bf16[64,3200]{1,0:T(8,128)(2,1)S(1)}, bf16[64,3200]{1,0:T(8,128)(2,1)S(1)}, u32[]{:S(2)}, u32[]{:S(2)}) %collective-permute-start.2) | collective-permute-done | bytes 409632 | tf_op jit(solution)/shard_map/ppermute | solution.py:57
  35.8 11.0 %collective-permute-done.4.near_ref = bf16[4,128,1152]{2,1,0:T(8,128)(2,1)} collective-permute-done((bf16[4,128,1152]{2,1,0:T(8,128)(2,1)S(1)}, bf16[4,128,1152]{2,1,0:T(8,128)(2,1)}, u32[]{:S(2)}, u32[]{:S(2)}) %collective-permute-start.4) | collective-permute-done | bytes 1179680 | tf_op jit(solution)/shard_map/ppermute | solution.py:57
  47.1 2.9 %collective-permute-done.6.far_ref = bf16[4,128,1152]{2,1,0:T(8,128)(2,1)S(1)} collective-permute-done((bf16[4,128,1152]{2,1,0:T(8,128)(2,1)S(1)}, bf16[4,128,1152]{2,1,0:T(8,128)(2,1)S(1)}, u32[]{:S(2)}, u32[]{:S(2)}) %collective-permute-start.6) | collective-permute-done | bytes 1179680 | tf_op jit(solution)/shard_map/ppermute | solution.py:57
  56.8 3.9 %select.77.rest_0_ = bf16[2,768,2048]{2,1,0:T(8,128)(2,1)S(1)} custom-call(s32[18]{0:T(128)S(1)} %stack.140.info_ref, bf16[4,128,1152]{2,1,0:T(8,128)(2,1)S(1)} %pad_maximum_fusion.1.near_ref, bf16[4,128,2048]{2,1,0:T(8,128)(2,1)} %pad_maximum_fusion.g_ref), custom_call_target="tpu_custom_call" | custom-call | flops 201326 | bytes 5600 | tf_op jit(solution)/shard_map/select/pallas_call | solution.py:329
  75.4 11.8 %collective-permute-done.10.near_ref = bf16[2,128,1152]{2,1,0:T(8,128)(2,1)S(1)} collective-permute-done((bf16[2,128,1152]{2,1,0:T(8,128)(2,1)S(1)}, bf16[2,128,1152]{2,1,0:T(8,128)(2,1)S(1)}, u32[]{:S(2)}, u32[]{:S(2)}) %collective-permute-start.10) | collective-permute-done | bytes 589856 | tf_op jit(solution)/shard_map/ppermute | solution.py:57
  94.8 3.6 %select.78.rest_0_ = bf16[2,768,2048]{2,1,0:T(8,128)(2,1)S(1)} custom-call(s32[18]{0:T(128)S(1)} %stack.140.info_ref, bf16[4,128,1152]{2,1,0:T(8,128)(2,1)} %collective-permute-done.4.near_ref, bf16[4,128,1152]{2,1,0:T(8,128)(2,1)} %collective-permute-done.12.far_ref, bf16[2,768,2048]{2,1,0:T(8,128)(2,1)S(1)} %select.76.rest_0_), custom_call_target="tpu_custom_call", output_to_operand_aliasing={{}: (3, {})} | custom-call | flops 201326 | bytes 5600 | tf_op jit(solution)/shard_map/select/pallas_call | solution.py:329
  98.5 3.6 %select.79.rest_0_ = bf16[2,768,2048]{2,1,0:T(8,128)(2,1)S(1)} custom-call(s32[18]{0:T(128)S(1)} %stack.140.info_ref, bf16[4,128,1152]{2,1,0:T(8,128)(2,1)} %collective-permute-done.4.near_ref, bf16[4,128,2048]{2,1,0:T(8,128)(2,1)} %collective-permute-done.8.g_ref, bf16[2,768,2048]{2,1,0:T(8,128)(2,1)S(1)} %select.77.rest_0_), custom_call_target="tpu_custom_call", output_to_operand_aliasing={{}: (3, {})} | custom-call | flops 201326 | bytes 5600 | tf_op jit(solution)/shard_map/select/pallas_call | solution.py:329
  106.5 3.7 %select.83.rest_0_ = bf16[2,768,2048]{2,1,0:T(8,128)(2,1)S(1)} custom-call(s32[18]{0:T(128)S(1)} %stack.140.info_ref, bf16[4,128,1152]{2,1,0:T(8,128)(2,1)S(1)} %collective-permute-done.5.near_ref, bf16[4,128,2048]{2,1,0:T(8,128)(2,1)} %collective-permute-done.9.g_ref, bf16[2,768,2048]{2,1,0:T(8,128)(2,1)S(1)} %select.79.rest_0_), custom_call_target="tpu_custom_call", output_to_operand_aliasing={{}: (3, {})} | custom-call | flops 201326 | bytes 5600 | tf_op jit(solution)/shard_map/select/pallas_call | solution.py:329
  110.2 3.2 %collective-permute-done.17.far_ref = bf16[2,128,1152]{2,1,0:T(8,128)(2,1)S(1)} collective-permute-done((bf16[2,128,1152]{2,1,0:T(8,128)(2,1)S(1)}, bf16[2,128,1152]{2,1,0:T(8,128)(2,1)S(1)}, u32[]{:S(2)}, u32[]{:S(2)}) %collective-permute-start.17) | collective-permute-done | bytes 589856 | tf_op jit(solution)/shard_map/ppermute | solution.py:57
  114.7 3.2 %hidden.5 = f32[768,768]{1,0:T(8,128)S(1)} custom-call(s32[1]{0:T(128)S(6)} %sub.3.e_ref, bf16[2,768,2048]{2,1,0:T(8,128)(2,1)S(1)} %select.82.v_ref.xs_ref, bf16[2,768,2048]{2,1,0:T(8,128)(2,1)S(1)} %bitcast.65), custom_call_target="tpu_custom_call" | custom-call | flops 2415919 | bytes 9000 | tf_op jit(solution)/shard_map/hidden/pallas_call | solution.py:365
  120.4 3.0 %hidden.7 = f32[768,384]{1,0:T(8,128)S(1)} custom-call(s32[1]{0:T(128)S(6)} %sub.3.e_ref, bf16[2,768,2048]{2,1,0:T(8,128)(2,1)S(1)} %select.85.v_ref.gs_ref, bf16[2,384,2048]{2,1,0:T(8,128)(2,1)S(1)} %get-tuple-element.94.w_ref), custom_call_target="tpu_custom_call" | custom-call | flops 1207959 | bytes 9000 | tf_op jit(solution)/shard_map/hidden/pallas_call | solution.py:365
  124.0 3.0 %hidden.6.d_ref = f32[768,384]{1,0:T(8,128)S(1)} custom-call(s32[1]{0:T(128)} %bitcast.c_ref.e_ref, bf16[2,768,2048]{2,1,0:T(8,128)(2,1)S(1)} %select.85.v_ref.gs_ref, bf16[2,384,2048]{2,1,0:T(8,128)(2,1)S(1)} %get-tuple-element.94.w_ref), custom_call_target="tpu_custom_call" | custom-call | flops 1207959 | bytes 9000 | tf_op jit(solution)/shard_map/hidden/pallas_call | solution.py:365
  127.0 3.2 %hidden.4.a_ref = f32[768,768]{1,0:T(8,128)S(1)} custom-call(s32[1]{0:T(128)} %bitcast.c_ref.e_ref, bf16[2,768,2048]{2,1,0:T(8,128)(2,1)S(1)} %select.82.v_ref.xs_ref, bf16[2,768,2048]{2,1,0:T(8,128)(2,1)S(1)} %bitcast.65), custom_call_target="tpu_custom_call" | custom-call | flops 2415919 | bytes 9000 | tf_op jit(solution)/shard_map/hidden/pallas_call | solution.py:365
  131.3 4.1 %partial.2 = (bf16[4,2,768,256]{3,2,1,0:T(8,128)(2,1)S(1)}, bf16[16,2,48,1024]{3,2,1,0:T(8,128)(2,1)S(1)}) custom-call(s32[2]{0:T(128)S(1)} %get-tuple-element.135.e_ref.c_ref, bf16[768,1152]{1,0:T(8,128)(2,1)S(1)} %act.1.ad_ref.mine_ref, bf16[2,768,2048]{2,1,0:T(8,128)(2,1)S(1)} %bitcast.65), custom_call_target="tpu_custom_call" | custom-call | flops 2415919 | bytes 8000 | tf_op jit(solution)/shard_map/partial/pallas_call | solution.py:400
  135.4 4.1 %partial.3 = (bf16[4,2,768,256]{3,2,1,0:T(8,128)(2,1)S(1)}, bf16[16,2,48,1024]{3,2,1,0:T(8,128)(2,1)S(1)}) custom-call(s32[2]{0:T(128)S(1)} %get-tuple-element.136.e_ref, bf16[768,1152]{1,0:T(8,128)(2,1)S(1)} %collective-permute-done.20.ad_ref.theirs_ref, bf16[2,768,2048]{2,1,0:T(8,128)(2,1)S(1)} %bitcast.65, ...), custom_call_target="tpu_custom_call", output_to_operand_aliasing={{0}: (3, {}), {1}: (4, {})} | custom-call | flops 2415919 | bytes 8000 | tf_op jit(solution)/shard_map/partial/pallas_call | solution.py:400
  142.8 5.8 %all-to-all-start = ((bf16[16,2,48,1024]{3,2,1,0:T(8,128)(2,1)}), bf16[16,2,48,1024]{3,2,1,0:T(8,128)(2,1)}, u32[]{:S(2)}, u32[]{:S(2)}) async-start(bf16[16,2,48,1024]{3,2,1,0:T(8,128)(2,1)} %copy-done.6), calls=%async_computation | async-start | bytes 6291456 | tf_op jit(solution)/shard_map/all_to_all | solution.py:422
  160.6 12.2 %weights.1 = (bf16[2,192,4096]{2,1,0:T(8,128)(2,1)}, bf16[2,192,4096]{2,1,0:T(8,128)(2,1)}, bf16[2,192,4096]{2,1,0:T(8,128)(2,1)}, bf16[2,3,192,2048]{3,2,1,0:T(8,128)(2,1)S(1)}) custom-call(s32[1]{0:T(128)} %bitcast.c_ref.e_ref, bf16[768,1152]{1,0:T(8,128)(2,1)S(1)} %act.1.ad_ref.mine_ref, bf16[768,1152]{1,0:T(8,128)(2,1)S(1)} %copy-done.12, ...), custom_call_target="tpu_custom_call" | custom-call | flops 7247757 | bytes 24000 | tf_op jit(solution)/shard_map/weights/pallas_call | solution.py:425
  175.0 13.3 %collective-permute-done.21 = bf16[2,768,256]{2,1,0:T(8,128)(2,1)S(1)} collective-permute-done((bf16[2,768,256]{2,1,0:T(8,128)(2,1)S(1)}, bf16[2,768,256]{2,1,0:T(8,128)(2,1)S(1)}, u32[]{:S(2)}, u32[]{:S(2)}) %collective-permute-start.21) | collective-permute-done | bytes 786464 | tf_op jit(solution)/shard_map/ppermute | solution.py:417
  191.4 6.6 %all-to-all-done.ret_ref = bf16[16,2,48,1024]{3,2,1,0:T(8,128)(2,1)} async-done(((bf16[16,2,48,1024]{3,2,1,0:T(8,128)(2,1)}), bf16[16,2,48,1024]{3,2,1,0:T(8,128)(2,1)}, u32[]{:S(2)}, u32[]{:S(2)}) %all-to-all-start) | async-done | bytes 3145760 | tf_op jit(solution)/shard_map/all_to_all | solution.py:422
  198.0 4.4 %all-to-all-start.1 = ((bf16[16,2,48,256]{3,2,1,0:T(8,128)(2,1)}), bf16[16,2,48,256]{3,2,1,0:T(8,128)(2,1)S(1)}, u32[]{:S(2)}, u32[]{:S(2)}) async-start(bf16[16,2,48,256]{3,2,1,0:T(8,128)(2,1)} %bitcast.63), calls=%async_computation.1 | async-start | bytes 1572864 | tf_op jit(solution)/shard_map/all_to_all | solution.py:448
  209.5 5.0 %settle.1 = (bf16[2,192,4096]{2,1,0:T(8,128)(2,1)}, bf16[2,192,4096]{2,1,0:T(8,128)(2,1)}, bf16[2,192,4096]{2,1,0:T(8,128)(2,1)}) custom-call(s32[1]{0:T(128)} %bitcast.c_ref.e_ref, bf16[2,3,192,2048]{3,2,1,0:T(8,128)(2,1)} %collective-permute-done.27.in_ref, ...), custom_call_target="tpu_custom_call", output_to_operand_aliasing={{0}: (2, {}), {1}: (3, {}), {2}: (4, {})} | custom-call | bytes 9400 | tf_op jit(solution)/shard_map/settle/pallas_call | solution.py:450
  (132 shorter events, 86.7 us)
Async XLA Ops:
  4.3 14.7 %collective-permute-start = (bf16[128,3200]{1,0:T(8,128)(2,1)}, bf16[128,3200]{1,0:T(8,128)(2,1)S(1)}, u32[]{:S(2)}, u32[]{:S(2)}) collective-permute-start(bf16[128,3200]{1,0:T(8,128)(2,1)} %pack.1.pw_ref), channel_id=1, source_target_pairs={{0,32},{1,9},{2,34},{3,11},{4,36},{5,13},{6,38},{7,15},{8,40},{9,1... | collective-permute-start | bytes 2457608 | tf_op jit(solution)/shard_map/ppermute | solution.py:57
  6.3 12.7 %collective-permute-start.1 = (bf16[128,3200]{1,0:T(8,128)(2,1)}, bf16[128,3200]{1,0:T(8,128)(2,1)S(1)}, u32[]{:S(2)}, u32[]{:S(2)}) collective-permute-start(bf16[128,3200]{1,0:T(8,128)(2,1)} %pack.1.pw_ref), channel_id=1, source_target_pairs={{0,96},{1,25},{2,98},{3,27},{4,100},{5,29},{6,102},{7,31},{8,104},... | collective-permute-start | bytes 2457608 | tf_op jit(solution)/shard_map/ppermute | solution.py:57
  19.0 32.0 %collective-permute-start.7 = (bf16[6,192,2048]{2,1,0:T(8,128)(2,1)}, bf16[6,192,2048]{2,1,0:T(8,128)(2,1)S(1)}, u32[]{:S(2)}, u32[]{:S(2)}) collective-permute-start(bf16[6,192,2048]{2,1,0:T(8,128)(2,1)} %outgoing.1), channel_id=1, source_target_pairs={{0,1},{1,0},{2,3},{3,2},{4,5},{5,4},{6,7},{7,6},{8,9},{9,8},{10,11... | collective-permute-start | bytes 14155784 | tf_op jit(solution)/shard_map/ppermute | solution.py:36
  29.2 17.6 %collective-permute-start.4 = (bf16[4,128,1152]{2,1,0:T(8,128)(2,1)S(1)}, bf16[4,128,1152]{2,1,0:T(8,128)(2,1)}, u32[]{:S(2)}, u32[]{:S(2)}) collective-permute-start(bf16[4,128,1152]{2,1,0:T(8,128)(2,1)S(1)} %pad_maximum_fusion.1.near_ref), channel_id=1, source_target_pairs={{0,8},{1,33},{2,10},{3,35},{4,12},{5,37},{6,14},{7,39},{8,16},{9,4... | collective-permute-start | bytes 3538952 | tf_op jit(solution)/shard_map/ppermute | solution.py:57
  30.9 16.2 %collective-permute-start.5 = (bf16[4,128,1152]{2,1,0:T(8,128)(2,1)S(1)}, bf16[4,128,1152]{2,1,0:T(8,128)(2,1)S(1)}, u32[]{:S(2)}, u32[]{:S(2)}) collective-permute-start(bf16[4,128,1152]{2,1,0:T(8,128)(2,1)S(1)} %pad_maximum_fusion.1.near_ref), channel_id=1, source_target_pairs={{0,24},{1,97},{2,26},{3,99},{4,28},{5,101},{6,30},{7,103},{8,0},{9... | collective-permute-start | bytes 3538952 | tf_op jit(solution)/shard_map/ppermute | solution.py:57
  32.5 17.4 %collective-permute-start.6 = (bf16[4,128,1152]{2,1,0:T(8,128)(2,1)S(1)}, bf16[4,128,1152]{2,1,0:T(8,128)(2,1)S(1)}, u32[]{:S(2)}, u32[]{:S(2)}) collective-permute-start(bf16[4,128,1152]{2,1,0:T(8,128)(2,1)S(1)} %pad_maximum_fusion.1.near_ref), channel_id=1, source_target_pairs={{0,2},{1,7},{2,4},{3,1},{4,6},{5,3},{6,0},{7,5},{8,10},{9,15},{10,... | collective-permute-start | bytes 3538952 | tf_op jit(solution)/shard_map/ppermute | solution.py:57
  53.2 17.7 %collective-permute-start.12 = (bf16[4,128,1152]{2,1,0:T(8,128)(2,1)}, bf16[4,128,1152]{2,1,0:T(8,128)(2,1)}, u32[]{:S(2)}, u32[]{:S(2)}) collective-permute-start(bf16[4,128,1152]{2,1,0:T(8,128)(2,1)} %collective-permute-done.4.near_ref), channel_id=1, source_target_pairs={{0,2},{1,7},{2,4},{3,1},{4,6},{5,3},{6,0},{7,5},{8,10},{9,15},{10,... | collective-permute-start | bytes 3538952 | tf_op jit(solution)/shard_map/ppermute | solution.py:57
  53.4 33.8 %collective-permute-start.8 = (bf16[4,128,2048]{2,1,0:T(8,128)(2,1)}, bf16[4,128,2048]{2,1,0:T(8,128)(2,1)}, u32[]{:S(2)}, u32[]{:S(2)}) collective-permute-start(bf16[4,128,2048]{2,1,0:T(8,128)(2,1)} %pad_maximum_fusion.g_ref), channel_id=1, source_target_pairs={{0,8},{1,33},{2,10},{3,35},{4,12},{5,37},{6,14},{7,39},{8,16},{9,4... | collective-permute-start | bytes 6291464 | tf_op jit(solution)/shard_map/ppermute | solution.py:57
  53.8 33.4 %collective-permute-start.9 = (bf16[4,128,2048]{2,1,0:T(8,128)(2,1)}, bf16[4,128,2048]{2,1,0:T(8,128)(2,1)}, u32[]{:S(2)}, u32[]{:S(2)}) collective-permute-start(bf16[4,128,2048]{2,1,0:T(8,128)(2,1)} %pad_maximum_fusion.g_ref), channel_id=1, source_target_pairs={{0,24},{1,97},{2,26},{3,99},{4,28},{5,101},{6,30},{7,103},{8,0},{9... | collective-permute-start | bytes 6291464 | tf_op jit(solution)/shard_map/ppermute | solution.py:57
  70.9 17.4 %collective-permute-start.13 = (bf16[4,128,1152]{2,1,0:T(8,128)(2,1)S(1)}, bf16[4,128,1152]{2,1,0:T(8,128)(2,1)S(1)}, u32[]{:S(2)}, u32[]{:S(2)}) collective-permute-start(bf16[4,128,1152]{2,1,0:T(8,128)(2,1)S(1)} %collective-permute-done.5.near_ref), channel_id=1, source_target_pairs={{0,2},{1,7},{2,4},{3,1},{4,6},{5,3},{6,0},{7,5},{8,10},{9,15},{10,... | collective-permute-start | bytes 3538952 | tf_op jit(solution)/shard_map/ppermute | solution.py:57
  72.1 15.2 %collective-permute-start.10 = (bf16[2,128,1152]{2,1,0:T(8,128)(2,1)S(1)}, bf16[2,128,1152]{2,1,0:T(8,128)(2,1)S(1)}, u32[]{:S(2)}, u32[]{:S(2)}) collective-permute-start(bf16[2,128,1152]{2,1,0:T(8,128)(2,1)S(1)} %slice.76), channel_id=1, source_target_pairs={{0,8},{1,33},{2,10},{3,35},{4,12},{5,37},{6,14},{7,39},{8,16},{9,4... | collective-permute-start | bytes 1769480 | tf_op jit(solution)/shard_map/ppermute | solution.py:57
  72.5 14.7 %collective-permute-start.11 = (bf16[2,128,1152]{2,1,0:T(8,128)(2,1)S(1)}, bf16[2,128,1152]{2,1,0:T(8,128)(2,1)S(1)}, u32[]{:S(2)}, u32[]{:S(2)}) collective-permute-start(bf16[2,128,1152]{2,1,0:T(8,128)(2,1)S(1)} %slice.77), channel_id=1, source_target_pairs={{0,24},{1,97},{2,26},{3,99},{4,28},{5,101},{6,30},{7,103},{8,0},{9... | collective-permute-start | bytes 1769480 | tf_op jit(solution)/shard_map/ppermute | solution.py:57
  88.3 13.8 %collective-permute-start.16 = (bf16[2,128,1152]{2,1,0:T(8,128)(2,1)S(1)}, bf16[2,128,1152]{2,1,0:T(8,128)(2,1)S(1)}, u32[]{:S(2)}, u32[]{:S(2)}) collective-permute-start(bf16[2,128,1152]{2,1,0:T(8,128)(2,1)S(1)} %collective-permute-done.10.near_ref), channel_id=1, source_target_pairs={{0,2},{1,7},{2,4},{3,1},{4,6},{5,3},{6,0},{7,5},{8,10},{9,15},{10,... | collective-permute-start | bytes 1769480 | tf_op jit(solution)/shard_map/ppermute | solution.py:57
  90.1 24.5 %collective-permute-start.14 = (bf16[2,128,2048]{2,1,0:T(8,128)(2,1)S(1)}, bf16[2,128,2048]{2,1,0:T(8,128)(2,1)S(1)}, u32[]{:S(2)}, u32[]{:S(2)}) collective-permute-start(bf16[2,128,2048]{2,1,0:T(8,128)(2,1)S(1)} %slice.78), channel_id=1, source_target_pairs={{0,8},{1,33},{2,10},{3,35},{4,12},{5,37},{6,14},{7,39},{8,16},{9,4... | collective-permute-start | bytes 3145736 | tf_op jit(solution)/shard_map/ppermute | solution.py:57
  92.3 22.4 %collective-permute-start.15 = (bf16[2,128,2048]{2,1,0:T(8,128)(2,1)S(1)}, bf16[2,128,2048]{2,1,0:T(8,128)(2,1)S(1)}, u32[]{:S(2)}, u32[]{:S(2)}) collective-permute-start(bf16[2,128,2048]{2,1,0:T(8,128)(2,1)S(1)} %slice.79), channel_id=1, source_target_pairs={{0,24},{1,97},{2,26},{3,99},{4,28},{5,101},{6,30},{7,103},{8,0},{9... | collective-permute-start | bytes 3145736 | tf_op jit(solution)/shard_map/ppermute | solution.py:57
  102.1 11.3 %collective-permute-start.17 = (bf16[2,128,1152]{2,1,0:T(8,128)(2,1)S(1)}, bf16[2,128,1152]{2,1,0:T(8,128)(2,1)S(1)}, u32[]{:S(2)}, u32[]{:S(2)}) collective-permute-start(bf16[2,128,1152]{2,1,0:T(8,128)(2,1)S(1)} %collective-permute-done.11.near_ref), channel_id=1, source_target_pairs={{0,2},{1,7},{2,4},{3,1},{4,6},{5,3},{6,0},{7,5},{8,10},{9,15},{10,... | collective-permute-start | bytes 1769480 | tf_op jit(solution)/shard_map/ppermute | solution.py:57
  117.9 12.4 %collective-permute-start.18 = (f32[768,768]{1,0:T(8,128)S(1)}, f32[768,768]{1,0:T(8,128)S(1)}, u32[]{:S(2)}, u32[]{:S(2)}) collective-permute-start(f32[768,768]{1,0:T(8,128)S(1)} %hidden.5), channel_id=1, source_target_pairs={{0,1},{1,0},{2,3},{3,2},{4,5},{5,4},{6,7},{7,6},{8,9},{9,8},{10,11... | collective-permute-start | bytes 7077896 | tf_op jit(solution)/shard_map/ppermute | solution.py:36
  142.8 55.2 %all-to-all-start = ((bf16[16,2,48,1024]{3,2,1,0:T(8,128)(2,1)}), bf16[16,2,48,1024]{3,2,1,0:T(8,128)(2,1)}, u32[]{:S(2)}, u32[]{:S(2)}) async-start(bf16[16,2,48,1024]{3,2,1,0:T(8,128)(2,1)} %copy-done.6), calls=%async_computation | async-start | bytes 6291456 | tf_op jit(solution)/shard_map/all_to_all | solution.py:422
  150.6 37.8 %collective-permute-start.21 = (bf16[2,768,256]{2,1,0:T(8,128)(2,1)S(1)}, bf16[2,768,256]{2,1,0:T(8,128)(2,1)S(1)}, u32[]{:S(2)}, u32[]{:S(2)}) collective-permute-start(bf16[2,768,256]{2,1,0:T(8,128)(2,1)S(1)} %get-tuple-element.130), channel_id=1, source_target_pairs={{0,2},{2,4},{4,6},{6,0},{1,3},{3,5},{5,7},{7,1},{8,10},{10,12},{12... | collective-permute-start | bytes 2359304 | tf_op jit(solution)/shard_map/ppermute | solution.py:417
  150.7 37.7 %collective-permute-start.22 = (bf16[2,768,256]{2,1,0:T(8,128)(2,1)S(1)}, bf16[2,768,256]{2,1,0:T(8,128)(2,1)S(1)}, u32[]{:S(2)}, u32[]{:S(2)}) collective-permute-start(bf16[2,768,256]{2,1,0:T(8,128)(2,1)S(1)} %get-tuple-element.129), channel_id=1, source_target_pairs={{0,4},{2,6},{4,0},{6,2},{1,5},{3,7},{5,1},{7,3},{8,12},{10,14},{12... | collective-permute-start | bytes 2359304 | tf_op jit(solution)/shard_map/ppermute | solution.py:417
  152.6 36.3 %collective-permute-start.23 = (bf16[2,768,256]{2,1,0:T(8,128)(2,1)S(1)}, bf16[2,768,256]{2,1,0:T(8,128)(2,1)S(1)}, u32[]{:S(2)}, u32[]{:S(2)}) collective-permute-start(bf16[2,768,256]{2,1,0:T(8,128)(2,1)S(1)} %get-tuple-element.128), channel_id=1, source_target_pairs={{0,6},{2,0},{4,2},{6,4},{1,7},{3,1},{5,3},{7,5},{8,14},{10,8},{12,... | collective-permute-start | bytes 2359304 | tf_op jit(solution)/shard_map/ppermute | solution.py:417
  198.0 11.5 %collective-permute-start.27 = (bf16[2,3,192,2048]{3,2,1,0:T(8,128)(2,1)}, bf16[2,3,192,2048]{3,2,1,0:T(8,128)(2,1)}, u32[]{:S(2)}, u32[]{:S(2)}) collective-permute-start(bf16[2,3,192,2048]{3,2,1,0:T(8,128)(2,1)} %copy-done.17), channel_id=1, source_target_pairs={{0,1},{1,0},{2,3},{3,2},{4,5},{5,4},{6,7},{7,6},{8,9},{9,8},{10,11... | collective-permute-start | bytes 14155784 | tf_op jit(solution)/shard_map/ppermute | solution.py:36
  198.0 19.5 %all-to-all-start.1 = ((bf16[16,2,48,256]{3,2,1,0:T(8,128)(2,1)}), bf16[16,2,48,256]{3,2,1,0:T(8,128)(2,1)S(1)}, u32[]{:S(2)}, u32[]{:S(2)}) async-start(bf16[16,2,48,256]{3,2,1,0:T(8,128)(2,1)} %bitcast.63), calls=%async_computation.1 | async-start | bytes 1572864 | tf_op jit(solution)/shard_map/all_to_all | solution.py:448
  205.0 9.7 %collective-permute-start.24 = (f32[128,256]{1,0:T(8,128)S(1)}, f32[128,256]{1,0:T(8,128)S(1)}, u32[]{:S(2)}, u32[]{:S(2)}) collective-permute-start(f32[128,256]{1,0:T(8,128)S(1)} %get-tuple-element.133), channel_id=1, source_target_pairs={{0,2},{2,4},{4,6},{6,0},{1,3},{3,5},{5,7},{7,1},{8,10},{10,12},{12... | collective-permute-start | bytes 393224 | tf_op jit(solution)/shard_map/ppermute | solution.py:417
  (30 other events, 189.2 us)

commit v5 on v4

--- a/solution.py
+++ b/solution.py
@@ -175,12 +175,12 @@
     out_ref[:, 2 * n :] = (silu * up).astype(BF)
 
 
-def partial_kernel(e_ref, ad_ref, wgu_ref, *rest):
-    ring_ref, rows_ref = rest[-2:]
-    n = wgu_ref.shape[1]
-    got = mm(ad_ref[:, 0:n], wgu_ref[0]).astype(BF)
-    ring_ref[0, 0] = got[:, 0:256]
-    rows_ref[:, 0] = got[:, 256:512].reshape(16, CAP, 256)
+def by_x_kernel(e_ref, ad_ref, wgu_ref, out_ref):
+    out_ref[0] = mm(ad_ref[:, 0 : wgu_ref.shape[1]], wgu_ref[0]).astype(BF)
+
+
+def by_block_kernel(e_ref, ad_ref, wgu_ref, out_ref):
+    out_ref[...] = mm(ad_ref[:, 0 : wgu_ref.shape[1]], wgu_ref[0]).astype(BF).reshape(out_ref.shape)
 
 
 def weight_kernel(c_ref, mine_ref, theirs_ref, xs_ref, gs_ref, gg_ref, gu_ref, gd_ref, send_ref, dt):
@@ -212,26 +212,27 @@
         gd_ref[e] = in_ref[e, 2]
 
 
-def gathering(c_ref, pw_ref):
-    low = c_ref[0] == 0
+def gathering(parity, pw_ref):
+    low = parity == 0
     places = pw_ref[0:32, 1024:1152].astype(F32)
     picks = []
     for e in range(16):
-        a, b = places[2 * e : 2 * e + 1], places[2 * e + 1 : 2 * e + 2]
-        picks.append(chosen(jnp.where(low, a, b)).astype(F32))
-        picks.append(chosen(jnp.where(low, b, a)).astype(F32))
+        row = jnp.where(low, places[2 * e : 2 * e + 1], places[2 * e + 1 : 2 * e + 2])
+        picks.append(chosen(row).astype(F32))
     return jnp.concatenate(picks, axis=0).T.astype(BF)
 
 
 def rows_kernel(c_ref, pw_ref, ret_ref, out_ref):
-    total = mm(gathering(c_ref, pw_ref), ret_ref[...].reshape(32 * CAP, 1024))
+    total = mm(gathering(c_ref[0], pw_ref), ret_ref[...].reshape(16 * CAP, 2048)).astype(BF)
     for j in range(4):
-        out_ref[lax.rem(j - c_ref[1] + 4, 4)] = total[:, j * 256 : (j + 1) * 256]
+        out_ref[lax.rem(j - c_ref[1] + 4, 4)] = total[:, j * 512 : (j + 1) * 512]
 
 
 def combine_kernel(c_ref, pw_ref, ret_ref, a_ref, b_ref, d_ref, e_ref, out_ref):
-    out_ref[:, 0:256] = mm(gathering(c_ref, pw_ref), ret_ref[...].reshape(32 * CAP, 256)).astype(BF)
-    out_ref[:, 256:512] = (a_ref[...] + b_ref[...] + d_ref[...] + e_ref[...]).astype(BF)
+    total = mm(gathering(1 - c_ref[0], pw_ref), ret_ref[...].reshape(16 * CAP, 512))
+    for ref in (a_ref, b_ref, d_ref, e_ref):
+        total = total + ref[...].astype(F32)
+    out_ref[...] = total.astype(BF)
 
 
 def shards(tokens, expert_ids, route_weights, grad_out, w_gate, w_up, w_down):
@@ -280,17 +281,12 @@
 
     up, down = hop(own, first(1)), hop(own, first(-1))
     up, down, outgoing = together(up, down, outgoing)
-    far = jnp.concatenate([hop(up[:64], first(1)), hop(down[64:], first(-1))], axis=0)
-    incoming = swap(outgoing)
+    far0, far1, incoming = hop(up[:64], first(1)), hop(down[64:], first(-1)), swap(outgoing)
+    far0, far1, incoming = together(far0, far1, incoming)
+    far = jnp.concatenate([far0, far1], axis=0)
     line = [own, up, down, far]
     xg = jnp.stack([v[:, :1152] for v in line])
     gg = jnp.stack([v[:, 1152:] for v in line])
-    xm, xr, xg_far = hop(xg, second(1)), hop(xg, second(-1)), hop(xg, along)
-    gg, xm, xr, xg_far, incoming = together(gg, xm, xr, xg_far, incoming)
-    gm, gr = hop(gg, second(1)), hop(gg, second(-1))
-    xd0, xd1 = hop(xm[:2], second(1)), hop(xr[2:], second(-1))
-    xm_far = hop(xm, along)
-
     wgu, wd = pl.pallas_call(
         assemble_kernel,
         grid_spec=prefetched(
@@ -307,6 +303,11 @@
         cost_estimate=cost(0, 19e6),
         name="assemble",
     )(cs, w_gate, w_up, w_down, incoming)
+    xm, xr, xg_far = hop(xg, second(1)), hop(xg, second(-1)), hop(xg, along)
+    gg, xm, xr, xg_far, wgu, wd = together(gg, xm, xr, xg_far, wgu, wd)
+    gm, gr = hop(gg, second(1)), hop(gg, second(-1))
+    xd0, xd1 = hop(xm[:2], second(1)), hop(xr[2:], second(-1))
+    xm_far = hop(xm, along)
 
     offsets = (0, -1, 1, 2)
     table = []
@@ -316,16 +317,16 @@
             table.append((z + oz + 4) % 4 * 4 + (y + oy + 4) % 4)
     info = jnp.stack([2 * (z * 4 + y), side] + table).astype(jnp.int32)
 
-    def select(kernel, start, near, other, into):
+    def select(kernel, start, near, other, into, skip=0):
         is_x = kernel is select_x_kernel
         if is_x:
             specs = [pl.BlockSpec((1, rows, 1152), lambda i, fo: (i, 0, 0))] * 2
         else:
             specs = [
-                pl.BlockSpec((1, rows, 128), lambda i, fo: (i, 0, 8)),
+                pl.BlockSpec((1, rows, 128), lambda i, fo: (i + skip, 0, 8)),
                 pl.BlockSpec((1, rows, half), lambda i, fo: (i, 0, 0)),
             ]
-        n = near.shape[0]
+        n = other.shape[0]
         return pl.pallas_call(
             kernel,
             grid_spec=prefetched(
@@ -343,23 +344,17 @@
 
     xs = select(select_x_kernel, 0, xg, xg_far, [])
     gs = select(select_g_kernel, 0, xg, gg, [])
-    xm_far, xr_go, xs, gs, wgu, wd = together(xm_far, xr, xs, gs, wgu, wd)
+    xm_far, xr_go, xs, gs = together(xm_far, xr, xs, gs)
     xr_far = hop(xr_go, along)
-    gm, gr, xd0, xd1, xr_far = together(gm, gr, xd0, xd1, xr_far)
+    xs = select(select_x_kernel, 4, xm, xm_far, [xs])
+    gm, gr, xd0, xd1, xr_far, xs = together(gm, gr, xd0, xd1, xr_far, xs)
     gd0, gd1 = hop(gm[:2], second(1)), hop(gr[2:], second(-1))
-    xd0_far = hop(xd0, along)
-    xs = select(select_x_kernel, 4, xm, xm_far, [xs])
+    xd = jnp.concatenate([xd0, xd1], axis=0)
+    xd_far = hop(xd, along)
     gs = select(select_g_kernel, 4, xm, gm, [gs])
-    xd0_far, xd1, xs, gs = together(xd0_far, xd1, xs, gs)
-    xd1_far = hop(xd1, along)
     xs = select(select_x_kernel, 8, xr, xr_far, [xs])
-    xs = select(select_x_kernel, 12, xd0, xd0_far, [xs])
     gs = select(select_g_kernel, 8, xr, gr, [gs])
-    xs = select(select_x_kernel, 14, xd1, xd1_far, [xs])
-    gd0, gd1, xs, gs = together(gd0, gd1, xs, gs)
-    gs = select(select_g_kernel, 12, xd0, gd0, [gs])
-    gs = select(select_g_kernel, 14, xd1, gd1, [gs])
-
+    xs = select(select_x_kernel, 12, xd, xd_far, [xs])
     def hidden(which, v, w, chunk):
         n = w.shape[1]
         return pl.pallas_call(
@@ -378,8 +373,11 @@
             name="hidden",
         )(which, v, w)
 
-    pre_in = swap(hidden(others, xs, wgu, 256))
-    pre = hidden(cs, xs, wgu, 256)
+    pre_out, pre = hidden(others, xs, wgu, 256), hidden(cs, xs, wgu, 256)
+    gd0, gd1, gs, pre_out, pre = together(gd0, gd1, gs, pre_out, pre)
+    pre_in = swap(pre_out)
+    gs = select(select_g_kernel, 12, xd, gd0, [gs])
+    gs = select(select_g_kernel, 14, xd, gd1, [gs], 2)
     dh_in = swap(hidden(others, gs, wd, 128))
     dh = hidden(cs, gs, wd, 128)
     quarter = lambda n: pl.BlockSpec((slots // 4, n), lambda j: (j, 0))
@@ -395,31 +393,32 @@
     )(pre, pre_in, dh, dh_in)
     theirs = swap(mine)
 
-    def partial(which, place, ad, into):
-        specs = [VMEM, pl.BlockSpec((1, 4 * f, 512), lambda j, er: (er[0], 0, j))]
+    def partial(kernel, which, ad):
+        if kernel is by_x_kernel:
+            shape = (4, slots, 512)
+            out = pl.BlockSpec((1, slots, 512), lambda j, er: (lax.rem(j - er[1] + 4, 4), 0, 0))
+        else:
+            shape = (16, CAP, half)
+            out = pl.BlockSpec((16, CAP, 512), lambda j, er: (0, 0, j))
         return pl.pallas_call(
-            partial_kernel,
+            kernel,
             grid_spec=prefetched(
-                (4,),
-                specs + [pl.BlockSpec(memory_space=pl.ANY)] * len(into),
-                [
-                    pl.BlockSpec((1, 1, slots, 256), lambda j, er: (lax.rem(j - er[1] + 4, 4), place, 0, 0)),
-                    pl.BlockSpec((16, 1, CAP, 256), lambda j, er: (0, place, 0, j)),
-                ],
+                (4,), [VMEM, pl.BlockSpec((1, 4 * f, 512), lambda j, er: (er[0], 0, j))], out
             ),
-            out_shape=(like((4, 2, slots, 256)), like((16, 2, CAP, 1024))),
-            input_output_aliases={3: 0, 4: 1} if into else {},
+            out_shape=like(shape),
             compiler_params=params(24),
             cost_estimate=cost(2 * slots * half * 4 * f, 8e6),
             name="partial",
-        )(jnp.concatenate([which, xx]), ad, wgu, *into)
+        )(jnp.concatenate([which, xx]), ad, wgu)
 
     shift = lambda v, k: lax.ppermute(v, "x", [(i, (i + k) % 4) for i in range(4)])
     xx = jnp.reshape(x, (1,)).astype(jnp.int32)
-    ring, by_rows = partial(others, 1, theirs, partial(cs, 0, mine, []))
+    by_block = partial(by_block_kernel, cs, mine)
+    row_sums = lax.all_to_all(by_block, ZY, split_axis=0, concat_axis=0, tiled=True)
+    by_block, theirs = together(by_block, theirs)
+    ring = partial(by_x_kernel, others, theirs)
+    ring, mine, theirs = together(ring, mine, theirs)
     r1, r2, r3 = shift(ring[1], 1), shift(ring[2], 2), shift(ring[3], -1)
-    by_rows, mine, theirs = together(by_rows, mine, theirs)
-    row_sums = lax.all_to_all(by_rows, ZY, split_axis=0, concat_axis=0, tiled=True)
 
     pick = lambda i, cr: jnp.where(i == 0, cr[0], 1 - cr[0])
     gg, gu, gd, send = pl.pallas_call(
@@ -443,7 +442,7 @@
     )(cs, mine, theirs, xs, gs)
     r1, r2, r3, gg, gu, gd, send = together(r1, r2, r3, gg, gu, gd, send)
     kept = sum(v.astype(F32) for v in (ring[0], r1, r2, r3)).astype(BF)
-    kept = kept.reshape(2, 16, CAP, 256).transpose(1, 0, 2, 3)
+    kept = kept.reshape(16, CAP, 512)
     row_sums, kept, gg, gu, gd, send = together(row_sums, kept, gg, gu, gd, send)
     returned = lax.all_to_all(kept, ZY, split_axis=0, concat_axis=0, tiled=True)
     strips = pl.BlockSpec(strip, lambda j, cr: (0, 0, 2 * j + 1 - cr[0]))
@@ -463,7 +462,7 @@
     cx = jnp.concatenate([cs, xx])
     sums = pl.pallas_call(
         rows_kernel,
-        out_shape=like((4, rows, 256), F32),
+        out_shape=like((4, rows, 512)),
         in_specs=[SMEM, VMEM, VMEM],
         out_specs=VMEM,
         compiler_params=params(24),

time: 220 us -> 213 us (0.968)
  starting transfers between devices: 44.5 us -> 35.6 us
  local copies, waits for them, and re-layouts: 25.6 us -> 18.1 us
  Pallas kernels: 76.1 us -> 82 us
  waiting for transfers between devices: 68.3 us -> 71.4 us
    ppermute x6, waiting for transfers between devices: 14.8 us -> 22.6 us  [shards(): lax.ppermute(v, 'x', [(i, (i + k) % 4) for i in range(4)])]
    unnamed x49 -> x46, local copies, waits for them, and re-layouts: 17.7 us -> 11.8 us
    all_to_all x1, waiting for transfers between devices: 6.57 us -> 0.72 us  [shards(): lax.all_to_all(by_block, ZY, split_axis=0, concat_axis=0, tiled=True)]
    ppermute x17 -> x16, starting transfers between devices: 24.5 us -> 19 us  [hop(): return lax.ppermute(v, ('z', 'y', 'x', 'c'), to)]
    ppermute x6, starting transfers between devices: 8.85 us -> 5.11 us  [shards(): lax.ppermute(v, 'x', [(i, (i + k) % 4) for i in range(4)])]
    pallas_call x3, Pallas kernels: 10.7 us -> 14.2 us  [the longest x2 11.7 us: partial(): pl.pallas_call(kernel, grid_spec=prefetched((4,), [VMEM, pl.BlockSpec((1,...]
    ppermute x17 -> x16, waiting for transfers between devices: 44.8 us -> 46.3 us  [hop(): return lax.ppermute(v, ('z', 'y', 'x', 'c'), to)]
    pallas_call x10 -> x9, Pallas kernels: 23.1 us -> 22.1 us  [select(): pl.pallas_call(kernel, grid_spec=prefetched((n,), specs + [pl.BlockSpec(m...]
  transfers between devices with their start and end apart: 30 -> 29, of which waited for: 16 -> 17; matrix products, arithmetic and copies ran while one was open for 5% -> 4% of each run, Pallas kernels for 29% -> 36%
where the time goes in v5:
time: 213 us; the launch traced here: 212 us
  Pallas kernels  82 us (38%)
  waiting for transfers between devices  71.4 us (34%)
  starting transfers between devices  35.6 us (17%)
  local copies, waits for them, and re-layouts  18.1 us (8%)
  other arithmetic  3.45 us (2%)
    ppermute x16, waiting for transfers between devices, hop(): return lax.ppermute(v, ('z', 'y', 'x', 'c'), to)  46.3 us
    ppermute x6, waiting for transfers between devices, shards(): lax.ppermute(v, 'x', [(i, (i + k) % 4) for i in range(4)])  22.6 us
    pallas_call x9, Pallas kernels, select(): pl.pallas_call(kernel, grid_spec=prefetched((n,), specs + [pl.BlockSpec(m...  22.1 us
    ppermute x16, starting transfers between devices, hop(): return lax.ppermute(v, ('z', 'y', 'x', 'c'), to)  19 us
    pallas_call x1, Pallas kernels, shards(): pl.pallas_call(weight_kernel, grid_spec=prefetched((2, 4), [VMEM, VMEM, p...  14.2 us
    pallas_call x4, Pallas kernels, hidden(): pl.pallas_call(hidden_kernel, grid_spec=prefetched((n // chunk,), [pl.Blo...  12.4 us
    unnamed x46, local copies, waits for them, and re-layouts  11.8 us
    pallas_call x2, Pallas kernels, partial(): pl.pallas_call(kernel, grid_spec=prefetched((4,), [VMEM, pl.BlockSpec((1,...  11.7 us
  transfers between devices with their start and end apart: 29, of which 17 were waited for; matrix products, arithmetic and copies ran while one was open for 4% of the time, Pallas kernels for 36%

profile of v5, /device:TPU:0, one launch (start us, length us, event | category | flops | bytes accessed | tf_op | source)
XLA Modules:
  0.0 211.8 jit_solution(13016132712918697483)
XLA Ops:
  1.2 2.9 %pack.1.pw_ref = bf16[128,3200]{1,0:T(8,128)(2,1)} custom-call(s32[6]{0:T(128)} %stack.111.at_ref, s32[8,128]{1,0:T(8,128)} %bitcast.67, f32[8,128]{1,0:T(8,128)} %bitcast.68, bf16[128,4096]{1,0:T(8,128)(2,1)} %t1.1, bf16[128,4096]{1,0:T(8,128)(2,1)} %t1.1, bf16[128,4096]{1,0:T(8,128)(2,1)} %g3.1, bf16[128,4096]{1,0:T(8,128)(2,1)} %g3.1, ...), custom_call_target="tpu_custom_call" | custom-call | flops 10000 | bytes 2000 | tf_op jit(solution)/shard_map/pack/pallas_call | solution.py:254
  4.2 4.1 %collective-permute-start.1 = (bf16[128,3200]{1,0:T(8,128)(2,1)}, bf16[128,3200]{1,0:T(8,128)(2,1)S(1)}, u32[]{:S(2)}, u32[]{:S(2)}) collective-permute-start(bf16[128,3200]{1,0:T(8,128)(2,1)} %pack.1.pw_ref), channel_id=1, source_target_pairs={{0,96},{1,25},{2,98},{3,27},{4,100},{5,29},{6,102},{7,31},{8,104},... | collective-permute-start | bytes 2457608 | tf_op jit(solution)/shard_map/ppermute | solution.py:57
  8.3 5.1 %outgoing.1 = bf16[6,192,2048]{2,1,0:T(8,128)(2,1)} custom-call(s32[1]{0:T(128)} %bitcast.c_ref.e_ref, bf16[2,192,4096]{2,1,0:T(8,128)(2,1)} %g_ref.3, bf16[2,192,4096]{2,1,0:T(8,128)(2,1)} %u_ref.3, bf16[2,192,4096]{2,1,0:T(8,128)(2,1)} %d_ref.3), custom_call_target="tpu_custom_call" | custom-call | bytes 9400 | tf_op jit(solution)/shard_map/outgoing/pallas_call | solution.py:270
  13.4 5.1 %collective-permute-done.1 = bf16[128,3200]{1,0:T(8,128)(2,1)S(1)} collective-permute-done((bf16[128,3200]{1,0:T(8,128)(2,1)}, bf16[128,3200]{1,0:T(8,128)(2,1)S(1)}, u32[]{:S(2)}, u32[]{:S(2)}) %collective-permute-start.1) | collective-permute-done | bytes 819232 | tf_op jit(solution)/shard_map/ppermute | solution.py:57
  18.5 3.6 %collective-permute-done = bf16[128,3200]{1,0:T(8,128)(2,1)S(1)} collective-permute-done((bf16[128,3200]{1,0:T(8,128)(2,1)}, bf16[128,3200]{1,0:T(8,128)(2,1)S(1)}, u32[]{:S(2)}, u32[]{:S(2)}) %collective-permute-start) | collective-permute-done | bytes 819232 | tf_op jit(solution)/shard_map/ppermute | solution.py:57
  24.4 5.9 %collective-permute-done.3 = bf16[64,3200]{1,0:T(8,128)(2,1)S(1)} collective-permute-done((bf16[64,3200]{1,0:T(8,128)(2,1)S(1)}, bf16[64,3200]{1,0:T(8,128)(2,1)S(1)}, u32[]{:S(2)}, u32[]{:S(2)}) %collective-permute-start.3) | collective-permute-done | bytes 409632 | tf_op jit(solution)/shard_map/ppermute | solution.py:57
  45.4 5.3 %collective-permute-done.7.far_ref = bf16[4,128,1152]{2,1,0:T(8,128)(2,1)S(1)} collective-permute-done((bf16[4,128,1152]{2,1,0:T(8,128)(2,1)S(1)}, bf16[4,128,1152]{2,1,0:T(8,128)(2,1)S(1)}, u32[]{:S(2)}, u32[]{:S(2)}) %collective-permute-start.7) | collective-permute-done | bytes 1179680 | tf_op jit(solution)/shard_map/ppermute | solution.py:57
  57.6 3.6 %select.76.rest_0_ = bf16[2,768,2048]{2,1,0:T(8,128)(2,1)S(1)} custom-call(s32[18]{0:T(128)S(1)} %stack.140.info_ref, bf16[4,128,1152]{2,1,0:T(8,128)(2,1)S(1)} %pad_maximum_fusion.1.near_ref, bf16[4,128,2048]{2,1,0:T(8,128)(2,1)} %pad_maximum_fusion.g_ref), custom_call_target="tpu_custom_call" | custom-call | flops 201326 | bytes 5600 | tf_op jit(solution)/shard_map/select/pallas_call | solution.py:330
  63.0 8.7 %collective-permute-done.12.far_ref = bf16[4,128,1152]{2,1,0:T(8,128)(2,1)} collective-permute-done((bf16[4,128,1152]{2,1,0:T(8,128)(2,1)}, bf16[4,128,1152]{2,1,0:T(8,128)(2,1)}, u32[]{:S(2)}, u32[]{:S(2)}) %collective-permute-start.12) | collective-permute-done | bytes 1179680 | tf_op jit(solution)/shard_map/ppermute | solution.py:57
  75.2 3.6 %select.77.rest_0_ = bf16[2,768,2048]{2,1,0:T(8,128)(2,1)S(1)} custom-call(s32[18]{0:T(128)S(1)} %stack.140.info_ref, bf16[4,128,1152]{2,1,0:T(8,128)(2,1)} %collective-permute-done.5.near_ref, bf16[4,128,1152]{2,1,0:T(8,128)(2,1)} %collective-permute-done.12.far_ref, bf16[2,768,2048]{2,1,0:T(8,128)(2,1)S(1)} %select.75.rest_0_), custom_call_target="tpu_custom_call", output_to_operand_aliasing={{}: (3, {})} | custom-call | flops 201326 | bytes 5600 | tf_op jit(solution)/shard_map/select/pallas_call | solution.py:330
  78.8 9.2 %collective-permute-done.11 = bf16[2,128,1152]{2,1,0:T(8,128)(2,1)S(1)} collective-permute-done((bf16[2,128,1152]{2,1,0:T(8,128)(2,1)S(1)}, bf16[2,128,1152]{2,1,0:T(8,128)(2,1)S(1)}, u32[]{:S(2)}, u32[]{:S(2)}) %collective-permute-start.11) | collective-permute-done | bytes 589856 | tf_op jit(solution)/shard_map/ppermute | solution.py:57
  95.4 3.6 %select.78.rest_0_ = bf16[2,768,2048]{2,1,0:T(8,128)(2,1)S(1)} custom-call(s32[18]{0:T(128)S(1)} %stack.140.info_ref, bf16[4,128,1152]{2,1,0:T(8,128)(2,1)} %collective-permute-done.5.near_ref, bf16[4,128,2048]{2,1,0:T(8,128)(2,1)} %collective-permute-done.8.g_ref, bf16[2,768,2048]{2,1,0:T(8,128)(2,1)S(1)} %select.76.rest_0_), custom_call_target="tpu_custom_call", output_to_operand_aliasing={{}: (3, {})} | custom-call | flops 201326 | bytes 5600 | tf_op jit(solution)/shard_map/select/pallas_call | solution.py:330
  99.0 3.6 %select.79.rest_0_ = bf16[2,768,2048]{2,1,0:T(8,128)(2,1)S(1)} custom-call(s32[18]{0:T(128)S(1)} %stack.140.info_ref, bf16[4,128,1152]{2,1,0:T(8,128)(2,1)S(1)} %collective-permute-done.6.near_ref, bf16[4,128,2048]{2,1,0:T(8,128)(2,1)} %collective-permute-done.9.g_ref, bf16[2,768,2048]{2,1,0:T(8,128)(2,1)S(1)} %select.78.rest_0_), custom_call_target="tpu_custom_call", output_to_operand_aliasing={{}: (3, {})} | custom-call | flops 201326 | bytes 5600 | tf_op jit(solution)/shard_map/select/pallas_call | solution.py:330
  108.7 3.2 %hidden.5.a_ref = f32[768,768]{1,0:T(8,128)S(1)} custom-call(s32[1]{0:T(128)} %bitcast.c_ref.e_ref, bf16[2,768,2048]{2,1,0:T(8,128)(2,1)S(1)} %select.81.v_ref.xs_ref, bf16[2,768,2048]{2,1,0:T(8,128)(2,1)S(1)} %bitcast.66), custom_call_target="tpu_custom_call" | custom-call | flops 2415919 | bytes 9000 | tf_op jit(solution)/shard_map/hidden/pallas_call | solution.py:360
  111.9 3.2 %hidden.4 = f32[768,768]{1,0:T(8,128)S(1)} custom-call(s32[1]{0:T(128)S(6)} %sub.3.e_ref, bf16[2,768,2048]{2,1,0:T(8,128)(2,1)S(1)} %select.81.v_ref.xs_ref, bf16[2,768,2048]{2,1,0:T(8,128)(2,1)S(1)} %bitcast.66), custom_call_target="tpu_custom_call" | custom-call | flops 2415919 | bytes 9000 | tf_op jit(solution)/shard_map/hidden/pallas_call | solution.py:360
  118.3 3.0 %hidden.7 = f32[768,384]{1,0:T(8,128)S(1)} custom-call(s32[1]{0:T(128)S(6)} %sub.3.e_ref, bf16[2,768,2048]{2,1,0:T(8,128)(2,1)S(1)} %select.83.v_ref.gs_ref, bf16[2,384,2048]{2,1,0:T(8,128)(2,1)S(1)} %copy-done.10), custom_call_target="tpu_custom_call" | custom-call | flops 1207959 | bytes 9000 | tf_op jit(solution)/shard_map/hidden/pallas_call | solution.py:360
  121.9 3.0 %hidden.6.d_ref = f32[768,384]{1,0:T(8,128)S(1)} custom-call(s32[1]{0:T(128)} %bitcast.c_ref.e_ref, bf16[2,768,2048]{2,1,0:T(8,128)(2,1)S(1)} %select.83.v_ref.gs_ref, bf16[2,384,2048]{2,1,0:T(8,128)(2,1)S(1)} %copy-done.10), custom_call_target="tpu_custom_call" | custom-call | flops 1207959 | bytes 9000 | tf_op jit(solution)/shard_map/hidden/pallas_call | solution.py:360
  127.2 5.6 %partial.2 = bf16[16,48,2048]{2,1,0:T(8,128)(2,1)S(1)} custom-call(s32[2]{0:T(128)S(1)} %pad_add_fusion.e_ref.c_ref, bf16[768,1152]{1,0:T(8,128)(2,1)} %act.1.ad_ref.mine_ref, bf16[2,768,2048]{2,1,0:T(8,128)(2,1)S(1)} %bitcast.66), custom_call_target="tpu_custom_call" | custom-call | flops 2415919 | bytes 8000 | tf_op jit(solution)/shard_map/partial/pallas_call | solution.py:403
  134.5 4.6 %all-to-all-start = ((bf16[16,48,2048]{2,1,0:T(8,128)(2,1)}), bf16[16,48,2048]{2,1,0:T(8,128)(2,1)}, u32[]{:S(2)}, u32[]{:S(2)}) async-start(bf16[16,48,2048]{2,1,0:T(8,128)(2,1)} %copy-done.5), calls=%async_computation | async-start | bytes 6291456 | tf_op jit(solution)/shard_map/all_to_all | solution.py:417
  142.1 6.1 %partial.3 = bf16[4,768,512]{2,1,0:T(8,128)(2,1)S(1)} custom-call(s32[2]{0:T(128)S(1)} %pad_add_fusion.1.e_ref, bf16[768,1152]{1,0:T(8,128)(2,1)} %collective-permute-done.19.ad_ref.theirs_ref, bf16[2,768,2048]{2,1,0:T(8,128)(2,1)S(1)} %copy-done.3), custom_call_target="tpu_custom_call" | custom-call | flops 2415919 | bytes 8000 | tf_op jit(solution)/shard_map/partial/pallas_call | solution.py:403
  150.6 14.2 %weights.1 = (bf16[2,192,4096]{2,1,0:T(8,128)(2,1)}, bf16[2,192,4096]{2,1,0:T(8,128)(2,1)}, bf16[2,192,4096]{2,1,0:T(8,128)(2,1)}, bf16[2,3,192,2048]{3,2,1,0:T(8,128)(2,1)S(1)}) custom-call(s32[1]{0:T(128)} %bitcast.c_ref.e_ref, bf16[768,1152]{1,0:T(8,128)(2,1)} %act.1.ad_ref.mine_ref, bf16[768,1152]{1,0:T(8,128)(2,1)} %collective-permute-done.19.ad_ref.theirs_ref, ...), custom_call_target="tpu_custom_call" | custom-call | flops 7247757 | bytes 24000 | tf_op jit(solution)/shard_map/weights/pallas_call | solution.py:424
  171.0 16.1 %collective-permute-done.20 = bf16[768,512]{1,0:T(8,128)(2,1)S(1)} collective-permute-done((bf16[768,512]{1,0:T(8,128)(2,1)S(1)}, bf16[768,512]{1,0:T(8,128)(2,1)S(1)}, u32[]{:S(2)}, u32[]{:S(2)}) %collective-permute-start.20) | collective-permute-done | bytes 786464 | tf_op jit(solution)/shard_map/ppermute | solution.py:414
  189.1 6.1 %all-to-all-start.1 = ((bf16[16,48,512]{2,1,0:T(8,128)(2,1)}), bf16[16,48,512]{2,1,0:T(8,128)(2,1)S(1)}, u32[]{:S(2)}, u32[]{:S(2)}) async-start(bf16[16,48,512]{2,1,0:T(8,128)(2,1)} %bitcast.39), calls=%async_computation.1 | async-start | bytes 1572864 | tf_op jit(solution)/shard_map/all_to_all | solution.py:447
  200.8 5.0 %settle.1 = (bf16[2,192,4096]{2,1,0:T(8,128)(2,1)}, bf16[2,192,4096]{2,1,0:T(8,128)(2,1)}, bf16[2,192,4096]{2,1,0:T(8,128)(2,1)}) custom-call(s32[1]{0:T(128)} %bitcast.c_ref.e_ref, bf16[2,3,192,2048]{3,2,1,0:T(8,128)(2,1)} %collective-permute-done.26.in_ref, ...), custom_call_target="tpu_custom_call", output_to_operand_aliasing={{0}: (2, {}), {1}: (3, {}), {2}: (4, {})} | custom-call | bytes 9400 | tf_op jit(solution)/shard_map/settle/pallas_call | solution.py:449
  (129 shorter events, 76.1 us)
Async XLA Ops:
  4.2 14.3 %collective-permute-start.1 = (bf16[128,3200]{1,0:T(8,128)(2,1)}, bf16[128,3200]{1,0:T(8,128)(2,1)S(1)}, u32[]{:S(2)}, u32[]{:S(2)}) collective-permute-start(bf16[128,3200]{1,0:T(8,128)(2,1)} %pack.1.pw_ref), channel_id=1, source_target_pairs={{0,96},{1,25},{2,98},{3,27},{4,100},{5,29},{6,102},{7,31},{8,104},... | collective-permute-start | bytes 2457608 | tf_op jit(solution)/shard_map/ppermute | solution.py:57
  8.3 13.8 %collective-permute-start = (bf16[128,3200]{1,0:T(8,128)(2,1)}, bf16[128,3200]{1,0:T(8,128)(2,1)S(1)}, u32[]{:S(2)}, u32[]{:S(2)}) collective-permute-start(bf16[128,3200]{1,0:T(8,128)(2,1)} %pack.1.pw_ref), channel_id=1, source_target_pairs={{0,32},{1,9},{2,34},{3,11},{4,36},{5,13},{6,38},{7,15},{8,40},{9,1... | collective-permute-start | bytes 2457608 | tf_op jit(solution)/shard_map/ppermute | solution.py:57
  22.1 10.8 %collective-permute-start.4 = (bf16[6,192,2048]{2,1,0:T(8,128)(2,1)}, bf16[6,192,2048]{2,1,0:T(8,128)(2,1)S(1)}, u32[]{:S(2)}, u32[]{:S(2)}) collective-permute-start(bf16[6,192,2048]{2,1,0:T(8,128)(2,1)} %outgoing.1), channel_id=1, source_target_pairs={{0,1},{1,0},{2,3},{3,2},{4,5},{5,4},{6,7},{7,6},{8,9},{9,8},{10,11... | collective-permute-start | bytes 14155784 | tf_op jit(solution)/shard_map/ppermute | solution.py:36
  23.7 9.2 %collective-permute-start.2 = (bf16[64,3200]{1,0:T(8,128)(2,1)S(1)}, bf16[64,3200]{1,0:T(8,128)(2,1)S(1)}, u32[]{:S(2)}, u32[]{:S(2)}) collective-permute-start(bf16[64,3200]{1,0:T(8,128)(2,1)S(1)} %slice.69), channel_id=1, source_target_pairs={{0,32},{1,9},{2,34},{3,11},{4,36},{5,13},{6,38},{7,15},{8,40},{9,1... | collective-permute-start | bytes 1228808 | tf_op jit(solution)/shard_map/ppermute | solution.py:57
  33.2 17.5 %collective-permute-start.7 = (bf16[4,128,1152]{2,1,0:T(8,128)(2,1)S(1)}, bf16[4,128,1152]{2,1,0:T(8,128)(2,1)S(1)}, u32[]{:S(2)}, u32[]{:S(2)}) collective-permute-start(bf16[4,128,1152]{2,1,0:T(8,128)(2,1)S(1)} %pad_maximum_fusion.1.near_ref), channel_id=1, source_target_pairs={{0,2},{1,7},{2,4},{3,1},{4,6},{5,3},{6,0},{7,5},{8,10},{9,15},{10,... | collective-permute-start | bytes 3538952 | tf_op jit(solution)/shard_map/ppermute | solution.py:57
  34.7 16.9 %collective-permute-start.6 = (bf16[4,128,1152]{2,1,0:T(8,128)(2,1)S(1)}, bf16[4,128,1152]{2,1,0:T(8,128)(2,1)S(1)}, u32[]{:S(2)}, u32[]{:S(2)}) collective-permute-start(bf16[4,128,1152]{2,1,0:T(8,128)(2,1)S(1)} %pad_maximum_fusion.1.near_ref), channel_id=1, source_target_pairs={{0,24},{1,97},{2,26},{3,99},{4,28},{5,101},{6,30},{7,103},{8,0},{9... | collective-permute-start | bytes 3538952 | tf_op jit(solution)/shard_map/ppermute | solution.py:57
  36.4 17.5 %collective-permute-start.5 = (bf16[4,128,1152]{2,1,0:T(8,128)(2,1)S(1)}, bf16[4,128,1152]{2,1,0:T(8,128)(2,1)}, u32[]{:S(2)}, u32[]{:S(2)}) collective-permute-start(bf16[4,128,1152]{2,1,0:T(8,128)(2,1)S(1)} %pad_maximum_fusion.1.near_ref), channel_id=1, source_target_pairs={{0,8},{1,33},{2,10},{3,35},{4,12},{5,37},{6,14},{7,39},{8,16},{9,4... | collective-permute-start | bytes 3538952 | tf_op jit(solution)/shard_map/ppermute | solution.py:57
  54.0 17.7 %collective-permute-start.12 = (bf16[4,128,1152]{2,1,0:T(8,128)(2,1)}, bf16[4,128,1152]{2,1,0:T(8,128)(2,1)}, u32[]{:S(2)}, u32[]{:S(2)}) collective-permute-start(bf16[4,128,1152]{2,1,0:T(8,128)(2,1)} %collective-permute-done.5.near_ref), channel_id=1, source_target_pairs={{0,2},{1,7},{2,4},{3,1},{4,6},{5,3},{6,0},{7,5},{8,10},{9,15},{10,... | collective-permute-start | bytes 3538952 | tf_op jit(solution)/shard_map/ppermute | solution.py:57
  55.5 33.8 %collective-permute-start.9 = (bf16[4,128,2048]{2,1,0:T(8,128)(2,1)}, bf16[4,128,2048]{2,1,0:T(8,128)(2,1)}, u32[]{:S(2)}, u32[]{:S(2)}) collective-permute-start(bf16[4,128,2048]{2,1,0:T(8,128)(2,1)} %pad_maximum_fusion.g_ref), channel_id=1, source_target_pairs={{0,24},{1,97},{2,26},{3,99},{4,28},{5,101},{6,30},{7,103},{8,0},{9... | collective-permute-start | bytes 6291464 | tf_op jit(solution)/shard_map/ppermute | solution.py:57
  55.5 33.8 %collective-permute-start.8 = (bf16[4,128,2048]{2,1,0:T(8,128)(2,1)}, bf16[4,128,2048]{2,1,0:T(8,128)(2,1)}, u32[]{:S(2)}, u32[]{:S(2)}) collective-permute-start(bf16[4,128,2048]{2,1,0:T(8,128)(2,1)} %pad_maximum_fusion.g_ref), channel_id=1, source_target_pairs={{0,8},{1,33},{2,10},{3,35},{4,12},{5,37},{6,14},{7,39},{8,16},{9,4... | collective-permute-start | bytes 6291464 | tf_op jit(solution)/shard_map/ppermute | solution.py:57
  71.7 17.5 %collective-permute-start.13 = (bf16[4,128,1152]{2,1,0:T(8,128)(2,1)S(1)}, bf16[4,128,1152]{2,1,0:T(8,128)(2,1)S(1)}, u32[]{:S(2)}, u32[]{:S(2)}) collective-permute-start(bf16[4,128,1152]{2,1,0:T(8,128)(2,1)S(1)} %collective-permute-done.6.near_ref), channel_id=1, source_target_pairs={{0,2},{1,7},{2,4},{3,1},{4,6},{5,3},{6,0},{7,5},{8,10},{9,15},{10,... | collective-permute-start | bytes 3538952 | tf_op jit(solution)/shard_map/ppermute | solution.py:57
  73.1 14.9 %collective-permute-start.11 = (bf16[2,128,1152]{2,1,0:T(8,128)(2,1)S(1)}, bf16[2,128,1152]{2,1,0:T(8,128)(2,1)S(1)}, u32[]{:S(2)}, u32[]{:S(2)}) collective-permute-start(bf16[2,128,1152]{2,1,0:T(8,128)(2,1)S(1)} %slice.77), channel_id=1, source_target_pairs={{0,24},{1,97},{2,26},{3,99},{4,28},{5,101},{6,30},{7,103},{8,0},{9... | collective-permute-start | bytes 1769480 | tf_op jit(solution)/shard_map/ppermute | solution.py:57
  73.2 16.0 %collective-permute-start.10 = (bf16[2,128,1152]{2,1,0:T(8,128)(2,1)S(1)}, bf16[2,128,1152]{2,1,0:T(8,128)(2,1)S(1)}, u32[]{:S(2)}, u32[]{:S(2)}) collective-permute-start(bf16[2,128,1152]{2,1,0:T(8,128)(2,1)S(1)} %slice.76), channel_id=1, source_target_pairs={{0,8},{1,33},{2,10},{3,35},{4,12},{5,37},{6,14},{7,39},{8,16},{9,4... | collective-permute-start | bytes 1769480 | tf_op jit(solution)/shard_map/ppermute | solution.py:57
  89.4 17.5 %collective-permute-start.16 = (bf16[4,128,1152]{2,1,0:T(8,128)(2,1)S(1)}, bf16[4,128,1152]{2,1,0:T(8,128)(2,1)S(1)}, u32[]{:S(2)}, u32[]{:S(2)}) collective-permute-start(bf16[4,128,1152]{2,1,0:T(8,128)(2,1)S(1)} %constant_dynamic-update-slice_fusion.2.near_ref), channel_id=1, source_target_pairs={{0,2},{1,7},{2,4},{3,1},{4,6},{5,3},{6,0},{7,5},{8,10},{9,15},{10,... | collective-permute-start | bytes 3538952 | tf_op jit(solution)/shard_map/ppermute | solution.py:57
  93.3 21.8 %collective-permute-start.15 = (bf16[2,128,2048]{2,1,0:T(8,128)(2,1)S(1)}, bf16[2,128,2048]{2,1,0:T(8,128)(2,1)S(1)}, u32[]{:S(2)}, u32[]{:S(2)}) collective-permute-start(bf16[2,128,2048]{2,1,0:T(8,128)(2,1)S(1)} %slice.79), channel_id=1, source_target_pairs={{0,24},{1,97},{2,26},{3,99},{4,28},{5,101},{6,30},{7,103},{8,0},{9... | collective-permute-start | bytes 3145736 | tf_op jit(solution)/shard_map/ppermute | solution.py:57
  93.4 21.7 %collective-permute-start.14 = (bf16[2,128,2048]{2,1,0:T(8,128)(2,1)S(1)}, bf16[2,128,2048]{2,1,0:T(8,128)(2,1)S(1)}, u32[]{:S(2)}, u32[]{:S(2)}) collective-permute-start(bf16[2,128,2048]{2,1,0:T(8,128)(2,1)S(1)} %slice.78), channel_id=1, source_target_pairs={{0,8},{1,33},{2,10},{3,35},{4,12},{5,37},{6,14},{7,39},{8,16},{9,4... | collective-permute-start | bytes 3145736 | tf_op jit(solution)/shard_map/ppermute | solution.py:57
  115.1 9.8 %collective-permute-start.17 = (f32[768,768]{1,0:T(8,128)S(1)}, f32[768,768]{1,0:T(8,128)S(1)}, u32[]{:S(2)}, u32[]{:S(2)}) collective-permute-start(f32[768,768]{1,0:T(8,128)S(1)} %hidden.4), channel_id=1, source_target_pairs={{0,1},{1,0},{2,3},{3,2},{4,5},{5,4},{6,7},{7,6},{8,9},{9,8},{10,11... | collective-permute-start | bytes 7077896 | tf_op jit(solution)/shard_map/ppermute | solution.py:36
  127.1 12.1 %collective-permute-start.19 = (bf16[768,1152]{1,0:T(8,128)(2,1)}, bf16[768,1152]{1,0:T(8,128)(2,1)}, u32[]{:S(2)}, u32[]{:S(2)}) collective-permute-start(bf16[768,1152]{1,0:T(8,128)(2,1)} %act.1.ad_ref.mine_ref), channel_id=1, source_target_pairs={{0,1},{1,0},{2,3},{3,2},{4,5},{5,4},{6,7},{7,6},{8,9},{9,8},{10,11... | collective-permute-start | bytes 5308424 | tf_op jit(solution)/shard_map/ppermute | solution.py:36
  134.5 54.6 %all-to-all-start = ((bf16[16,48,2048]{2,1,0:T(8,128)(2,1)}), bf16[16,48,2048]{2,1,0:T(8,128)(2,1)}, u32[]{:S(2)}, u32[]{:S(2)}) async-start(bf16[16,48,2048]{2,1,0:T(8,128)(2,1)} %copy-done.5), calls=%async_computation | async-start | bytes 6291456 | tf_op jit(solution)/shard_map/all_to_all | solution.py:417
  148.4 20.4 %collective-permute-start.22 = (bf16[768,512]{1,0:T(8,128)(2,1)S(1)}, bf16[768,512]{1,0:T(8,128)(2,1)S(1)}, u32[]{:S(2)}, u32[]{:S(2)}) collective-permute-start(bf16[768,512]{1,0:T(8,128)(2,1)S(1)} %get-tuple-element.122), channel_id=1, source_target_pairs={{0,6},{2,0},{4,2},{6,4},{1,7},{3,1},{5,3},{7,5},{8,14},{10,8},{12,... | collective-permute-start | bytes 2359304 | tf_op jit(solution)/shard_map/ppermute | solution.py:414
  149.1 21.9 %collective-permute-start.21 = (bf16[768,512]{1,0:T(8,128)(2,1)S(1)}, bf16[768,512]{1,0:T(8,128)(2,1)S(1)}, u32[]{:S(2)}, u32[]{:S(2)}) collective-permute-start(bf16[768,512]{1,0:T(8,128)(2,1)S(1)} %get-tuple-element.123), channel_id=1, source_target_pairs={{0,4},{2,6},{4,0},{6,2},{1,5},{3,7},{5,1},{7,3},{8,12},{10,14},{12... | collective-permute-start | bytes 2359304 | tf_op jit(solution)/shard_map/ppermute | solution.py:414
  150.6 36.5 %collective-permute-start.20 = (bf16[768,512]{1,0:T(8,128)(2,1)S(1)}, bf16[768,512]{1,0:T(8,128)(2,1)S(1)}, u32[]{:S(2)}, u32[]{:S(2)}) collective-permute-start(bf16[768,512]{1,0:T(8,128)(2,1)S(1)} %get-tuple-element.124), channel_id=1, source_target_pairs={{0,2},{2,4},{4,6},{6,0},{1,3},{3,5},{5,7},{7,1},{8,10},{10,12},{12... | collective-permute-start | bytes 2359304 | tf_op jit(solution)/shard_map/ppermute | solution.py:414
  189.1 11.7 %collective-permute-start.26 = (bf16[2,3,192,2048]{3,2,1,0:T(8,128)(2,1)}, bf16[2,3,192,2048]{3,2,1,0:T(8,128)(2,1)}, u32[]{:S(2)}, u32[]{:S(2)}) collective-permute-start(bf16[2,3,192,2048]{3,2,1,0:T(8,128)(2,1)} %copy-done.13), channel_id=1, source_target_pairs={{0,1},{1,0},{2,3},{3,2},{4,5},{5,4},{6,7},{7,6},{8,9},{9,8},{10,11... | collective-permute-start | bytes 14155784 | tf_op jit(solution)/shard_map/ppermute | solution.py:36
  189.1 21.1 %all-to-all-start.1 = ((bf16[16,48,512]{2,1,0:T(8,128)(2,1)}), bf16[16,48,512]{2,1,0:T(8,128)(2,1)S(1)}, u32[]{:S(2)}, u32[]{:S(2)}) async-start(bf16[16,48,512]{2,1,0:T(8,128)(2,1)} %bitcast.39), calls=%async_computation.1 | async-start | bytes 1572864 | tf_op jit(solution)/shard_map/all_to_all | solution.py:447
  (27 other events, 174.1 us)

commit v6 on v5

--- a/solution.py
+++ b/solution.py
@@ -163,24 +163,42 @@
     out_ref[...] = nt(v_ref[0], w_ref[0])
 
 
-def act_kernel(a_ref, b_ref, d_ref, e_ref, out_ref):
+def act_kernel(e_ref, v_ref, w_ref, d_ref, g0_ref, g1_ref, u0_ref, u1_ref, out_ref):
     n = out_ref.shape[1] // 3
-    h = a_ref[...] + b_ref[...]
-    gate, up = h[:, 0:n], h[:, n:]
-    d = d_ref[...] + e_ref[...]
+    d = nt(v_ref[0], w_ref[0]) + d_ref[...]
+    gate, up = g0_ref[...] + g1_ref[...], u0_ref[...] + u1_ref[...]
     sig = jax.nn.sigmoid(gate)
     silu = gate * sig
-    out_ref[:, 0:n] = (d * up * sig * (1.0 + gate * (1.0 - sig))).astype(BF)
-    out_ref[:, n : 2 * n] = (d * silu).astype(BF)
-    out_ref[:, 2 * n :] = (silu * up).astype(BF)
+    outs = (d * up * sig * (1.0 + gate * (1.0 - sig)), d * silu, silu * up)
+    for i, value in enumerate(outs):
+        at = pl.multiple_of(i * n + pl.program_id(0) * 128, 128)
+        out_ref[:, pl.ds(at, 128)] = value.astype(BF)
 
 
 def by_x_kernel(e_ref, ad_ref, wgu_ref, out_ref):
     out_ref[0] = mm(ad_ref[:, 0 : wgu_ref.shape[1]], wgu_ref[0]).astype(BF)
 
 
-def by_block_kernel(e_ref, ad_ref, wgu_ref, out_ref):
-    out_ref[...] = mm(ad_ref[:, 0 : wgu_ref.shape[1]], wgu_ref[0]).astype(BF).reshape(out_ref.shape)
+def by_block_kernel(e_ref, ad_ref, wgu_ref, out_ref, stage, sems):
+    step = pl.program_id(0)
+    turn = lax.rem(step, 2)
+
+    def leaving(j, slot):
+        cols = pl.ds(pl.multiple_of(j * 512, 512), 512)
+        return pltpu.make_async_copy(stage.at[slot], out_ref.at[:, :, cols], sems.at[slot])
+
+    @pl.when(step >= 2)
+    def _():
+        leaving(step - 2, turn).wait()
+
+    got = mm(ad_ref[:, 0 : wgu_ref.shape[1]], wgu_ref[0]).astype(BF)
+    stage[turn] = got.reshape(stage.shape[1:])
+    leaving(step, turn).start()
+
+    @pl.when(step == 3)
+    def _():
+        leaving(2, 0).wait()
+        leaving(3, 1).wait()
 
 
 def weight_kernel(c_ref, mine_ref, theirs_ref, xs_ref, gs_ref, gg_ref, gu_ref, gd_ref, send_ref, dt):
@@ -373,39 +391,53 @@
             name="hidden",
         )(which, v, w)
 
-    pre_out, pre = hidden(others, xs, wgu, 256), hidden(cs, xs, wgu, 256)
-    gd0, gd1, gs, pre_out, pre = together(gd0, gd1, gs, pre_out, pre)
+    pre_out = hidden(others, xs, wgu, 256)
+    gd0, gd1, gs, pre_out = together(gd0, gd1, gs, pre_out)
     pre_in = swap(pre_out)
     gs = select(select_g_kernel, 12, xd, gd0, [gs])
     gs = select(select_g_kernel, 14, xd, gd1, [gs], 2)
-    dh_in = swap(hidden(others, gs, wd, 128))
-    dh = hidden(cs, gs, wd, 128)
-    quarter = lambda n: pl.BlockSpec((slots // 4, n), lambda j: (j, 0))
+    dh_out = hidden(others, gs, wd, 128)
+    xs, dh_out = together(xs, dh_out)
+    dh_in = swap(dh_out)
+    pre = hidden(cs, xs, wgu, 256)
+    column = lambda k: pl.BlockSpec((slots, 128), lambda j, er: (0, k + j))
     mine = pl.pallas_call(
         act_kernel,
-        grid=(4,),
+        grid_spec=prefetched(
+            (3,),
+            [
+                pl.BlockSpec((1, slots, half), lambda j, er: (er[0], 0, 0)),
+                pl.BlockSpec((1, 128, half), lambda j, er: (er[0], j, 0)),
+                column(0),
+                column(0),
+                column(0),
+                column(3),
+                column(3),
+            ],
+            pl.BlockSpec((slots, 6 * f), lambda j, er: (0, 0)),
+        ),
         out_shape=like((slots, 6 * f)),
-        in_specs=[quarter(4 * f), quarter(4 * f), quarter(2 * f), quarter(2 * f)],
-        out_specs=quarter(6 * f),
         compiler_params=params(24),
-        cost_estimate=cost(1e7, 9e6),
+        cost_estimate=cost(2 * slots * half * 2 * f, 9e6),
         name="act",
-    )(pre, pre_in, dh, dh_in)
+    )(cs, gs, wd, dh_in, pre, pre_in, pre, pre_in)
     theirs = swap(mine)
 
     def partial(kernel, which, ad):
+        scratch = []
         if kernel is by_x_kernel:
-            shape = (4, slots, 512)
+            shape = like((4, slots, 512))
             out = pl.BlockSpec((1, slots, 512), lambda j, er: (lax.rem(j - er[1] + 4, 4), 0, 0))
         else:
-            shape = (16, CAP, half)
-            out = pl.BlockSpec((16, CAP, 512), lambda j, er: (0, 0, j))
+            shape = pltpu.HBM((16, CAP, half), BF)
+            out = pl.BlockSpec(memory_space=pltpu.HBM)
+            scratch = [pltpu.VMEM((2, 16, CAP, 512), BF), pltpu.SemaphoreType.DMA((2,))]
         return pl.pallas_call(
             kernel,
             grid_spec=prefetched(
-                (4,), [VMEM, pl.BlockSpec((1, 4 * f, 512), lambda j, er: (er[0], 0, j))], out
+                (4,), [VMEM, pl.BlockSpec((1, 4 * f, 512), lambda j, er: (er[0], 0, j))], out, scratch
             ),
-            out_shape=like(shape),
+            out_shape=shape,
             compiler_params=params(24),
             cost_estimate=cost(2 * slots * half * 4 * f, 8e6),
             name="partial",
@@ -436,7 +468,7 @@
             [pltpu.VMEM((6 * f, slots), BF)],
         ),
         out_shape=[like((2, f, width))] * 3 + [like((2, 3, f, half))],
-        compiler_params=params(24),
+        compiler_params=params(58),
         cost_estimate=cost(4 * slots * half * 6 * f, 24e6),
         name="weights",
     )(cs, mine, theirs, xs, gs)

time: 213 us -> 209 us (0.981)
  starting transfers between devices: 35.6 us -> 45.3 us
  waiting for transfers between devices: 71.4 us -> 61.8 us
  local copies, waits for them, and re-layouts: 18.1 us -> 15 us
  Pallas kernels: 82 us -> 79.8 us
    ppermute x16, waiting for transfers between devices: 46.3 us -> 39.3 us  [hop(): return lax.ppermute(v, ('z', 'y', 'x', 'c'), to)]
    ppermute x16, starting transfers between devices: 19 us -> 23.1 us  [hop(): return lax.ppermute(v, ('z', 'y', 'x', 'c'), to)]
    unnamed x46 -> x38, local copies, waits for them, and re-layouts: 11.8 us -> 7.79 us
    ppermute x6, starting transfers between devices: 5.11 us -> 8.39 us  [shards(): lax.ppermute(v, 'x', [(i, (i + k) % 4) for i in range(4)])]
    pallas_call x4 -> x3, Pallas kernels: 12.4 us -> 9.38 us  [hidden(): pl.pallas_call(hidden_kernel, grid_spec=prefetched((n // chunk,), [pl.Blo...]
  transfers between devices with their start and end apart: 29 -> 29, of which waited for: 17 -> 15; matrix products, arithmetic and copies ran while one was open for 4% -> 5% of each run, Pallas kernels for 36% -> 34%
where the time goes in v6:
time: 209 us; the launch traced here: 208 us
  Pallas kernels  79.8 us (38%)
  waiting for transfers between devices  61.8 us (30%)
  starting transfers between devices  45.3 us (22%)
  local copies, waits for them, and re-layouts  15 us (7%)
  other arithmetic  5.02 us (2%)
    ppermute x16, waiting for transfers between devices, hop(): return lax.ppermute(v, ('z', 'y', 'x', 'c'), to)  39.3 us
    ppermute x16, starting transfers between devices, hop(): return lax.ppermute(v, ('z', 'y', 'x', 'c'), to)  23.1 us
    pallas_call x9, Pallas kernels, select(): pl.pallas_call(kernel, grid_spec=prefetched((n,), specs + [pl.BlockSpec(m...  22.1 us
    ppermute x6, waiting for transfers between devices, shards(): lax.ppermute(v, 'x', [(i, (i + k) % 4) for i in range(4)])  20.6 us
    pallas_call x1, Pallas kernels, shards(): pl.pallas_call(weight_kernel, grid_spec=prefetched((2, 4), [VMEM, VMEM, p...  14.9 us
    pallas_call x2, Pallas kernels, partial(): pl.pallas_call(kernel, grid_spec=prefetched((4,), [VMEM, pl.BlockSpec((1,...  10.3 us
    pallas_call x3, Pallas kernels, hidden(): pl.pallas_call(hidden_kernel, grid_spec=prefetched((n // chunk,), [pl.Blo...  9.38 us
    ppermute x6, starting transfers between devices, shards(): lax.ppermute(v, 'x', [(i, (i + k) % 4) for i in range(4)])  8.39 us
  transfers between devices with their start and end apart: 29, of which 15 were waited for; matrix products, arithmetic and copies ran while one was open for 5% of the time, Pallas kernels for 34%

profile of v6, /device:TPU:0, one launch (start us, length us, event | category | flops | bytes accessed | tf_op | source)
XLA Modules:
  0.0 208.0 jit_solution(13558290738271708928)
XLA Ops:
  1.3 2.9 %pack.1.pw_ref = bf16[128,3200]{1,0:T(8,128)(2,1)} custom-call(s32[6]{0:T(128)} %stack.111.at_ref, s32[8,128]{1,0:T(8,128)} %bitcast.63, f32[8,128]{1,0:T(8,128)} %bitcast.64, bf16[128,4096]{1,0:T(8,128)(2,1)} %t1.1, bf16[128,4096]{1,0:T(8,128)(2,1)} %t1.1, bf16[128,4096]{1,0:T(8,128)(2,1)} %g3.1, bf16[128,4096]{1,0:T(8,128)(2,1)} %g3.1, ...), custom_call_target="tpu_custom_call" | custom-call | flops 10000 | bytes 2000 | tf_op jit(solution)/shard_map/pack/pallas_call | solution.py:272
  8.4 5.0 %outgoing.1 = bf16[6,192,2048]{2,1,0:T(8,128)(2,1)} custom-call(s32[1]{0:T(128)} %bitcast.c_ref.e_ref, bf16[2,192,4096]{2,1,0:T(8,128)(2,1)} %g_ref.3, bf16[2,192,4096]{2,1,0:T(8,128)(2,1)} %u_ref.3, bf16[2,192,4096]{2,1,0:T(8,128)(2,1)} %d_ref.3), custom_call_target="tpu_custom_call" | custom-call | bytes 9400 | tf_op jit(solution)/shard_map/outgoing/pallas_call | solution.py:288
  13.5 5.5 %collective-permute-done = bf16[128,3200]{1,0:T(8,128)(2,1)S(1)} collective-permute-done((bf16[128,3200]{1,0:T(8,128)(2,1)}, bf16[128,3200]{1,0:T(8,128)(2,1)S(1)}, u32[]{:S(2)}, u32[]{:S(2)}) %collective-permute-start) | collective-permute-done | bytes 819232 | tf_op jit(solution)/shard_map/ppermute | solution.py:57
  22.6 5.8 %collective-permute-done.2 = bf16[64,3200]{1,0:T(8,128)(2,1)S(1)} collective-permute-done((bf16[64,3200]{1,0:T(8,128)(2,1)S(1)}, bf16[64,3200]{1,0:T(8,128)(2,1)S(1)}, u32[]{:S(2)}, u32[]{:S(2)}) %collective-permute-start.2) | collective-permute-done | bytes 409632 | tf_op jit(solution)/shard_map/ppermute | solution.py:57
  42.7 4.3 %collective-permute-done.5.near_ref = bf16[4,128,1152]{2,1,0:T(8,128)(2,1)} collective-permute-done((bf16[4,128,1152]{2,1,0:T(8,128)(2,1)S(1)}, bf16[4,128,1152]{2,1,0:T(8,128)(2,1)}, u32[]{:S(2)}, u32[]{:S(2)}) %collective-permute-start.5) | collective-permute-done | bytes 1179680 | tf_op jit(solution)/shard_map/ppermute | solution.py:57
  54.7 3.6 %select.76.rest_0_ = bf16[2,768,2048]{2,1,0:T(8,128)(2,1)S(1)} custom-call(s32[18]{0:T(128)S(1)} %stack.130.info_ref, bf16[4,128,1152]{2,1,0:T(8,128)(2,1)S(1)} %pad_maximum_fusion.1.near_ref, bf16[4,128,2048]{2,1,0:T(8,128)(2,1)} %pad_maximum_fusion.g_ref), custom_call_target="tpu_custom_call" | custom-call | flops 201326 | bytes 5600 | tf_op jit(solution)/shard_map/select/pallas_call | solution.py:348
  60.1 8.7 %collective-permute-done.12.far_ref = bf16[4,128,1152]{2,1,0:T(8,128)(2,1)} collective-permute-done((bf16[4,128,1152]{2,1,0:T(8,128)(2,1)}, bf16[4,128,1152]{2,1,0:T(8,128)(2,1)}, u32[]{:S(2)}, u32[]{:S(2)}) %collective-permute-start.12) | collective-permute-done | bytes 1179680 | tf_op jit(solution)/shard_map/ppermute | solution.py:57
  73.3 3.6 %select.77.rest_0_ = bf16[2,768,2048]{2,1,0:T(8,128)(2,1)S(1)} custom-call(s32[18]{0:T(128)S(1)} %stack.130.info_ref, bf16[4,128,1152]{2,1,0:T(8,128)(2,1)} %collective-permute-done.5.near_ref, bf16[4,128,1152]{2,1,0:T(8,128)(2,1)} %collective-permute-done.12.far_ref, bf16[2,768,2048]{2,1,0:T(8,128)(2,1)S(1)} %select.75.rest_0_), custom_call_target="tpu_custom_call", output_to_operand_aliasing={{}: (3, {})} | custom-call | flops 201326 | bytes 5600 | tf_op jit(solution)/shard_map/select/pallas_call | solution.py:348
  76.9 8.2 %collective-permute-done.10 = bf16[2,128,1152]{2,1,0:T(8,128)(2,1)S(1)} collective-permute-done((bf16[2,128,1152]{2,1,0:T(8,128)(2,1)S(1)}, bf16[2,128,1152]{2,1,0:T(8,128)(2,1)S(1)}, u32[]{:S(2)}, u32[]{:S(2)}) %collective-permute-start.10) | collective-permute-done | bytes 589856 | tf_op jit(solution)/shard_map/ppermute | solution.py:57
  92.9 3.6 %select.78.rest_0_ = bf16[2,768,2048]{2,1,0:T(8,128)(2,1)S(1)} custom-call(s32[18]{0:T(128)S(1)} %stack.130.info_ref, bf16[4,128,1152]{2,1,0:T(8,128)(2,1)} %collective-permute-done.5.near_ref, bf16[4,128,2048]{2,1,0:T(8,128)(2,1)} %collective-permute-done.8.g_ref, bf16[2,768,2048]{2,1,0:T(8,128)(2,1)S(1)} %select.76.rest_0_), custom_call_target="tpu_custom_call", output_to_operand_aliasing={{}: (3, {})} | custom-call | flops 201326 | bytes 5600 | tf_op jit(solution)/shard_map/select/pallas_call | solution.py:348
  96.5 3.6 %select.79.rest_0_ = bf16[2,768,2048]{2,1,0:T(8,128)(2,1)S(1)} custom-call(s32[18]{0:T(128)S(1)} %stack.130.info_ref, bf16[4,128,1152]{2,1,0:T(8,128)(2,1)S(1)} %copy-done.12, bf16[4,128,2048]{2,1,0:T(8,128)(2,1)} %collective-permute-done.9.g_ref, bf16[2,768,2048]{2,1,0:T(8,128)(2,1)S(1)} %select.78.rest_0_), custom_call_target="tpu_custom_call", output_to_operand_aliasing={{}: (3, {})} | custom-call | flops 201326 | bytes 5600 | tf_op jit(solution)/shard_map/select/pallas_call | solution.py:348
  105.6 3.2 %hidden.3 = f32[768,768]{1,0:T(8,128)S(1)} custom-call(s32[1]{0:T(128)S(6)} %sub.3.e_ref, bf16[2,768,2048]{2,1,0:T(8,128)(2,1)S(1)} %select.81.v_ref.xs_ref, bf16[2,768,2048]{2,1,0:T(8,128)(2,1)S(1)} %bitcast.62), custom_call_target="tpu_custom_call" | custom-call | flops 2415919 | bytes 9000 | tf_op jit(solution)/shard_map/hidden/pallas_call | solution.py:378
  112.2 3.0 %hidden.4 = f32[768,384]{1,0:T(8,128)S(1)} custom-call(s32[1]{0:T(128)S(6)} %sub.3.e_ref, bf16[2,768,2048]{2,1,0:T(8,128)(2,1)S(1)} %select.83.v_ref.gs_ref, bf16[2,384,2048]{2,1,0:T(8,128)(2,1)S(1)} %copy-done.7), custom_call_target="tpu_custom_call" | custom-call | flops 1207959 | bytes 9000 | tf_op jit(solution)/shard_map/hidden/pallas_call | solution.py:378
  115.8 3.2 %hidden.5.g0_ref.u0_ref = f32[768,768]{1,0:T(8,128)S(1)} custom-call(s32[1]{0:T(128)} %bitcast.c_ref.e_ref, bf16[2,768,2048]{2,1,0:T(8,128)(2,1)S(1)} %select.81.v_ref.xs_ref, bf16[2,768,2048]{2,1,0:T(8,128)(2,1)S(1)} %bitcast.62), custom_call_target="tpu_custom_call" | custom-call | flops 2415919 | bytes 9000 | tf_op jit(solution)/shard_map/hidden/pallas_call | solution.py:378
  119.0 3.7 %act.1.ad_ref.mine_ref = bf16[768,1152]{1,0:T(8,128)(2,1)S(1)} custom-call(s32[1]{0:T(128)} %bitcast.c_ref.e_ref, bf16[2,768,2048]{2,1,0:T(8,128)(2,1)S(1)} %select.83.v_ref.gs_ref, bf16[2,384,2048]{2,1,0:T(8,128)(2,1)S(1)} %copy-done.7, f32[768,384]{1,0:T(8,128)S(1)} %collective-permute-done.17.d_ref, f32[768,768]{1,0:T(8,128)S(1)} %hidden.5.g0_ref.u0_ref, ...), custom_call_target="tpu_custom_call" | custom-call | flops 1207959 | bytes 9000 | tf_op jit(solution)/shard_map/act/pallas_call | solution.py:404
  123.0 5.0 %partial.2 = bf16[16,48,2048]{2,1,0:T(8,128)(2,1)} custom-call(s32[2]{0:T(128)S(1)} %pad_add_fusion.e_ref.c_ref, bf16[768,1152]{1,0:T(8,128)(2,1)S(1)} %act.1.ad_ref.mine_ref, bf16[2,768,2048]{2,1,0:T(8,128)(2,1)S(1)} %bitcast.62), custom_call_target="tpu_custom_call" | custom-call | flops 2415919 | bytes 8000 | tf_op jit(solution)/shard_map/partial/pallas_call | solution.py:435
  127.9 6.0 %all-to-all-start = ((bf16[16,48,2048]{2,1,0:T(8,128)(2,1)}), bf16[16,48,2048]{2,1,0:T(8,128)(2,1)}, u32[]{:S(2)}, u32[]{:S(2)}) async-start(bf16[16,48,2048]{2,1,0:T(8,128)(2,1)} %partial.2), calls=%async_computation | async-start | bytes 6291456 | tf_op jit(solution)/shard_map/all_to_all | solution.py:449
  136.8 5.4 %partial.3 = bf16[4,768,512]{2,1,0:T(8,128)(2,1)S(1)} custom-call(s32[2]{0:T(128)S(1)} %pad_add_fusion.1.e_ref, bf16[768,1152]{1,0:T(8,128)(2,1)} %collective-permute-done.19.ad_ref.theirs_ref, bf16[2,768,2048]{2,1,0:T(8,128)(2,1)S(1)} %copy-done.3), custom_call_target="tpu_custom_call" | custom-call | flops 2415919 | bytes 8000 | tf_op jit(solution)/shard_map/partial/pallas_call | solution.py:435
  143.5 2.9 %collective-permute-start.21 = (bf16[768,512]{1,0:T(8,128)(2,1)S(1)}, bf16[768,512]{1,0:T(8,128)(2,1)}, u32[]{:S(2)}, u32[]{:S(2)}) collective-permute-start(bf16[768,512]{1,0:T(8,128)(2,1)S(1)} %get-tuple-element.125), channel_id=1, source_target_pairs={{0,4},{2,6},{4,0},{6,2},{1,5},{3,7},{5,1},{7,3},{8,12},{10,14},{12... | collective-permute-start | bytes 2359304 | tf_op jit(solution)/shard_map/ppermute | solution.py:446
  147.4 14.9 %weights.1 = (bf16[2,192,4096]{2,1,0:T(8,128)(2,1)}, bf16[2,192,4096]{2,1,0:T(8,128)(2,1)}, bf16[2,192,4096]{2,1,0:T(8,128)(2,1)}, bf16[2,3,192,2048]{3,2,1,0:T(8,128)(2,1)}) custom-call(s32[1]{0:T(128)} %bitcast.c_ref.e_ref, bf16[768,1152]{1,0:T(8,128)(2,1)} %copy-done.4, bf16[768,1152]{1,0:T(8,128)(2,1)} %collective-permute-done.19.ad_ref.theirs_ref, ...), custom_call_target="tpu_custom_call" | custom-call | flops 7247757 | bytes 24000 | tf_op jit(solution)/shard_map/weights/pallas_call | solution.py:456
  165.1 16.1 %collective-permute-done.21 = bf16[768,512]{1,0:T(8,128)(2,1)} collective-permute-done((bf16[768,512]{1,0:T(8,128)(2,1)S(1)}, bf16[768,512]{1,0:T(8,128)(2,1)}, u32[]{:S(2)}, u32[]{:S(2)}) %collective-permute-start.21) | collective-permute-done | bytes 786464 | tf_op jit(solution)/shard_map/ppermute | solution.py:446
  184.5 6.9 %all-to-all-start.1 = ((bf16[16,48,512]{2,1,0:T(8,128)(2,1)}), bf16[16,48,512]{2,1,0:T(8,128)(2,1)S(1)}, u32[]{:S(2)}, u32[]{:S(2)}) async-start(bf16[16,48,512]{2,1,0:T(8,128)(2,1)} %bitcast.39), calls=%async_computation.1 | async-start | bytes 1572864 | tf_op jit(solution)/shard_map/all_to_all | solution.py:479
  195.0 3.2 %collective-permute-start.24 = (bf16[128,512]{1,0:T(8,128)(2,1)S(1)}, bf16[128,512]{1,0:T(8,128)(2,1)S(1)}, u32[]{:S(2)}, u32[]{:S(2)}) collective-permute-start(bf16[128,512]{1,0:T(8,128)(2,1)S(1)} %get-tuple-element.128), channel_id=1, source_target_pairs={{0,4},{2,6},{4,0},{6,2},{1,5},{3,7},{5,1},{7,3},{8,12},{10,14},{12... | collective-permute-start | bytes 393224 | tf_op jit(solution)/shard_map/ppermute | solution.py:446
  198.2 5.0 %settle.1 = (bf16[2,192,4096]{2,1,0:T(8,128)(2,1)}, bf16[2,192,4096]{2,1,0:T(8,128)(2,1)}, bf16[2,192,4096]{2,1,0:T(8,128)(2,1)}) custom-call(s32[1]{0:T(128)} %bitcast.c_ref.e_ref, bf16[2,3,192,2048]{3,2,1,0:T(8,128)(2,1)} %collective-permute-done.26.in_ref, ...), custom_call_target="tpu_custom_call", output_to_operand_aliasing={{0}: (2, {}), {1}: (3, {}), {2}: (4, {})} | custom-call | bytes 9400 | tf_op jit(solution)/shard_map/settle/pallas_call | solution.py:481
  (118 shorter events, 73.5 us)
Async XLA Ops:
  4.3 14.7 %collective-permute-start = (bf16[128,3200]{1,0:T(8,128)(2,1)}, bf16[128,3200]{1,0:T(8,128)(2,1)S(1)}, u32[]{:S(2)}, u32[]{:S(2)}) collective-permute-start(bf16[128,3200]{1,0:T(8,128)(2,1)} %pack.1.pw_ref), channel_id=1, source_target_pairs={{0,32},{1,9},{2,34},{3,11},{4,36},{5,13},{6,38},{7,15},{8,40},{9,1... | collective-permute-start | bytes 2457608 | tf_op jit(solution)/shard_map/ppermute | solution.py:57
  6.3 12.7 %collective-permute-start.1 = (bf16[128,3200]{1,0:T(8,128)(2,1)}, bf16[128,3200]{1,0:T(8,128)(2,1)S(1)}, u32[]{:S(2)}, u32[]{:S(2)}) collective-permute-start(bf16[128,3200]{1,0:T(8,128)(2,1)} %pack.1.pw_ref), channel_id=1, source_target_pairs={{0,96},{1,25},{2,98},{3,27},{4,100},{5,29},{6,102},{7,31},{8,104},... | collective-permute-start | bytes 2457608 | tf_op jit(solution)/shard_map/ppermute | solution.py:57
  19.0 10.0 %collective-permute-start.4 = (bf16[6,192,2048]{2,1,0:T(8,128)(2,1)}, bf16[6,192,2048]{2,1,0:T(8,128)(2,1)S(1)}, u32[]{:S(2)}, u32[]{:S(2)}) collective-permute-start(bf16[6,192,2048]{2,1,0:T(8,128)(2,1)} %outgoing.1), channel_id=1, source_target_pairs={{0,1},{1,0},{2,3},{3,2},{4,5},{5,4},{6,7},{7,6},{8,9},{9,8},{10,11... | collective-permute-start | bytes 14155784 | tf_op jit(solution)/shard_map/ppermute | solution.py:36
  29.3 17.6 %collective-permute-start.5 = (bf16[4,128,1152]{2,1,0:T(8,128)(2,1)S(1)}, bf16[4,128,1152]{2,1,0:T(8,128)(2,1)}, u32[]{:S(2)}, u32[]{:S(2)}) collective-permute-start(bf16[4,128,1152]{2,1,0:T(8,128)(2,1)S(1)} %pad_maximum_fusion.1.near_ref), channel_id=1, source_target_pairs={{0,8},{1,33},{2,10},{3,35},{4,12},{5,37},{6,14},{7,39},{8,16},{9,4... | collective-permute-start | bytes 3538952 | tf_op jit(solution)/shard_map/ppermute | solution.py:57
  31.0 16.2 %collective-permute-start.6 = (bf16[4,128,1152]{2,1,0:T(8,128)(2,1)S(1)}, bf16[4,128,1152]{2,1,0:T(8,128)(2,1)S(1)}, u32[]{:S(2)}, u32[]{:S(2)}) collective-permute-start(bf16[4,128,1152]{2,1,0:T(8,128)(2,1)S(1)} %pad_maximum_fusion.1.near_ref), channel_id=1, source_target_pairs={{0,24},{1,97},{2,26},{3,99},{4,28},{5,101},{6,30},{7,103},{8,0},{9... | collective-permute-start | bytes 3538952 | tf_op jit(solution)/shard_map/ppermute | solution.py:57
  32.6 17.4 %collective-permute-start.7 = (bf16[4,128,1152]{2,1,0:T(8,128)(2,1)S(1)}, bf16[4,128,1152]{2,1,0:T(8,128)(2,1)S(1)}, u32[]{:S(2)}, u32[]{:S(2)}) collective-permute-start(bf16[4,128,1152]{2,1,0:T(8,128)(2,1)S(1)} %pad_maximum_fusion.1.near_ref), channel_id=1, source_target_pairs={{0,2},{1,7},{2,4},{3,1},{4,6},{5,3},{6,0},{7,5},{8,10},{9,15},{10,... | collective-permute-start | bytes 3538952 | tf_op jit(solution)/shard_map/ppermute | solution.py:57
  51.0 17.7 %collective-permute-start.12 = (bf16[4,128,1152]{2,1,0:T(8,128)(2,1)}, bf16[4,128,1152]{2,1,0:T(8,128)(2,1)}, u32[]{:S(2)}, u32[]{:S(2)}) collective-permute-start(bf16[4,128,1152]{2,1,0:T(8,128)(2,1)} %collective-permute-done.5.near_ref), channel_id=1, source_target_pairs={{0,2},{1,7},{2,4},{3,1},{4,6},{5,3},{6,0},{7,5},{8,10},{9,15},{10,... | collective-permute-start | bytes 3538952 | tf_op jit(solution)/shard_map/ppermute | solution.py:57
  51.3 33.8 %collective-permute-start.8 = (bf16[4,128,2048]{2,1,0:T(8,128)(2,1)}, bf16[4,128,2048]{2,1,0:T(8,128)(2,1)}, u32[]{:S(2)}, u32[]{:S(2)}) collective-permute-start(bf16[4,128,2048]{2,1,0:T(8,128)(2,1)} %pad_maximum_fusion.g_ref), channel_id=1, source_target_pairs={{0,8},{1,33},{2,10},{3,35},{4,12},{5,37},{6,14},{7,39},{8,16},{9,4... | collective-permute-start | bytes 6291464 | tf_op jit(solution)/shard_map/ppermute | solution.py:57
  52.3 32.9 %collective-permute-start.9 = (bf16[4,128,2048]{2,1,0:T(8,128)(2,1)}, bf16[4,128,2048]{2,1,0:T(8,128)(2,1)}, u32[]{:S(2)}, u32[]{:S(2)}) collective-permute-start(bf16[4,128,2048]{2,1,0:T(8,128)(2,1)} %pad_maximum_fusion.g_ref), channel_id=1, source_target_pairs={{0,24},{1,97},{2,26},{3,99},{4,28},{5,101},{6,30},{7,103},{8,0},{9... | collective-permute-start | bytes 6291464 | tf_op jit(solution)/shard_map/ppermute | solution.py:57
  68.8 17.4 %collective-permute-start.13 = (bf16[4,128,1152]{2,1,0:T(8,128)(2,1)S(1)}, bf16[4,128,1152]{2,1,0:T(8,128)(2,1)S(1)}, u32[]{:S(2)}, u32[]{:S(2)}) collective-permute-start(bf16[4,128,1152]{2,1,0:T(8,128)(2,1)S(1)} %copy-done.12), channel_id=1, source_target_pairs={{0,2},{1,7},{2,4},{3,1},{4,6},{5,3},{6,0},{7,5},{8,10},{9,15},{10,... | collective-permute-start | bytes 3538952 | tf_op jit(solution)/shard_map/ppermute | solution.py:57
  70.0 15.2 %collective-permute-start.10 = (bf16[2,128,1152]{2,1,0:T(8,128)(2,1)S(1)}, bf16[2,128,1152]{2,1,0:T(8,128)(2,1)S(1)}, u32[]{:S(2)}, u32[]{:S(2)}) collective-permute-start(bf16[2,128,1152]{2,1,0:T(8,128)(2,1)S(1)} %slice.76), channel_id=1, source_target_pairs={{0,8},{1,33},{2,10},{3,35},{4,12},{5,37},{6,14},{7,39},{8,16},{9,4... | collective-permute-start | bytes 1769480 | tf_op jit(solution)/shard_map/ppermute | solution.py:57
  70.4 14.7 %collective-permute-start.11 = (bf16[2,128,1152]{2,1,0:T(8,128)(2,1)S(1)}, bf16[2,128,1152]{2,1,0:T(8,128)(2,1)S(1)}, u32[]{:S(2)}, u32[]{:S(2)}) collective-permute-start(bf16[2,128,1152]{2,1,0:T(8,128)(2,1)S(1)} %slice.77), channel_id=1, source_target_pairs={{0,24},{1,97},{2,26},{3,99},{4,28},{5,101},{6,30},{7,103},{8,0},{9... | collective-permute-start | bytes 1769480 | tf_op jit(solution)/shard_map/ppermute | solution.py:57
  86.3 17.5 %collective-permute-start.16 = (bf16[4,128,1152]{2,1,0:T(8,128)(2,1)S(1)}, bf16[4,128,1152]{2,1,0:T(8,128)(2,1)S(1)}, u32[]{:S(2)}, u32[]{:S(2)}) collective-permute-start(bf16[4,128,1152]{2,1,0:T(8,128)(2,1)S(1)} %constant_dynamic-update-slice_fusion.2.near_ref), channel_id=1, source_target_pairs={{0,2},{1,7},{2,4},{3,1},{4,6},{5,3},{6,0},{7,5},{8,10},{9,15},{10,... | collective-permute-start | bytes 3538952 | tf_op jit(solution)/shard_map/ppermute | solution.py:57
  88.2 20.7 %collective-permute-start.14 = (bf16[2,128,2048]{2,1,0:T(8,128)(2,1)S(1)}, bf16[2,128,2048]{2,1,0:T(8,128)(2,1)S(1)}, u32[]{:S(2)}, u32[]{:S(2)}) collective-permute-start(bf16[2,128,2048]{2,1,0:T(8,128)(2,1)S(1)} %slice.78), channel_id=1, source_target_pairs={{0,8},{1,33},{2,10},{3,35},{4,12},{5,37},{6,14},{7,39},{8,16},{9,4... | collective-permute-start | bytes 3145736 | tf_op jit(solution)/shard_map/ppermute | solution.py:57
  90.5 18.3 %collective-permute-start.15 = (bf16[2,128,2048]{2,1,0:T(8,128)(2,1)S(1)}, bf16[2,128,2048]{2,1,0:T(8,128)(2,1)S(1)}, u32[]{:S(2)}, u32[]{:S(2)}) collective-permute-start(bf16[2,128,2048]{2,1,0:T(8,128)(2,1)S(1)} %slice.79), channel_id=1, source_target_pairs={{0,24},{1,97},{2,26},{3,99},{4,28},{5,101},{6,30},{7,103},{8,0},{9... | collective-permute-start | bytes 3145736 | tf_op jit(solution)/shard_map/ppermute | solution.py:57
  108.8 10.2 %collective-permute-start.18 = (f32[768,768]{1,0:T(8,128)S(1)}, f32[768,768]{1,0:T(8,128)S(1)}, u32[]{:S(2)}, u32[]{:S(2)}) collective-permute-start(f32[768,768]{1,0:T(8,128)S(1)} %hidden.3), channel_id=1, source_target_pairs={{0,1},{1,0},{2,3},{3,2},{4,5},{5,4},{6,7},{7,6},{8,9},{9,8},{10,11... | collective-permute-start | bytes 7077896 | tf_op jit(solution)/shard_map/ppermute | solution.py:36
  122.7 11.3 %collective-permute-start.19 = (bf16[768,1152]{1,0:T(8,128)(2,1)S(1)}, bf16[768,1152]{1,0:T(8,128)(2,1)}, u32[]{:S(2)}, u32[]{:S(2)}) collective-permute-start(bf16[768,1152]{1,0:T(8,128)(2,1)S(1)} %act.1.ad_ref.mine_ref), channel_id=1, source_target_pairs={{0,1},{1,0},{2,3},{3,2},{4,5},{5,4},{6,7},{7,6},{8,9},{9,8},{10,11... | collective-permute-start | bytes 5308424 | tf_op jit(solution)/shard_map/ppermute | solution.py:36
  127.9 56.6 %all-to-all-start = ((bf16[16,48,2048]{2,1,0:T(8,128)(2,1)}), bf16[16,48,2048]{2,1,0:T(8,128)(2,1)}, u32[]{:S(2)}, u32[]{:S(2)}) async-start(bf16[16,48,2048]{2,1,0:T(8,128)(2,1)} %partial.2), calls=%async_computation | async-start | bytes 6291456 | tf_op jit(solution)/shard_map/all_to_all | solution.py:449
  143.2 21.9 %collective-permute-start.20 = (bf16[768,512]{1,0:T(8,128)(2,1)}, bf16[768,512]{1,0:T(8,128)(2,1)}, u32[]{:S(2)}, u32[]{:S(2)}) collective-permute-start(bf16[768,512]{1,0:T(8,128)(2,1)} %get-tuple-element.126), channel_id=1, source_target_pairs={{0,2},{2,4},{4,6},{6,0},{1,3},{3,5},{5,7},{7,1},{8,10},{10,12},{12... | collective-permute-start | bytes 2359304 | tf_op jit(solution)/shard_map/ppermute | solution.py:446
  143.5 37.7 %collective-permute-start.21 = (bf16[768,512]{1,0:T(8,128)(2,1)S(1)}, bf16[768,512]{1,0:T(8,128)(2,1)}, u32[]{:S(2)}, u32[]{:S(2)}) collective-permute-start(bf16[768,512]{1,0:T(8,128)(2,1)S(1)} %get-tuple-element.125), channel_id=1, source_target_pairs={{0,4},{2,6},{4,0},{6,2},{1,5},{3,7},{5,1},{7,3},{8,12},{10,14},{12... | collective-permute-start | bytes 2359304 | tf_op jit(solution)/shard_map/ppermute | solution.py:446
  146.4 35.2 %collective-permute-start.22 = (bf16[768,512]{1,0:T(8,128)(2,1)S(1)}, bf16[768,512]{1,0:T(8,128)(2,1)}, u32[]{:S(2)}, u32[]{:S(2)}) collective-permute-start(bf16[768,512]{1,0:T(8,128)(2,1)S(1)} %get-tuple-element.124), channel_id=1, source_target_pairs={{0,6},{2,0},{4,2},{6,4},{1,7},{3,1},{5,3},{7,5},{8,14},{10,8},{12,... | collective-permute-start | bytes 2359304 | tf_op jit(solution)/shard_map/ppermute | solution.py:446
  184.5 13.7 %collective-permute-start.26 = (bf16[2,3,192,2048]{3,2,1,0:T(8,128)(2,1)}, bf16[2,3,192,2048]{3,2,1,0:T(8,128)(2,1)}, u32[]{:S(2)}, u32[]{:S(2)}) collective-permute-start(bf16[2,3,192,2048]{3,2,1,0:T(8,128)(2,1)} %get-tuple-element.111), channel_id=1, source_target_pairs={{0,1},{1,0},{2,3},{3,2},{4,5},{5,4},{6,7},{7,6},{8,9},{9,8},{10,11... | collective-permute-start | bytes 14155784 | tf_op jit(solution)/shard_map/ppermute | solution.py:36
  184.5 21.9 %all-to-all-start.1 = ((bf16[16,48,512]{2,1,0:T(8,128)(2,1)}), bf16[16,48,512]{2,1,0:T(8,128)(2,1)S(1)}, u32[]{:S(2)}, u32[]{:S(2)}) async-start(bf16[16,48,512]{2,1,0:T(8,128)(2,1)} %bitcast.39), calls=%async_computation.1 | async-start | bytes 1572864 | tf_op jit(solution)/shard_map/all_to_all | solution.py:479
  195.0 9.6 %collective-permute-start.24 = (bf16[128,512]{1,0:T(8,128)(2,1)S(1)}, bf16[128,512]{1,0:T(8,128)(2,1)S(1)}, u32[]{:S(2)}, u32[]{:S(2)}) collective-permute-start(bf16[128,512]{1,0:T(8,128)(2,1)S(1)} %get-tuple-element.128), channel_id=1, source_target_pairs={{0,4},{2,6},{4,0},{6,2},{1,5},{3,7},{5,1},{7,3},{8,12},{10,14},{12... | collective-permute-start | bytes 393224 | tf_op jit(solution)/shard_map/ppermute | solution.py:446
  (23 other events, 149.3 us)

commit v7 on v6

--- a/solution.py
+++ b/solution.py
@@ -171,8 +171,7 @@
     silu = gate * sig
     outs = (d * up * sig * (1.0 + gate * (1.0 - sig)), d * silu, silu * up)
     for i, value in enumerate(outs):
-        at = pl.multiple_of(i * n + pl.program_id(0) * 128, 128)
-        out_ref[:, pl.ds(at, 128)] = value.astype(BF)
+        out_ref[:, i * n : (i + 1) * n] = value.astype(BF)
 
 
 def by_x_kernel(e_ref, ad_ref, wgu_ref, out_ref):
@@ -391,28 +390,28 @@
             name="hidden",
         )(which, v, w)
 
-    pre_out = hidden(others, xs, wgu, 256)
+    pre_out = hidden(others, xs, wgu, 4 * f)
     gd0, gd1, gs, pre_out = together(gd0, gd1, gs, pre_out)
     pre_in = swap(pre_out)
     gs = select(select_g_kernel, 12, xd, gd0, [gs])
     gs = select(select_g_kernel, 14, xd, gd1, [gs], 2)
-    dh_out = hidden(others, gs, wd, 128)
+    dh_out = hidden(others, gs, wd, 2 * f)
     xs, dh_out = together(xs, dh_out)
     dh_in = swap(dh_out)
-    pre = hidden(cs, xs, wgu, 256)
-    column = lambda k: pl.BlockSpec((slots, 128), lambda j, er: (0, k + j))
+    pre = hidden(cs, xs, wgu, 4 * f)
+    column = lambda k: pl.BlockSpec((slots, 2 * f), lambda j, er: (0, k))
     mine = pl.pallas_call(
         act_kernel,
         grid_spec=prefetched(
-            (3,),
+            (1,),
             [
                 pl.BlockSpec((1, slots, half), lambda j, er: (er[0], 0, 0)),
-                pl.BlockSpec((1, 128, half), lambda j, er: (er[0], j, 0)),
+                pl.BlockSpec((1, 2 * f, half), lambda j, er: (er[0], j, 0)),
                 column(0),
                 column(0),
                 column(0),
-                column(3),
-                column(3),
+                column(1),
+                column(1),
             ],
             pl.BlockSpec((slots, 6 * f), lambda j, er: (0, 0)),
         ),

time: 209 us -> 205 us (0.981)
  Pallas kernels: 79.8 us -> 76.1 us
    pallas_call x3, Pallas kernels: 9.38 us -> 7.08 us  [hidden(): pl.pallas_call(hidden_kernel, grid_spec=prefetched((n // chunk,), [pl.Blo...]
where the time goes in v7:
time: 205 us; the launch traced here: 204 us
  Pallas kernels  76.1 us (37%)
  waiting for transfers between devices  61.1 us (30%)
  starting transfers between devices  45.8 us (22%)
  local copies, waits for them, and re-layouts  14.9 us (7%)
  other arithmetic  5.02 us (2%)
    ppermute x16, waiting for transfers between devices, hop(): return lax.ppermute(v, ('z', 'y', 'x', 'c'), to)  39.1 us
    ppermute x16, starting transfers between devices, hop(): return lax.ppermute(v, ('z', 'y', 'x', 'c'), to)  23.2 us
    pallas_call x9, Pallas kernels, select(): pl.pallas_call(kernel, grid_spec=prefetched((n,), specs + [pl.BlockSpec(m...  22.1 us
    ppermute x6, waiting for transfers between devices, shards(): lax.ppermute(v, 'x', [(i, (i + k) % 4) for i in range(4)])  20.1 us
    pallas_call x1, Pallas kernels, shards(): pl.pallas_call(weight_kernel, grid_spec=prefetched((2, 4), [VMEM, VMEM, p...  14.9 us
    pallas_call x2, Pallas kernels, partial(): pl.pallas_call(kernel, grid_spec=prefetched((4,), [VMEM, pl.BlockSpec((1,...  10.3 us
    ppermute x6, starting transfers between devices, shards(): lax.ppermute(v, 'x', [(i, (i + k) % 4) for i in range(4)])  8.78 us
    unnamed x38, local copies, waits for them, and re-layouts  7.78 us
  transfers between devices with their start and end apart: 29, of which 15 were waited for; matrix products, arithmetic and copies ran while one was open for 5% of the time, Pallas kernels for 34%

profile of v7, /device:TPU:0, one launch (start us, length us, event | category | flops | bytes accessed | tf_op | source)
XLA Modules:
  0.0 204.1 jit_solution(4610219839265652336)
XLA Ops:
  1.3 2.9 %pack.1.pw_ref = bf16[128,3200]{1,0:T(8,128)(2,1)} custom-call(s32[6]{0:T(128)} %stack.111.at_ref, s32[8,128]{1,0:T(8,128)} %bitcast.63, f32[8,128]{1,0:T(8,128)} %bitcast.64, bf16[128,4096]{1,0:T(8,128)(2,1)} %t1.1, bf16[128,4096]{1,0:T(8,128)(2,1)} %t1.1, bf16[128,4096]{1,0:T(8,128)(2,1)} %g3.1, bf16[128,4096]{1,0:T(8,128)(2,1)} %g3.1, ...), custom_call_target="tpu_custom_call" | custom-call | flops 10000 | bytes 2000 | tf_op jit(solution)/shard_map/pack/pallas_call | solution.py:271
  8.4 5.0 %outgoing.1 = bf16[6,192,2048]{2,1,0:T(8,128)(2,1)} custom-call(s32[1]{0:T(128)} %bitcast.c_ref.e_ref, bf16[2,192,4096]{2,1,0:T(8,128)(2,1)} %g_ref.3, bf16[2,192,4096]{2,1,0:T(8,128)(2,1)} %u_ref.3, bf16[2,192,4096]{2,1,0:T(8,128)(2,1)} %d_ref.3), custom_call_target="tpu_custom_call" | custom-call | bytes 9400 | tf_op jit(solution)/shard_map/outgoing/pallas_call | solution.py:287
  13.5 5.5 %collective-permute-done = bf16[128,3200]{1,0:T(8,128)(2,1)S(1)} collective-permute-done((bf16[128,3200]{1,0:T(8,128)(2,1)}, bf16[128,3200]{1,0:T(8,128)(2,1)S(1)}, u32[]{:S(2)}, u32[]{:S(2)}) %collective-permute-start) | collective-permute-done | bytes 819232 | tf_op jit(solution)/shard_map/ppermute | solution.py:57
  22.6 5.8 %collective-permute-done.2 = bf16[64,3200]{1,0:T(8,128)(2,1)S(1)} collective-permute-done((bf16[64,3200]{1,0:T(8,128)(2,1)S(1)}, bf16[64,3200]{1,0:T(8,128)(2,1)S(1)}, u32[]{:S(2)}, u32[]{:S(2)}) %collective-permute-start.2) | collective-permute-done | bytes 409632 | tf_op jit(solution)/shard_map/ppermute | solution.py:57
  42.7 4.3 %collective-permute-done.5.near_ref = bf16[4,128,1152]{2,1,0:T(8,128)(2,1)} collective-permute-done((bf16[4,128,1152]{2,1,0:T(8,128)(2,1)S(1)}, bf16[4,128,1152]{2,1,0:T(8,128)(2,1)}, u32[]{:S(2)}, u32[]{:S(2)}) %collective-permute-start.5) | collective-permute-done | bytes 1179680 | tf_op jit(solution)/shard_map/ppermute | solution.py:57
  47.2 2.9 %collective-permute-done.7.far_ref = bf16[4,128,1152]{2,1,0:T(8,128)(2,1)S(1)} collective-permute-done((bf16[4,128,1152]{2,1,0:T(8,128)(2,1)S(1)}, bf16[4,128,1152]{2,1,0:T(8,128)(2,1)S(1)}, u32[]{:S(2)}, u32[]{:S(2)}) %collective-permute-start.7) | collective-permute-done | bytes 1179680 | tf_op jit(solution)/shard_map/ppermute | solution.py:57
  54.7 3.6 %select.76.rest_0_ = bf16[2,768,2048]{2,1,0:T(8,128)(2,1)S(1)} custom-call(s32[18]{0:T(128)S(1)} %stack.130.info_ref, bf16[4,128,1152]{2,1,0:T(8,128)(2,1)S(1)} %pad_maximum_fusion.1.near_ref, bf16[4,128,2048]{2,1,0:T(8,128)(2,1)} %pad_maximum_fusion.g_ref), custom_call_target="tpu_custom_call" | custom-call | flops 201326 | bytes 5600 | tf_op jit(solution)/shard_map/select/pallas_call | solution.py:347
  60.1 8.7 %collective-permute-done.12.far_ref = bf16[4,128,1152]{2,1,0:T(8,128)(2,1)} collective-permute-done((bf16[4,128,1152]{2,1,0:T(8,128)(2,1)}, bf16[4,128,1152]{2,1,0:T(8,128)(2,1)}, u32[]{:S(2)}, u32[]{:S(2)}) %collective-permute-start.12) | collective-permute-done | bytes 1179680 | tf_op jit(solution)/shard_map/ppermute | solution.py:57
  70.4 2.9 %collective-permute-start.11 = (bf16[2,128,1152]{2,1,0:T(8,128)(2,1)S(1)}, bf16[2,128,1152]{2,1,0:T(8,128)(2,1)S(1)}, u32[]{:S(2)}, u32[]{:S(2)}) collective-permute-start(bf16[2,128,1152]{2,1,0:T(8,128)(2,1)S(1)} %slice.77), channel_id=1, source_target_pairs={{0,24},{1,97},{2,26},{3,99},{4,28},{5,101},{6,30},{7,103},{8,0},{9... | collective-permute-start | bytes 1769480 | tf_op jit(solution)/shard_map/ppermute | solution.py:57
  73.3 3.6 %select.77.rest_0_ = bf16[2,768,2048]{2,1,0:T(8,128)(2,1)S(1)} custom-call(s32[18]{0:T(128)S(1)} %stack.130.info_ref, bf16[4,128,1152]{2,1,0:T(8,128)(2,1)} %collective-permute-done.5.near_ref, bf16[4,128,1152]{2,1,0:T(8,128)(2,1)} %collective-permute-done.12.far_ref, bf16[2,768,2048]{2,1,0:T(8,128)(2,1)S(1)} %select.75.rest_0_), custom_call_target="tpu_custom_call", output_to_operand_aliasing={{}: (3, {})} | custom-call | flops 201326 | bytes 5600 | tf_op jit(solution)/shard_map/select/pallas_call | solution.py:347
  76.9 8.2 %collective-permute-done.10 = bf16[2,128,1152]{2,1,0:T(8,128)(2,1)S(1)} collective-permute-done((bf16[2,128,1152]{2,1,0:T(8,128)(2,1)S(1)}, bf16[2,128,1152]{2,1,0:T(8,128)(2,1)S(1)}, u32[]{:S(2)}, u32[]{:S(2)}) %collective-permute-start.10) | collective-permute-done | bytes 589856 | tf_op jit(solution)/shard_map/ppermute | solution.py:57
  93.0 3.6 %select.78.rest_0_ = bf16[2,768,2048]{2,1,0:T(8,128)(2,1)S(1)} custom-call(s32[18]{0:T(128)S(1)} %stack.130.info_ref, bf16[4,128,1152]{2,1,0:T(8,128)(2,1)} %collective-permute-done.5.near_ref, bf16[4,128,2048]{2,1,0:T(8,128)(2,1)} %collective-permute-done.8.g_ref, bf16[2,768,2048]{2,1,0:T(8,128)(2,1)S(1)} %select.76.rest_0_), custom_call_target="tpu_custom_call", output_to_operand_aliasing={{}: (3, {})} | custom-call | flops 201326 | bytes 5600 | tf_op jit(solution)/shard_map/select/pallas_call | solution.py:347
  96.7 3.6 %select.79.rest_0_ = bf16[2,768,2048]{2,1,0:T(8,128)(2,1)S(1)} custom-call(s32[18]{0:T(128)S(1)} %stack.130.info_ref, bf16[4,128,1152]{2,1,0:T(8,128)(2,1)S(1)} %copy-done.12, bf16[4,128,2048]{2,1,0:T(8,128)(2,1)} %collective-permute-done.9.g_ref, bf16[2,768,2048]{2,1,0:T(8,128)(2,1)S(1)} %select.78.rest_0_), custom_call_target="tpu_custom_call", output_to_operand_aliasing={{}: (3, {})} | custom-call | flops 201326 | bytes 5600 | tf_op jit(solution)/shard_map/select/pallas_call | solution.py:347
  119.1 5.0 %partial.2 = bf16[16,48,2048]{2,1,0:T(8,128)(2,1)} custom-call(s32[2]{0:T(128)S(1)} %pad_add_fusion.e_ref.c_ref, bf16[768,1152]{1,0:T(8,128)(2,1)S(1)} %act.1.ad_ref.mine_ref, bf16[2,768,2048]{2,1,0:T(8,128)(2,1)S(1)} %bitcast.62), custom_call_target="tpu_custom_call" | custom-call | flops 2415919 | bytes 8000 | tf_op jit(solution)/shard_map/partial/pallas_call | solution.py:434
  124.1 6.0 %all-to-all-start = ((bf16[16,48,2048]{2,1,0:T(8,128)(2,1)}), bf16[16,48,2048]{2,1,0:T(8,128)(2,1)}, u32[]{:S(2)}, u32[]{:S(2)}) async-start(bf16[16,48,2048]{2,1,0:T(8,128)(2,1)} %partial.2), calls=%async_computation | async-start | bytes 6291456 | tf_op jit(solution)/shard_map/all_to_all | solution.py:448
  130.2 2.8 %copy-done.3 = bf16[2,768,2048]{2,1,0:T(8,128)(2,1)S(1)} copy-done((bf16[2,768,2048]{2,1,0:T(8,128)(2,1)S(1)}, bf16[2,768,2048]{2,1,0:T(8,128)(2,1)}, u32[]{:S(2)}) %copy-start.3) | copy-done | bytes 6291480
  133.0 5.3 %partial.3 = bf16[4,768,512]{2,1,0:T(8,128)(2,1)S(1)} custom-call(s32[2]{0:T(128)S(1)} %pad_add_fusion.1.e_ref, bf16[768,1152]{1,0:T(8,128)(2,1)} %collective-permute-done.19.ad_ref.theirs_ref, bf16[2,768,2048]{2,1,0:T(8,128)(2,1)S(1)} %copy-done.3), custom_call_target="tpu_custom_call" | custom-call | flops 2415919 | bytes 8000 | tf_op jit(solution)/shard_map/partial/pallas_call | solution.py:434
  139.7 2.9 %collective-permute-start.21 = (bf16[768,512]{1,0:T(8,128)(2,1)S(1)}, bf16[768,512]{1,0:T(8,128)(2,1)}, u32[]{:S(2)}, u32[]{:S(2)}) collective-permute-start(bf16[768,512]{1,0:T(8,128)(2,1)S(1)} %get-tuple-element.125), channel_id=1, source_target_pairs={{0,4},{2,6},{4,0},{6,2},{1,5},{3,7},{5,1},{7,3},{8,12},{10,14},{12... | collective-permute-start | bytes 2359304 | tf_op jit(solution)/shard_map/ppermute | solution.py:445
  143.7 14.9 %weights.1 = (bf16[2,192,4096]{2,1,0:T(8,128)(2,1)}, bf16[2,192,4096]{2,1,0:T(8,128)(2,1)}, bf16[2,192,4096]{2,1,0:T(8,128)(2,1)}, bf16[2,3,192,2048]{3,2,1,0:T(8,128)(2,1)}) custom-call(s32[1]{0:T(128)} %bitcast.c_ref.e_ref, bf16[768,1152]{1,0:T(8,128)(2,1)} %copy-done.4, bf16[768,1152]{1,0:T(8,128)(2,1)} %collective-permute-done.19.ad_ref.theirs_ref, ...), custom_call_target="tpu_custom_call" | custom-call | flops 7247757 | bytes 24000 | tf_op jit(solution)/shard_map/weights/pallas_call | solution.py:455
  161.3 15.9 %collective-permute-done.21 = bf16[768,512]{1,0:T(8,128)(2,1)} collective-permute-done((bf16[768,512]{1,0:T(8,128)(2,1)S(1)}, bf16[768,512]{1,0:T(8,128)(2,1)}, u32[]{:S(2)}, u32[]{:S(2)}) %collective-permute-start.21) | collective-permute-done | bytes 786464 | tf_op jit(solution)/shard_map/ppermute | solution.py:445
  177.7 2.9 %fusion.2 = bf16[768,512]{1,0:T(8,128)(2,1)} fusion(bf16[768,512]{1,0:T(8,128)(2,1)} %collective-permute-done.22, bf16[768,512]{1,0:T(8,128)(2,1)} %collective-permute-done.21, bf16[768,512]{1,0:T(8,128)(2,1)} %collective-permute-done.20, bf16[4,768,512]{2,1,0:T(8,128)(2,1)S(1)} %partial.3), kind=kLoop, calls=%fused_computation.4 | loop fusion | flops 3145728 | bytes 3932160 | tf_op jit(solution)/shard_map/convert_element_type | solution.py:475
  180.6 6.9 %all-to-all-start.1 = ((bf16[16,48,512]{2,1,0:T(8,128)(2,1)}), bf16[16,48,512]{2,1,0:T(8,128)(2,1)S(1)}, u32[]{:S(2)}, u32[]{:S(2)}) async-start(bf16[16,48,512]{2,1,0:T(8,128)(2,1)} %bitcast.39), calls=%async_computation.1 | async-start | bytes 1572864 | tf_op jit(solution)/shard_map/all_to_all | solution.py:478
  191.2 3.0 %collective-permute-start.24 = (bf16[128,512]{1,0:T(8,128)(2,1)S(1)}, bf16[128,512]{1,0:T(8,128)(2,1)S(1)}, u32[]{:S(2)}, u32[]{:S(2)}) collective-permute-start(bf16[128,512]{1,0:T(8,128)(2,1)S(1)} %get-tuple-element.128), channel_id=1, source_target_pairs={{0,4},{2,6},{4,0},{6,2},{1,5},{3,7},{5,1},{7,3},{8,12},{10,14},{12... | collective-permute-start | bytes 393224 | tf_op jit(solution)/shard_map/ppermute | solution.py:445
  194.5 5.0 %settle.1 = (bf16[2,192,4096]{2,1,0:T(8,128)(2,1)}, bf16[2,192,4096]{2,1,0:T(8,128)(2,1)}, bf16[2,192,4096]{2,1,0:T(8,128)(2,1)}) custom-call(s32[1]{0:T(128)} %bitcast.c_ref.e_ref, bf16[2,3,192,2048]{3,2,1,0:T(8,128)(2,1)} %collective-permute-done.26.in_ref, ...), custom_call_target="tpu_custom_call", output_to_operand_aliasing={{0}: (2, {}), {1}: (3, {}), {2}: (4, {})} | custom-call | bytes 9400 | tf_op jit(solution)/shard_map/settle/pallas_call | solution.py:480
  (118 shorter events, 71.6 us)
Async XLA Ops:
  4.3 14.7 %collective-permute-start = (bf16[128,3200]{1,0:T(8,128)(2,1)}, bf16[128,3200]{1,0:T(8,128)(2,1)S(1)}, u32[]{:S(2)}, u32[]{:S(2)}) collective-permute-start(bf16[128,3200]{1,0:T(8,128)(2,1)} %pack.1.pw_ref), channel_id=1, source_target_pairs={{0,32},{1,9},{2,34},{3,11},{4,36},{5,13},{6,38},{7,15},{8,40},{9,1... | collective-permute-start | bytes 2457608 | tf_op jit(solution)/shard_map/ppermute | solution.py:57
  6.3 12.7 %collective-permute-start.1 = (bf16[128,3200]{1,0:T(8,128)(2,1)}, bf16[128,3200]{1,0:T(8,128)(2,1)S(1)}, u32[]{:S(2)}, u32[]{:S(2)}) collective-permute-start(bf16[128,3200]{1,0:T(8,128)(2,1)} %pack.1.pw_ref), channel_id=1, source_target_pairs={{0,96},{1,25},{2,98},{3,27},{4,100},{5,29},{6,102},{7,31},{8,104},... | collective-permute-start | bytes 2457608 | tf_op jit(solution)/shard_map/ppermute | solution.py:57
  19.0 10.0 %collective-permute-start.4 = (bf16[6,192,2048]{2,1,0:T(8,128)(2,1)}, bf16[6,192,2048]{2,1,0:T(8,128)(2,1)S(1)}, u32[]{:S(2)}, u32[]{:S(2)}) collective-permute-start(bf16[6,192,2048]{2,1,0:T(8,128)(2,1)} %outgoing.1), channel_id=1, source_target_pairs={{0,1},{1,0},{2,3},{3,2},{4,5},{5,4},{6,7},{7,6},{8,9},{9,8},{10,11... | collective-permute-start | bytes 14155784 | tf_op jit(solution)/shard_map/ppermute | solution.py:36
  29.3 17.6 %collective-permute-start.5 = (bf16[4,128,1152]{2,1,0:T(8,128)(2,1)S(1)}, bf16[4,128,1152]{2,1,0:T(8,128)(2,1)}, u32[]{:S(2)}, u32[]{:S(2)}) collective-permute-start(bf16[4,128,1152]{2,1,0:T(8,128)(2,1)S(1)} %pad_maximum_fusion.1.near_ref), channel_id=1, source_target_pairs={{0,8},{1,33},{2,10},{3,35},{4,12},{5,37},{6,14},{7,39},{8,16},{9,4... | collective-permute-start | bytes 3538952 | tf_op jit(solution)/shard_map/ppermute | solution.py:57
  31.0 16.2 %collective-permute-start.6 = (bf16[4,128,1152]{2,1,0:T(8,128)(2,1)S(1)}, bf16[4,128,1152]{2,1,0:T(8,128)(2,1)S(1)}, u32[]{:S(2)}, u32[]{:S(2)}) collective-permute-start(bf16[4,128,1152]{2,1,0:T(8,128)(2,1)S(1)} %pad_maximum_fusion.1.near_ref), channel_id=1, source_target_pairs={{0,24},{1,97},{2,26},{3,99},{4,28},{5,101},{6,30},{7,103},{8,0},{9... | collective-permute-start | bytes 3538952 | tf_op jit(solution)/shard_map/ppermute | solution.py:57
  32.6 17.4 %collective-permute-start.7 = (bf16[4,128,1152]{2,1,0:T(8,128)(2,1)S(1)}, bf16[4,128,1152]{2,1,0:T(8,128)(2,1)S(1)}, u32[]{:S(2)}, u32[]{:S(2)}) collective-permute-start(bf16[4,128,1152]{2,1,0:T(8,128)(2,1)S(1)} %pad_maximum_fusion.1.near_ref), channel_id=1, source_target_pairs={{0,2},{1,7},{2,4},{3,1},{4,6},{5,3},{6,0},{7,5},{8,10},{9,15},{10,... | collective-permute-start | bytes 3538952 | tf_op jit(solution)/shard_map/ppermute | solution.py:57
  51.0 17.7 %collective-permute-start.12 = (bf16[4,128,1152]{2,1,0:T(8,128)(2,1)}, bf16[4,128,1152]{2,1,0:T(8,128)(2,1)}, u32[]{:S(2)}, u32[]{:S(2)}) collective-permute-start(bf16[4,128,1152]{2,1,0:T(8,128)(2,1)} %collective-permute-done.5.near_ref), channel_id=1, source_target_pairs={{0,2},{1,7},{2,4},{3,1},{4,6},{5,3},{6,0},{7,5},{8,10},{9,15},{10,... | collective-permute-start | bytes 3538952 | tf_op jit(solution)/shard_map/ppermute | solution.py:57
  51.3 33.8 %collective-permute-start.8 = (bf16[4,128,2048]{2,1,0:T(8,128)(2,1)}, bf16[4,128,2048]{2,1,0:T(8,128)(2,1)}, u32[]{:S(2)}, u32[]{:S(2)}) collective-permute-start(bf16[4,128,2048]{2,1,0:T(8,128)(2,1)} %pad_maximum_fusion.g_ref), channel_id=1, source_target_pairs={{0,8},{1,33},{2,10},{3,35},{4,12},{5,37},{6,14},{7,39},{8,16},{9,4... | collective-permute-start | bytes 6291464 | tf_op jit(solution)/shard_map/ppermute | solution.py:57
  52.3 32.9 %collective-permute-start.9 = (bf16[4,128,2048]{2,1,0:T(8,128)(2,1)}, bf16[4,128,2048]{2,1,0:T(8,128)(2,1)}, u32[]{:S(2)}, u32[]{:S(2)}) collective-permute-start(bf16[4,128,2048]{2,1,0:T(8,128)(2,1)} %pad_maximum_fusion.g_ref), channel_id=1, source_target_pairs={{0,24},{1,97},{2,26},{3,99},{4,28},{5,101},{6,30},{7,103},{8,0},{9... | collective-permute-start | bytes 6291464 | tf_op jit(solution)/shard_map/ppermute | solution.py:57
  68.8 17.4 %collective-permute-start.13 = (bf16[4,128,1152]{2,1,0:T(8,128)(2,1)S(1)}, bf16[4,128,1152]{2,1,0:T(8,128)(2,1)S(1)}, u32[]{:S(2)}, u32[]{:S(2)}) collective-permute-start(bf16[4,128,1152]{2,1,0:T(8,128)(2,1)S(1)} %copy-done.12), channel_id=1, source_target_pairs={{0,2},{1,7},{2,4},{3,1},{4,6},{5,3},{6,0},{7,5},{8,10},{9,15},{10,... | collective-permute-start | bytes 3538952 | tf_op jit(solution)/shard_map/ppermute | solution.py:57
  70.0 15.2 %collective-permute-start.10 = (bf16[2,128,1152]{2,1,0:T(8,128)(2,1)S(1)}, bf16[2,128,1152]{2,1,0:T(8,128)(2,1)S(1)}, u32[]{:S(2)}, u32[]{:S(2)}) collective-permute-start(bf16[2,128,1152]{2,1,0:T(8,128)(2,1)S(1)} %slice.76), channel_id=1, source_target_pairs={{0,8},{1,33},{2,10},{3,35},{4,12},{5,37},{6,14},{7,39},{8,16},{9,4... | collective-permute-start | bytes 1769480 | tf_op jit(solution)/shard_map/ppermute | solution.py:57
  70.4 14.7 %collective-permute-start.11 = (bf16[2,128,1152]{2,1,0:T(8,128)(2,1)S(1)}, bf16[2,128,1152]{2,1,0:T(8,128)(2,1)S(1)}, u32[]{:S(2)}, u32[]{:S(2)}) collective-permute-start(bf16[2,128,1152]{2,1,0:T(8,128)(2,1)S(1)} %slice.77), channel_id=1, source_target_pairs={{0,24},{1,97},{2,26},{3,99},{4,28},{5,101},{6,30},{7,103},{8,0},{9... | collective-permute-start | bytes 1769480 | tf_op jit(solution)/shard_map/ppermute | solution.py:57
  86.3 17.5 %collective-permute-start.16 = (bf16[4,128,1152]{2,1,0:T(8,128)(2,1)S(1)}, bf16[4,128,1152]{2,1,0:T(8,128)(2,1)S(1)}, u32[]{:S(2)}, u32[]{:S(2)}) collective-permute-start(bf16[4,128,1152]{2,1,0:T(8,128)(2,1)S(1)} %constant_dynamic-update-slice_fusion.2.near_ref), channel_id=1, source_target_pairs={{0,2},{1,7},{2,4},{3,1},{4,6},{5,3},{6,0},{7,5},{8,10},{9,15},{10,... | collective-permute-start | bytes 3538952 | tf_op jit(solution)/shard_map/ppermute | solution.py:57
  88.2 20.1 %collective-permute-start.14 = (bf16[2,128,2048]{2,1,0:T(8,128)(2,1)S(1)}, bf16[2,128,2048]{2,1,0:T(8,128)(2,1)S(1)}, u32[]{:S(2)}, u32[]{:S(2)}) collective-permute-start(bf16[2,128,2048]{2,1,0:T(8,128)(2,1)S(1)} %slice.78), channel_id=1, source_target_pairs={{0,8},{1,33},{2,10},{3,35},{4,12},{5,37},{6,14},{7,39},{8,16},{9,4... | collective-permute-start | bytes 3145736 | tf_op jit(solution)/shard_map/ppermute | solution.py:57
  90.5 17.7 %collective-permute-start.15 = (bf16[2,128,2048]{2,1,0:T(8,128)(2,1)S(1)}, bf16[2,128,2048]{2,1,0:T(8,128)(2,1)S(1)}, u32[]{:S(2)}, u32[]{:S(2)}) collective-permute-start(bf16[2,128,2048]{2,1,0:T(8,128)(2,1)S(1)} %slice.79), channel_id=1, source_target_pairs={{0,24},{1,97},{2,26},{3,99},{4,28},{5,101},{6,30},{7,103},{8,0},{9... | collective-permute-start | bytes 3145736 | tf_op jit(solution)/shard_map/ppermute | solution.py:57
  118.8 11.4 %collective-permute-start.19 = (bf16[768,1152]{1,0:T(8,128)(2,1)S(1)}, bf16[768,1152]{1,0:T(8,128)(2,1)}, u32[]{:S(2)}, u32[]{:S(2)}) collective-permute-start(bf16[768,1152]{1,0:T(8,128)(2,1)S(1)} %act.1.ad_ref.mine_ref), channel_id=1, source_target_pairs={{0,1},{1,0},{2,3},{3,2},{4,5},{5,4},{6,7},{7,6},{8,9},{9,8},{10,11... | collective-permute-start | bytes 5308424 | tf_op jit(solution)/shard_map/ppermute | solution.py:36
  124.1 56.5 %all-to-all-start = ((bf16[16,48,2048]{2,1,0:T(8,128)(2,1)}), bf16[16,48,2048]{2,1,0:T(8,128)(2,1)}, u32[]{:S(2)}, u32[]{:S(2)}) async-start(bf16[16,48,2048]{2,1,0:T(8,128)(2,1)} %partial.2), calls=%async_computation | async-start | bytes 6291456 | tf_op jit(solution)/shard_map/all_to_all | solution.py:448
  139.4 21.9 %collective-permute-start.20 = (bf16[768,512]{1,0:T(8,128)(2,1)}, bf16[768,512]{1,0:T(8,128)(2,1)}, u32[]{:S(2)}, u32[]{:S(2)}) collective-permute-start(bf16[768,512]{1,0:T(8,128)(2,1)} %get-tuple-element.126), channel_id=1, source_target_pairs={{0,2},{2,4},{4,6},{6,0},{1,3},{3,5},{5,7},{7,1},{8,10},{10,12},{12... | collective-permute-start | bytes 2359304 | tf_op jit(solution)/shard_map/ppermute | solution.py:445
  139.7 37.6 %collective-permute-start.21 = (bf16[768,512]{1,0:T(8,128)(2,1)S(1)}, bf16[768,512]{1,0:T(8,128)(2,1)}, u32[]{:S(2)}, u32[]{:S(2)}) collective-permute-start(bf16[768,512]{1,0:T(8,128)(2,1)S(1)} %get-tuple-element.125), channel_id=1, source_target_pairs={{0,4},{2,6},{4,0},{6,2},{1,5},{3,7},{5,1},{7,3},{8,12},{10,14},{12... | collective-permute-start | bytes 2359304 | tf_op jit(solution)/shard_map/ppermute | solution.py:445
  142.6 35.1 %collective-permute-start.22 = (bf16[768,512]{1,0:T(8,128)(2,1)S(1)}, bf16[768,512]{1,0:T(8,128)(2,1)}, u32[]{:S(2)}, u32[]{:S(2)}) collective-permute-start(bf16[768,512]{1,0:T(8,128)(2,1)S(1)} %get-tuple-element.124), channel_id=1, source_target_pairs={{0,6},{2,0},{4,2},{6,4},{1,7},{3,1},{5,3},{7,5},{8,14},{10,8},{12,... | collective-permute-start | bytes 2359304 | tf_op jit(solution)/shard_map/ppermute | solution.py:445
  180.6 13.9 %collective-permute-start.26 = (bf16[2,3,192,2048]{3,2,1,0:T(8,128)(2,1)}, bf16[2,3,192,2048]{3,2,1,0:T(8,128)(2,1)}, u32[]{:S(2)}, u32[]{:S(2)}) collective-permute-start(bf16[2,3,192,2048]{3,2,1,0:T(8,128)(2,1)} %get-tuple-element.111), channel_id=1, source_target_pairs={{0,1},{1,0},{2,3},{3,2},{4,5},{5,4},{6,7},{7,6},{8,9},{9,8},{10,11... | collective-permute-start | bytes 14155784 | tf_op jit(solution)/shard_map/ppermute | solution.py:36
  180.6 21.9 %all-to-all-start.1 = ((bf16[16,48,512]{2,1,0:T(8,128)(2,1)}), bf16[16,48,512]{2,1,0:T(8,128)(2,1)S(1)}, u32[]{:S(2)}, u32[]{:S(2)}) async-start(bf16[16,48,512]{2,1,0:T(8,128)(2,1)} %bitcast.39), calls=%async_computation.1 | async-start | bytes 1572864 | tf_op jit(solution)/shard_map/all_to_all | solution.py:478
  190.1 9.5 %collective-permute-start.23 = (bf16[128,512]{1,0:T(8,128)(2,1)S(1)}, bf16[128,512]{1,0:T(8,128)(2,1)S(1)}, u32[]{:S(2)}, u32[]{:S(2)}) collective-permute-start(bf16[128,512]{1,0:T(8,128)(2,1)S(1)} %get-tuple-element.129), channel_id=1, source_target_pairs={{0,2},{2,4},{4,6},{6,0},{1,3},{3,5},{5,7},{7,1},{8,10},{10,12},{12... | collective-permute-start | bytes 393224 | tf_op jit(solution)/shard_map/ppermute | solution.py:445
  191.2 9.4 %collective-permute-start.24 = (bf16[128,512]{1,0:T(8,128)(2,1)S(1)}, bf16[128,512]{1,0:T(8,128)(2,1)S(1)}, u32[]{:S(2)}, u32[]{:S(2)}) collective-permute-start(bf16[128,512]{1,0:T(8,128)(2,1)S(1)} %get-tuple-element.128), channel_id=1, source_target_pairs={{0,4},{2,6},{4,0},{6,2},{1,5},{3,7},{5,1},{7,3},{8,12},{10,14},{12... | collective-permute-start | bytes 393224 | tf_op jit(solution)/shard_map/ppermute | solution.py:445
  (23 other events, 143.8 us)

commit v8 on v7

--- a/solution.py
+++ b/solution.py
@@ -180,24 +180,19 @@
 
 def by_block_kernel(e_ref, ad_ref, wgu_ref, out_ref, stage, sems):
     step = pl.program_id(0)
-    turn = lax.rem(step, 2)
 
     def leaving(j, slot):
-        cols = pl.ds(pl.multiple_of(j * 512, 512), 512)
+        cols = pl.ds(pl.multiple_of(j * 1024, 1024), 1024)
         return pltpu.make_async_copy(stage.at[slot], out_ref.at[:, :, cols], sems.at[slot])
 
-    @pl.when(step >= 2)
+    got = mm(ad_ref[:, 0 : wgu_ref.shape[1]], wgu_ref[0]).astype(BF)
+    stage[step] = got.reshape(stage.shape[1:])
+    leaving(step, step).start()
+
+    @pl.when(step == 1)
     def _():
-        leaving(step - 2, turn).wait()
-
-    got = mm(ad_ref[:, 0 : wgu_ref.shape[1]], wgu_ref[0]).astype(BF)
-    stage[turn] = got.reshape(stage.shape[1:])
-    leaving(step, turn).start()
-
-    @pl.when(step == 3)
-    def _():
-        leaving(2, 0).wait()
-        leaving(3, 1).wait()
+        leaving(0, 0).wait()
+        leaving(1, 1).wait()
 
 
 def weight_kernel(c_ref, mine_ref, theirs_ref, xs_ref, gs_ref, gg_ref, gu_ref, gd_ref, send_ref, dt):
@@ -424,17 +419,18 @@
 
     def partial(kernel, which, ad):
         scratch = []
+        wide = 512 if kernel is by_x_kernel else 1024
         if kernel is by_x_kernel:
             shape = like((4, slots, 512))
             out = pl.BlockSpec((1, slots, 512), lambda j, er: (lax.rem(j - er[1] + 4, 4), 0, 0))
         else:
             shape = pltpu.HBM((16, CAP, half), BF)
             out = pl.BlockSpec(memory_space=pltpu.HBM)
-            scratch = [pltpu.VMEM((2, 16, CAP, 512), BF), pltpu.SemaphoreType.DMA((2,))]
+            scratch = [pltpu.VMEM((2, 16, CAP, 1024), BF), pltpu.SemaphoreType.DMA((2,))]
         return pl.pallas_call(
             kernel,
             grid_spec=prefetched(
-                (4,), [VMEM, pl.BlockSpec((1, 4 * f, 512), lambda j, er: (er[0], 0, j))], out, scratch
+                (half // wide,), [VMEM, pl.BlockSpec((1, 4 * f, wide), lambda j, er: (er[0], 0, j))], out, scratch
             ),
             out_shape=shape,
             compiler_params=params(24),

time: 205 us -> 205 us (level)
  no operation moved by 1% of the time
where the time goes in v8:
time: 205 us; the launch traced here: 204 us
  Pallas kernels  75.9 us (37%)
  waiting for transfers between devices  61.1 us (30%)
  starting transfers between devices  45.8 us (22%)
  local copies, waits for them, and re-layouts  14.9 us (7%)
  other arithmetic  5.02 us (2%)
    ppermute x16, waiting for transfers between devices, hop(): return lax.ppermute(v, ('z', 'y', 'x', 'c'), to)  39.1 us
    ppermute x16, starting transfers between devices, hop(): return lax.ppermute(v, ('z', 'y', 'x', 'c'), to)  23.2 us
    pallas_call x9, Pallas kernels, select(): pl.pallas_call(kernel, grid_spec=prefetched((n,), specs + [pl.BlockSpec(m...  22.1 us
    ppermute x6, waiting for transfers between devices, shards(): lax.ppermute(v, 'x', [(i, (i + k) % 4) for i in range(4)])  20.1 us
    pallas_call x1, Pallas kernels, shards(): pl.pallas_call(weight_kernel, grid_spec=prefetched((2, 4), [VMEM, VMEM, p...  14.9 us
    pallas_call x2, Pallas kernels, partial(): pl.pallas_call(kernel, grid_spec=prefetched((half // wide,), [VMEM, pl.Bl...  10.2 us
    ppermute x6, starting transfers between devices, shards(): lax.ppermute(v, 'x', [(i, (i + k) % 4) for i in range(4)])  8.78 us
    unnamed x38, local copies, waits for them, and re-layouts  7.78 us
  transfers between devices with their start and end apart: 29, of which 15 were waited for; matrix products, arithmetic and copies ran while one was open for 5% of the time, Pallas kernels for 34%

profile of v8, /device:TPU:0, one launch (start us, length us, event | category | flops | bytes accessed | tf_op | source)
XLA Modules:
  0.0 203.9 jit_solution(14589608764319085886)
XLA Ops:
  1.3 2.9 %pack.1.pw_ref = bf16[128,3200]{1,0:T(8,128)(2,1)} custom-call(s32[6]{0:T(128)} %stack.111.at_ref, s32[8,128]{1,0:T(8,128)} %bitcast.63, f32[8,128]{1,0:T(8,128)} %bitcast.64, bf16[128,4096]{1,0:T(8,128)(2,1)} %t1.1, bf16[128,4096]{1,0:T(8,128)(2,1)} %t1.1, bf16[128,4096]{1,0:T(8,128)(2,1)} %g3.1, bf16[128,4096]{1,0:T(8,128)(2,1)} %g3.1, ...), custom_call_target="tpu_custom_call" | custom-call | flops 10000 | bytes 2000 | tf_op jit(solution)/shard_map/pack/pallas_call | solution.py:266
  8.4 5.0 %outgoing.1 = bf16[6,192,2048]{2,1,0:T(8,128)(2,1)} custom-call(s32[1]{0:T(128)} %bitcast.c_ref.e_ref, bf16[2,192,4096]{2,1,0:T(8,128)(2,1)} %g_ref.3, bf16[2,192,4096]{2,1,0:T(8,128)(2,1)} %u_ref.3, bf16[2,192,4096]{2,1,0:T(8,128)(2,1)} %d_ref.3), custom_call_target="tpu_custom_call" | custom-call | bytes 9400 | tf_op jit(solution)/shard_map/outgoing/pallas_call | solution.py:282
  13.5 5.5 %collective-permute-done = bf16[128,3200]{1,0:T(8,128)(2,1)S(1)} collective-permute-done((bf16[128,3200]{1,0:T(8,128)(2,1)}, bf16[128,3200]{1,0:T(8,128)(2,1)S(1)}, u32[]{:S(2)}, u32[]{:S(2)}) %collective-permute-start) | collective-permute-done | bytes 819232 | tf_op jit(solution)/shard_map/ppermute | solution.py:57
  22.6 5.8 %collective-permute-done.2 = bf16[64,3200]{1,0:T(8,128)(2,1)S(1)} collective-permute-done((bf16[64,3200]{1,0:T(8,128)(2,1)S(1)}, bf16[64,3200]{1,0:T(8,128)(2,1)S(1)}, u32[]{:S(2)}, u32[]{:S(2)}) %collective-permute-start.2) | collective-permute-done | bytes 409632 | tf_op jit(solution)/shard_map/ppermute | solution.py:57
  42.7 4.3 %collective-permute-done.5.near_ref = bf16[4,128,1152]{2,1,0:T(8,128)(2,1)} collective-permute-done((bf16[4,128,1152]{2,1,0:T(8,128)(2,1)S(1)}, bf16[4,128,1152]{2,1,0:T(8,128)(2,1)}, u32[]{:S(2)}, u32[]{:S(2)}) %collective-permute-start.5) | collective-permute-done | bytes 1179680 | tf_op jit(solution)/shard_map/ppermute | solution.py:57
  47.2 2.9 %collective-permute-done.7.far_ref = bf16[4,128,1152]{2,1,0:T(8,128)(2,1)S(1)} collective-permute-done((bf16[4,128,1152]{2,1,0:T(8,128)(2,1)S(1)}, bf16[4,128,1152]{2,1,0:T(8,128)(2,1)S(1)}, u32[]{:S(2)}, u32[]{:S(2)}) %collective-permute-start.7) | collective-permute-done | bytes 1179680 | tf_op jit(solution)/shard_map/ppermute | solution.py:57
  54.7 3.6 %select.76.rest_0_ = bf16[2,768,2048]{2,1,0:T(8,128)(2,1)S(1)} custom-call(s32[18]{0:T(128)S(1)} %stack.130.info_ref, bf16[4,128,1152]{2,1,0:T(8,128)(2,1)S(1)} %pad_maximum_fusion.1.near_ref, bf16[4,128,2048]{2,1,0:T(8,128)(2,1)} %pad_maximum_fusion.g_ref), custom_call_target="tpu_custom_call" | custom-call | flops 201326 | bytes 5600 | tf_op jit(solution)/shard_map/select/pallas_call | solution.py:342
  60.1 8.7 %collective-permute-done.12.far_ref = bf16[4,128,1152]{2,1,0:T(8,128)(2,1)} collective-permute-done((bf16[4,128,1152]{2,1,0:T(8,128)(2,1)}, bf16[4,128,1152]{2,1,0:T(8,128)(2,1)}, u32[]{:S(2)}, u32[]{:S(2)}) %collective-permute-start.12) | collective-permute-done | bytes 1179680 | tf_op jit(solution)/shard_map/ppermute | solution.py:57
  70.4 2.9 %collective-permute-start.11 = (bf16[2,128,1152]{2,1,0:T(8,128)(2,1)S(1)}, bf16[2,128,1152]{2,1,0:T(8,128)(2,1)S(1)}, u32[]{:S(2)}, u32[]{:S(2)}) collective-permute-start(bf16[2,128,1152]{2,1,0:T(8,128)(2,1)S(1)} %slice.77), channel_id=1, source_target_pairs={{0,24},{1,97},{2,26},{3,99},{4,28},{5,101},{6,30},{7,103},{8,0},{9... | collective-permute-start | bytes 1769480 | tf_op jit(solution)/shard_map/ppermute | solution.py:57
  73.3 3.6 %select.77.rest_0_ = bf16[2,768,2048]{2,1,0:T(8,128)(2,1)S(1)} custom-call(s32[18]{0:T(128)S(1)} %stack.130.info_ref, bf16[4,128,1152]{2,1,0:T(8,128)(2,1)} %collective-permute-done.5.near_ref, bf16[4,128,1152]{2,1,0:T(8,128)(2,1)} %collective-permute-done.12.far_ref, bf16[2,768,2048]{2,1,0:T(8,128)(2,1)S(1)} %select.75.rest_0_), custom_call_target="tpu_custom_call", output_to_operand_aliasing={{}: (3, {})} | custom-call | flops 201326 | bytes 5600 | tf_op jit(solution)/shard_map/select/pallas_call | solution.py:342
  76.9 8.2 %collective-permute-done.10 = bf16[2,128,1152]{2,1,0:T(8,128)(2,1)S(1)} collective-permute-done((bf16[2,128,1152]{2,1,0:T(8,128)(2,1)S(1)}, bf16[2,128,1152]{2,1,0:T(8,128)(2,1)S(1)}, u32[]{:S(2)}, u32[]{:S(2)}) %collective-permute-start.10) | collective-permute-done | bytes 589856 | tf_op jit(solution)/shard_map/ppermute | solution.py:57
  93.0 3.6 %select.78.rest_0_ = bf16[2,768,2048]{2,1,0:T(8,128)(2,1)S(1)} custom-call(s32[18]{0:T(128)S(1)} %stack.130.info_ref, bf16[4,128,1152]{2,1,0:T(8,128)(2,1)} %collective-permute-done.5.near_ref, bf16[4,128,2048]{2,1,0:T(8,128)(2,1)} %collective-permute-done.8.g_ref, bf16[2,768,2048]{2,1,0:T(8,128)(2,1)S(1)} %select.76.rest_0_), custom_call_target="tpu_custom_call", output_to_operand_aliasing={{}: (3, {})} | custom-call | flops 201326 | bytes 5600 | tf_op jit(solution)/shard_map/select/pallas_call | solution.py:342
  96.7 3.6 %select.79.rest_0_ = bf16[2,768,2048]{2,1,0:T(8,128)(2,1)S(1)} custom-call(s32[18]{0:T(128)S(1)} %stack.130.info_ref, bf16[4,128,1152]{2,1,0:T(8,128)(2,1)S(1)} %copy-done.12, bf16[4,128,2048]{2,1,0:T(8,128)(2,1)} %collective-permute-done.9.g_ref, bf16[2,768,2048]{2,1,0:T(8,128)(2,1)S(1)} %select.78.rest_0_), custom_call_target="tpu_custom_call", output_to_operand_aliasing={{}: (3, {})} | custom-call | flops 201326 | bytes 5600 | tf_op jit(solution)/shard_map/select/pallas_call | solution.py:342
  119.1 4.8 %partial.2 = bf16[16,48,2048]{2,1,0:T(8,128)(2,1)} custom-call(s32[2]{0:T(128)S(1)} %pad_add_fusion.e_ref.c_ref, bf16[768,1152]{1,0:T(8,128)(2,1)S(1)} %act.1.ad_ref.mine_ref, bf16[2,768,2048]{2,1,0:T(8,128)(2,1)S(1)} %bitcast.62), custom_call_target="tpu_custom_call" | custom-call | flops 2415919 | bytes 8000 | tf_op jit(solution)/shard_map/partial/pallas_call | solution.py:430
  124.0 6.0 %all-to-all-start = ((bf16[16,48,2048]{2,1,0:T(8,128)(2,1)}), bf16[16,48,2048]{2,1,0:T(8,128)(2,1)}, u32[]{:S(2)}, u32[]{:S(2)}) async-start(bf16[16,48,2048]{2,1,0:T(8,128)(2,1)} %partial.2), calls=%async_computation | async-start | bytes 6291456 | tf_op jit(solution)/shard_map/all_to_all | solution.py:444
  130.1 2.8 %copy-done.3 = bf16[2,768,2048]{2,1,0:T(8,128)(2,1)S(1)} copy-done((bf16[2,768,2048]{2,1,0:T(8,128)(2,1)S(1)}, bf16[2,768,2048]{2,1,0:T(8,128)(2,1)}, u32[]{:S(2)}) %copy-start.3) | copy-done | bytes 6291480
  132.8 5.3 %partial.3 = bf16[4,768,512]{2,1,0:T(8,128)(2,1)S(1)} custom-call(s32[2]{0:T(128)S(1)} %pad_add_fusion.1.e_ref, bf16[768,1152]{1,0:T(8,128)(2,1)} %collective-permute-done.19.ad_ref.theirs_ref, bf16[2,768,2048]{2,1,0:T(8,128)(2,1)S(1)} %copy-done.3), custom_call_target="tpu_custom_call" | custom-call | flops 2415919 | bytes 8000 | tf_op jit(solution)/shard_map/partial/pallas_call | solution.py:430
  139.5 2.9 %collective-permute-start.21 = (bf16[768,512]{1,0:T(8,128)(2,1)S(1)}, bf16[768,512]{1,0:T(8,128)(2,1)}, u32[]{:S(2)}, u32[]{:S(2)}) collective-permute-start(bf16[768,512]{1,0:T(8,128)(2,1)S(1)} %get-tuple-element.125), channel_id=1, source_target_pairs={{0,4},{2,6},{4,0},{6,2},{1,5},{3,7},{5,1},{7,3},{8,12},{10,14},{12... | collective-permute-start | bytes 2359304 | tf_op jit(solution)/shard_map/ppermute | solution.py:441
  143.6 14.9 %weights.1 = (bf16[2,192,4096]{2,1,0:T(8,128)(2,1)}, bf16[2,192,4096]{2,1,0:T(8,128)(2,1)}, bf16[2,192,4096]{2,1,0:T(8,128)(2,1)}, bf16[2,3,192,2048]{3,2,1,0:T(8,128)(2,1)}) custom-call(s32[1]{0:T(128)} %bitcast.c_ref.e_ref, bf16[768,1152]{1,0:T(8,128)(2,1)} %copy-done.4, bf16[768,1152]{1,0:T(8,128)(2,1)} %collective-permute-done.19.ad_ref.theirs_ref, ...), custom_call_target="tpu_custom_call" | custom-call | flops 7247757 | bytes 24000 | tf_op jit(solution)/shard_map/weights/pallas_call | solution.py:451
  161.2 15.9 %collective-permute-done.21 = bf16[768,512]{1,0:T(8,128)(2,1)} collective-permute-done((bf16[768,512]{1,0:T(8,128)(2,1)S(1)}, bf16[768,512]{1,0:T(8,128)(2,1)}, u32[]{:S(2)}, u32[]{:S(2)}) %collective-permute-start.21) | collective-permute-done | bytes 786464 | tf_op jit(solution)/shard_map/ppermute | solution.py:441
  177.5 2.9 %fusion.2 = bf16[768,512]{1,0:T(8,128)(2,1)} fusion(bf16[768,512]{1,0:T(8,128)(2,1)} %collective-permute-done.22, bf16[768,512]{1,0:T(8,128)(2,1)} %collective-permute-done.21, bf16[768,512]{1,0:T(8,128)(2,1)} %collective-permute-done.20, bf16[4,768,512]{2,1,0:T(8,128)(2,1)S(1)} %partial.3), kind=kLoop, calls=%fused_computation.4 | loop fusion | flops 3145728 | bytes 3932160 | tf_op jit(solution)/shard_map/convert_element_type | solution.py:471
  180.4 6.9 %all-to-all-start.1 = ((bf16[16,48,512]{2,1,0:T(8,128)(2,1)}), bf16[16,48,512]{2,1,0:T(8,128)(2,1)S(1)}, u32[]{:S(2)}, u32[]{:S(2)}) async-start(bf16[16,48,512]{2,1,0:T(8,128)(2,1)} %bitcast.39), calls=%async_computation.1 | async-start | bytes 1572864 | tf_op jit(solution)/shard_map/all_to_all | solution.py:474
  191.1 3.0 %collective-permute-start.24 = (bf16[128,512]{1,0:T(8,128)(2,1)S(1)}, bf16[128,512]{1,0:T(8,128)(2,1)S(1)}, u32[]{:S(2)}, u32[]{:S(2)}) collective-permute-start(bf16[128,512]{1,0:T(8,128)(2,1)S(1)} %get-tuple-element.128), channel_id=1, source_target_pairs={{0,4},{2,6},{4,0},{6,2},{1,5},{3,7},{5,1},{7,3},{8,12},{10,14},{12... | collective-permute-start | bytes 393224 | tf_op jit(solution)/shard_map/ppermute | solution.py:441
  194.4 5.0 %settle.1 = (bf16[2,192,4096]{2,1,0:T(8,128)(2,1)}, bf16[2,192,4096]{2,1,0:T(8,128)(2,1)}, bf16[2,192,4096]{2,1,0:T(8,128)(2,1)}) custom-call(s32[1]{0:T(128)} %bitcast.c_ref.e_ref, bf16[2,3,192,2048]{3,2,1,0:T(8,128)(2,1)} %collective-permute-done.26.in_ref, ...), custom_call_target="tpu_custom_call", output_to_operand_aliasing={{0}: (2, {}), {1}: (3, {}), {2}: (4, {})} | custom-call | bytes 9400 | tf_op jit(solution)/shard_map/settle/pallas_call | solution.py:476
  (118 shorter events, 71.6 us)
Async XLA Ops:
  4.3 14.7 %collective-permute-start = (bf16[128,3200]{1,0:T(8,128)(2,1)}, bf16[128,3200]{1,0:T(8,128)(2,1)S(1)}, u32[]{:S(2)}, u32[]{:S(2)}) collective-permute-start(bf16[128,3200]{1,0:T(8,128)(2,1)} %pack.1.pw_ref), channel_id=1, source_target_pairs={{0,32},{1,9},{2,34},{3,11},{4,36},{5,13},{6,38},{7,15},{8,40},{9,1... | collective-permute-start | bytes 2457608 | tf_op jit(solution)/shard_map/ppermute | solution.py:57
  6.3 12.7 %collective-permute-start.1 = (bf16[128,3200]{1,0:T(8,128)(2,1)}, bf16[128,3200]{1,0:T(8,128)(2,1)S(1)}, u32[]{:S(2)}, u32[]{:S(2)}) collective-permute-start(bf16[128,3200]{1,0:T(8,128)(2,1)} %pack.1.pw_ref), channel_id=1, source_target_pairs={{0,96},{1,25},{2,98},{3,27},{4,100},{5,29},{6,102},{7,31},{8,104},... | collective-permute-start | bytes 2457608 | tf_op jit(solution)/shard_map/ppermute | solution.py:57
  19.0 10.0 %collective-permute-start.4 = (bf16[6,192,2048]{2,1,0:T(8,128)(2,1)}, bf16[6,192,2048]{2,1,0:T(8,128)(2,1)S(1)}, u32[]{:S(2)}, u32[]{:S(2)}) collective-permute-start(bf16[6,192,2048]{2,1,0:T(8,128)(2,1)} %outgoing.1), channel_id=1, source_target_pairs={{0,1},{1,0},{2,3},{3,2},{4,5},{5,4},{6,7},{7,6},{8,9},{9,8},{10,11... | collective-permute-start | bytes 14155784 | tf_op jit(solution)/shard_map/ppermute | solution.py:36
  29.3 17.6 %collective-permute-start.5 = (bf16[4,128,1152]{2,1,0:T(8,128)(2,1)S(1)}, bf16[4,128,1152]{2,1,0:T(8,128)(2,1)}, u32[]{:S(2)}, u32[]{:S(2)}) collective-permute-start(bf16[4,128,1152]{2,1,0:T(8,128)(2,1)S(1)} %pad_maximum_fusion.1.near_ref), channel_id=1, source_target_pairs={{0,8},{1,33},{2,10},{3,35},{4,12},{5,37},{6,14},{7,39},{8,16},{9,4... | collective-permute-start | bytes 3538952 | tf_op jit(solution)/shard_map/ppermute | solution.py:57
  31.0 16.2 %collective-permute-start.6 = (bf16[4,128,1152]{2,1,0:T(8,128)(2,1)S(1)}, bf16[4,128,1152]{2,1,0:T(8,128)(2,1)S(1)}, u32[]{:S(2)}, u32[]{:S(2)}) collective-permute-start(bf16[4,128,1152]{2,1,0:T(8,128)(2,1)S(1)} %pad_maximum_fusion.1.near_ref), channel_id=1, source_target_pairs={{0,24},{1,97},{2,26},{3,99},{4,28},{5,101},{6,30},{7,103},{8,0},{9... | collective-permute-start | bytes 3538952 | tf_op jit(solution)/shard_map/ppermute | solution.py:57
  32.6 17.4 %collective-permute-start.7 = (bf16[4,128,1152]{2,1,0:T(8,128)(2,1)S(1)}, bf16[4,128,1152]{2,1,0:T(8,128)(2,1)S(1)}, u32[]{:S(2)}, u32[]{:S(2)}) collective-permute-start(bf16[4,128,1152]{2,1,0:T(8,128)(2,1)S(1)} %pad_maximum_fusion.1.near_ref), channel_id=1, source_target_pairs={{0,2},{1,7},{2,4},{3,1},{4,6},{5,3},{6,0},{7,5},{8,10},{9,15},{10,... | collective-permute-start | bytes 3538952 | tf_op jit(solution)/shard_map/ppermute | solution.py:57
  51.0 17.7 %collective-permute-start.12 = (bf16[4,128,1152]{2,1,0:T(8,128)(2,1)}, bf16[4,128,1152]{2,1,0:T(8,128)(2,1)}, u32[]{:S(2)}, u32[]{:S(2)}) collective-permute-start(bf16[4,128,1152]{2,1,0:T(8,128)(2,1)} %collective-permute-done.5.near_ref), channel_id=1, source_target_pairs={{0,2},{1,7},{2,4},{3,1},{4,6},{5,3},{6,0},{7,5},{8,10},{9,15},{10,... | collective-permute-start | bytes 3538952 | tf_op jit(solution)/shard_map/ppermute | solution.py:57
  51.3 33.8 %collective-permute-start.8 = (bf16[4,128,2048]{2,1,0:T(8,128)(2,1)}, bf16[4,128,2048]{2,1,0:T(8,128)(2,1)}, u32[]{:S(2)}, u32[]{:S(2)}) collective-permute-start(bf16[4,128,2048]{2,1,0:T(8,128)(2,1)} %pad_maximum_fusion.g_ref), channel_id=1, source_target_pairs={{0,8},{1,33},{2,10},{3,35},{4,12},{5,37},{6,14},{7,39},{8,16},{9,4... | collective-permute-start | bytes 6291464 | tf_op jit(solution)/shard_map/ppermute | solution.py:57
  52.3 32.9 %collective-permute-start.9 = (bf16[4,128,2048]{2,1,0:T(8,128)(2,1)}, bf16[4,128,2048]{2,1,0:T(8,128)(2,1)}, u32[]{:S(2)}, u32[]{:S(2)}) collective-permute-start(bf16[4,128,2048]{2,1,0:T(8,128)(2,1)} %pad_maximum_fusion.g_ref), channel_id=1, source_target_pairs={{0,24},{1,97},{2,26},{3,99},{4,28},{5,101},{6,30},{7,103},{8,0},{9... | collective-permute-start | bytes 6291464 | tf_op jit(solution)/shard_map/ppermute | solution.py:57
  68.8 17.4 %collective-permute-start.13 = (bf16[4,128,1152]{2,1,0:T(8,128)(2,1)S(1)}, bf16[4,128,1152]{2,1,0:T(8,128)(2,1)S(1)}, u32[]{:S(2)}, u32[]{:S(2)}) collective-permute-start(bf16[4,128,1152]{2,1,0:T(8,128)(2,1)S(1)} %copy-done.12), channel_id=1, source_target_pairs={{0,2},{1,7},{2,4},{3,1},{4,6},{5,3},{6,0},{7,5},{8,10},{9,15},{10,... | collective-permute-start | bytes 3538952 | tf_op jit(solution)/shard_map/ppermute | solution.py:57
  70.0 15.2 %collective-permute-start.10 = (bf16[2,128,1152]{2,1,0:T(8,128)(2,1)S(1)}, bf16[2,128,1152]{2,1,0:T(8,128)(2,1)S(1)}, u32[]{:S(2)}, u32[]{:S(2)}) collective-permute-start(bf16[2,128,1152]{2,1,0:T(8,128)(2,1)S(1)} %slice.76), channel_id=1, source_target_pairs={{0,8},{1,33},{2,10},{3,35},{4,12},{5,37},{6,14},{7,39},{8,16},{9,4... | collective-permute-start | bytes 1769480 | tf_op jit(solution)/shard_map/ppermute | solution.py:57
  70.4 14.7 %collective-permute-start.11 = (bf16[2,128,1152]{2,1,0:T(8,128)(2,1)S(1)}, bf16[2,128,1152]{2,1,0:T(8,128)(2,1)S(1)}, u32[]{:S(2)}, u32[]{:S(2)}) collective-permute-start(bf16[2,128,1152]{2,1,0:T(8,128)(2,1)S(1)} %slice.77), channel_id=1, source_target_pairs={{0,24},{1,97},{2,26},{3,99},{4,28},{5,101},{6,30},{7,103},{8,0},{9... | collective-permute-start | bytes 1769480 | tf_op jit(solution)/shard_map/ppermute | solution.py:57
  86.3 17.5 %collective-permute-start.16 = (bf16[4,128,1152]{2,1,0:T(8,128)(2,1)S(1)}, bf16[4,128,1152]{2,1,0:T(8,128)(2,1)S(1)}, u32[]{:S(2)}, u32[]{:S(2)}) collective-permute-start(bf16[4,128,1152]{2,1,0:T(8,128)(2,1)S(1)} %constant_dynamic-update-slice_fusion.2.near_ref), channel_id=1, source_target_pairs={{0,2},{1,7},{2,4},{3,1},{4,6},{5,3},{6,0},{7,5},{8,10},{9,15},{10,... | collective-permute-start | bytes 3538952 | tf_op jit(solution)/shard_map/ppermute | solution.py:57
  88.2 20.1 %collective-permute-start.14 = (bf16[2,128,2048]{2,1,0:T(8,128)(2,1)S(1)}, bf16[2,128,2048]{2,1,0:T(8,128)(2,1)S(1)}, u32[]{:S(2)}, u32[]{:S(2)}) collective-permute-start(bf16[2,128,2048]{2,1,0:T(8,128)(2,1)S(1)} %slice.78), channel_id=1, source_target_pairs={{0,8},{1,33},{2,10},{3,35},{4,12},{5,37},{6,14},{7,39},{8,16},{9,4... | collective-permute-start | bytes 3145736 | tf_op jit(solution)/shard_map/ppermute | solution.py:57
  90.5 17.7 %collective-permute-start.15 = (bf16[2,128,2048]{2,1,0:T(8,128)(2,1)S(1)}, bf16[2,128,2048]{2,1,0:T(8,128)(2,1)S(1)}, u32[]{:S(2)}, u32[]{:S(2)}) collective-permute-start(bf16[2,128,2048]{2,1,0:T(8,128)(2,1)S(1)} %slice.79), channel_id=1, source_target_pairs={{0,24},{1,97},{2,26},{3,99},{4,28},{5,101},{6,30},{7,103},{8,0},{9... | collective-permute-start | bytes 3145736 | tf_op jit(solution)/shard_map/ppermute | solution.py:57
  118.8 11.2 %collective-permute-start.19 = (bf16[768,1152]{1,0:T(8,128)(2,1)S(1)}, bf16[768,1152]{1,0:T(8,128)(2,1)}, u32[]{:S(2)}, u32[]{:S(2)}) collective-permute-start(bf16[768,1152]{1,0:T(8,128)(2,1)S(1)} %act.1.ad_ref.mine_ref), channel_id=1, source_target_pairs={{0,1},{1,0},{2,3},{3,2},{4,5},{5,4},{6,7},{7,6},{8,9},{9,8},{10,11... | collective-permute-start | bytes 5308424 | tf_op jit(solution)/shard_map/ppermute | solution.py:36
  124.0 56.5 %all-to-all-start = ((bf16[16,48,2048]{2,1,0:T(8,128)(2,1)}), bf16[16,48,2048]{2,1,0:T(8,128)(2,1)}, u32[]{:S(2)}, u32[]{:S(2)}) async-start(bf16[16,48,2048]{2,1,0:T(8,128)(2,1)} %partial.2), calls=%async_computation | async-start | bytes 6291456 | tf_op jit(solution)/shard_map/all_to_all | solution.py:444
  139.2 21.9 %collective-permute-start.20 = (bf16[768,512]{1,0:T(8,128)(2,1)}, bf16[768,512]{1,0:T(8,128)(2,1)}, u32[]{:S(2)}, u32[]{:S(2)}) collective-permute-start(bf16[768,512]{1,0:T(8,128)(2,1)} %get-tuple-element.126), channel_id=1, source_target_pairs={{0,2},{2,4},{4,6},{6,0},{1,3},{3,5},{5,7},{7,1},{8,10},{10,12},{12... | collective-permute-start | bytes 2359304 | tf_op jit(solution)/shard_map/ppermute | solution.py:441
  139.5 37.6 %collective-permute-start.21 = (bf16[768,512]{1,0:T(8,128)(2,1)S(1)}, bf16[768,512]{1,0:T(8,128)(2,1)}, u32[]{:S(2)}, u32[]{:S(2)}) collective-permute-start(bf16[768,512]{1,0:T(8,128)(2,1)S(1)} %get-tuple-element.125), channel_id=1, source_target_pairs={{0,4},{2,6},{4,0},{6,2},{1,5},{3,7},{5,1},{7,3},{8,12},{10,14},{12... | collective-permute-start | bytes 2359304 | tf_op jit(solution)/shard_map/ppermute | solution.py:441
  142.5 35.1 %collective-permute-start.22 = (bf16[768,512]{1,0:T(8,128)(2,1)S(1)}, bf16[768,512]{1,0:T(8,128)(2,1)}, u32[]{:S(2)}, u32[]{:S(2)}) collective-permute-start(bf16[768,512]{1,0:T(8,128)(2,1)S(1)} %get-tuple-element.124), channel_id=1, source_target_pairs={{0,6},{2,0},{4,2},{6,4},{1,7},{3,1},{5,3},{7,5},{8,14},{10,8},{12,... | collective-permute-start | bytes 2359304 | tf_op jit(solution)/shard_map/ppermute | solution.py:441
  180.4 13.9 %collective-permute-start.26 = (bf16[2,3,192,2048]{3,2,1,0:T(8,128)(2,1)}, bf16[2,3,192,2048]{3,2,1,0:T(8,128)(2,1)}, u32[]{:S(2)}, u32[]{:S(2)}) collective-permute-start(bf16[2,3,192,2048]{3,2,1,0:T(8,128)(2,1)} %get-tuple-element.111), channel_id=1, source_target_pairs={{0,1},{1,0},{2,3},{3,2},{4,5},{5,4},{6,7},{7,6},{8,9},{9,8},{10,11... | collective-permute-start | bytes 14155784 | tf_op jit(solution)/shard_map/ppermute | solution.py:36
  180.4 21.9 %all-to-all-start.1 = ((bf16[16,48,512]{2,1,0:T(8,128)(2,1)}), bf16[16,48,512]{2,1,0:T(8,128)(2,1)S(1)}, u32[]{:S(2)}, u32[]{:S(2)}) async-start(bf16[16,48,512]{2,1,0:T(8,128)(2,1)} %bitcast.39), calls=%async_computation.1 | async-start | bytes 1572864 | tf_op jit(solution)/shard_map/all_to_all | solution.py:474
  189.9 9.5 %collective-permute-start.23 = (bf16[128,512]{1,0:T(8,128)(2,1)S(1)}, bf16[128,512]{1,0:T(8,128)(2,1)S(1)}, u32[]{:S(2)}, u32[]{:S(2)}) collective-permute-start(bf16[128,512]{1,0:T(8,128)(2,1)S(1)} %get-tuple-element.129), channel_id=1, source_target_pairs={{0,2},{2,4},{4,6},{6,0},{1,3},{3,5},{5,7},{7,1},{8,10},{10,12},{12... | collective-permute-start | bytes 393224 | tf_op jit(solution)/shard_map/ppermute | solution.py:441
  191.1 9.4 %collective-permute-start.24 = (bf16[128,512]{1,0:T(8,128)(2,1)S(1)}, bf16[128,512]{1,0:T(8,128)(2,1)S(1)}, u32[]{:S(2)}, u32[]{:S(2)}) collective-permute-start(bf16[128,512]{1,0:T(8,128)(2,1)S(1)} %get-tuple-element.128), channel_id=1, source_target_pairs={{0,4},{2,6},{4,0},{6,2},{1,5},{3,7},{5,1},{7,3},{8,12},{10,14},{12... | collective-permute-start | bytes 393224 | tf_op jit(solution)/shard_map/ppermute | solution.py:441
  (23 other events, 143.6 us)
